TPU v7x, 32 devices: a whole 2x2x4 slice. The times are simulated.
32 devices in a mesh: ctx: 2 (over y), fsdp: 16 (over z, x, core).
Axes of the slice: x: 2, y: 2, z: 4, core: 2. Of those that a mesh axis runs over, the one named last changes fastest.
Arguments:
- hidden_rows: bfloat16 [16, 256, 4608], P('fsdp', 'ctx'), may hold values from -6 to 6
- query_proj: bfloat16 [16, 256, 2048], P('fsdp', 'ctx'), may hold values from -10 to 10
- key_proj: bfloat16 [16, 256, 1024], P('fsdp', 'ctx'), may hold values from -10 to 10
- value_proj: bfloat16 [16, 256, 1024], P('fsdp', 'ctx'), may hold values from -6 to 6
- order_pos: int32 [16, 256], P('fsdp', 'ctx'), may hold values from 0 to 255, each once within a row
- post_gain: float32 [4608], replicated, may hold values from 0.5 to 1.5
- out_weight: bfloat16 [2048, 4608], P('fsdp', 'ctx'), may hold values from -0.125 to 0.125
Outputs:
- residual_out: bfloat16 [16, 256, 4608], P('fsdp', 'ctx')
Inputs may be any that keep to these rules, and one draw needn't show every extreme that they name: Each document's row of order_pos holds every position of 0 to 255 exactly once.
All inputs are finite; a program needn't handle non-finite values.
Results may differ from a plain program's by a relative error of at most 0.0053.
Values may be sent and summed in bfloat16 or wider, within the bound.
No kernel may reach another device: no remote copies, remote signals or barrier semaphores. Data moves between devices by JAX's collectives and lax.ppermute only.
A program may use at most 64 MiB of HBM per device.

v0:
```python
import jax
import jax.numpy as jnp
from jax import lax
from jax.sharding import PartitionSpec as P

HQ = 16
HK = 8
DH = 128


score_scale = 1.0 / 12.0
soft_cap = 50.0
norm_eps = 1e-06


def weigh_keys(query_heads, query_pos, key_heads, value_heads, key_pos):
    scores = (
        jnp.einsum("thgd,nhd->hgtn", query_heads, key_heads, preferred_element_type=jnp.float32)
        * score_scale
    )
    capped = soft_cap * jnp.tanh(scores / soft_cap)
    visible = key_pos[None, :] <= query_pos[:, None]
    weights = jnp.where(visible, jnp.exp(capped), 0.0)
    rounded = weights.astype(jnp.bfloat16)
    numerator = jnp.einsum(
        "hgtn,nhd->thgd", rounded, value_heads, preferred_element_type=jnp.float32
    )
    denominator = jnp.transpose(jnp.sum(weights, axis=-1), (2, 0, 1))
    return (numerator, denominator)


def shards(hidden_rows, query_proj, key_proj, value_proj, order_pos, post_gain, out_weight):
    tokens = query_proj.shape[1]
    groups = HQ // HK
    all_positions = lax.all_gather(order_pos, "ctx", axis=1, tiled=True)[0]
    weight_block = lax.all_gather(out_weight, "fsdp", axis=0, tiled=True)
    own_pos = order_pos[0]
    query_heads = query_proj[0].reshape(tokens, HK, groups, DH)
    key_piece = lax.all_gather(key_proj, "ctx", axis=1, tiled=True)
    value_piece = lax.all_gather(value_proj, "ctx", axis=1, tiled=True)
    piece_rows = key_piece.shape[1]
    numerator, denominator = weigh_keys(
        query_heads,
        own_pos,
        key_piece[0].reshape(piece_rows, HK, DH),
        value_piece[0].reshape(piece_rows, HK, DH),
        all_positions,
    )
    numerator, denominator = (numerator, denominator)
    attended = (numerator / denominator[..., None]).astype(jnp.bfloat16).reshape(1, tokens, HQ * DH)
    projected = jnp.dot(
        lax.all_gather(attended, "ctx", axis=1, tiled=True)[0],
        weight_block,
        preferred_element_type=jnp.float32,
    )
    token_rows = lax.all_to_all(
        projected.astype(jnp.bfloat16), "ctx", split_axis=0, concat_axis=1, tiled=True
    )
    widened = token_rows.astype(jnp.float32)
    normed = (
        widened
        * lax.rsqrt(jnp.mean(widened * widened, axis=-1, keepdims=True) + norm_eps)
        * post_gain
    )
    return (hidden_rows[0].astype(jnp.float32) + normed).astype(jnp.bfloat16)[None]


def solution(mesh):
    placed = (
        P("fsdp", "ctx", None),
        P("fsdp", "ctx", None),
        P("fsdp", "ctx", None),
        P("fsdp", "ctx", None),
        P("fsdp", "ctx"),
        P(),
        P("fsdp", "ctx"),
    )
    return jax.shard_map(
        shards, mesh=mesh, in_specs=placed, out_specs=P("fsdp", "ctx", None), check_vma=False
    )
```

profile of v0, /device:TPU:0, one launch (start us, length us, event | category | flops | bytes accessed | tf_op | source)
XLA Modules:
  0.0 179.4 jit_solution(1312846751900850639)
XLA Ops:
  6.5 0.0 copy-start.2
  6.5 0.0 copy-start.1
  6.5 0.0 all-gather.3.cloned.1.call-start
  6.5 5.5 %all_gather.15 = s32[1,256]{1,0:T(1,128)S(1)} all-gather(s32[1,128]{1,0:T(1,128)} %param.11), channel_id=1, replica_groups=mesh['ctx'=2,'fsdp'=16] {'ctx'}, dimensions={1}, use_global_device_ids=true | all-gather | bytes 1536 | tf_op jit(solution)/shard_map/all_gather | solution.py:35
  12.0 1.1 copy.12
  13.1 7.9 %all_gather.16 = bf16[1,256,1024]{1,2,0:T(8,128)(2,1)S(1)} all-gather(bf16[1,128,1024]{1,2,0:T(8,128)(2,1)S(1)} %copy.12), channel_id=1, replica_groups=mesh['ctx'=2,'fsdp'=16] {'ctx'}, dimensions={1}, use_global_device_ids=true | all-gather | bytes 786432 | tf_op jit(solution)/shard_map/all_gather | solution.py:39
  21.0 1.4 reshape_squeeze.10
  22.4 0.0 copy-done.1
  22.4 7.1 %all_gather.17 = bf16[1,256,1024]{2,1,0:T(8,128)(2,1)S(1)} all-gather(bf16[1,128,1024]{2,1,0:T(8,128)(2,1)S(1)} %copy-done.1), channel_id=1, replica_groups=mesh['ctx'=2,'fsdp'=16] {'ctx'}, dimensions={1}, use_global_device_ids=true | all-gather | bytes 786432 | tf_op jit(solution)/shard_map/all_gather | solution.py:40
  29.5 0.2 copy.15
  29.7 0.0 copy-done.2
  29.7 0.1 broadcast_compare_fusion
  29.8 0.9 fusion.6
  30.7 1.1 fusion.2
  31.9 0.0 all-gather.3.cloned.1.call-update
  31.9 0.0 all-gather.5.cloned.1.call-start
  31.9 0.7 all-gather.5.cloned.1.call-update
  32.6 22.1 %all-gather.3.cloned.1.call-done = bf16[1,256,2048]{1,2,0:T(8,128)(2,1)} async-done(((bf16[1,128,2048]{1,2,0:T(8,128)(2,1)}), bf16[1,256,2048]{1,2,0:T(8,128)(2,1)}) %all-gather.3.cloned.1.call-update) | async-done | bytes 1048592 | tf_op jit(solution)/shard_map/all_gather | solution.py:52
  54.8 83.8 %all-gather.5.cloned.1.call-done = bf16[2048,2304]{1,0:T(8,128)(2,1)} async-done(((bf16[128,2304]{1,0:T(8,128)(2,1)}), bf16[2048,2304]{1,0:T(8,128)(2,1)}) %all-gather.5.cloned.1.call-update) | async-done | bytes 9437200 | tf_op jit(solution)/shard_map/all_gather | solution.py:36
  138.5 6.6 %convolution_convert_fusion = bf16[256,2304]{1,0:T(8,128)(2,1)S(1)} fusion(bf16[2048,2304]{1,0:T(8,128)(2,1)} %all-gather.5.cloned.1.call-done, bf16[1,256,2048]{1,2,0:T(8,128)(2,1)} %all-gather.3.cloned.1.call-done), kind=kOutput, calls=%fused_computation | convolution fusion | flops 2416508928 | bytes 11665408 | tf_op jit(solution)/shard_map/dot_general | solution.py:51
  145.2 18.2 %all_to_all.13 = bf16[2,128,2304]{2,1,0:T(8,128)(2,1)S(1)} all-to-all(bf16[2,128,2304]{2,1,0:T(8,128)(2,1)S(1)} %bitcast.32), channel_id=1, replica_groups=mesh['ctx'=2,'fsdp'=16] {'ctx'}, dimensions={0} | all-to-all | bytes 2359296 | tf_op jit(solution)/shard_map/all_to_all | solution.py:56
  163.3 0.3 fusion
  163.7 0.2 convert_bitcast_fusion
  163.8 3.2 %copy.17 = f32[128,2,2304]{2,1,0:T(2,128)} copy(f32[128,2,2304]{2,0,1:T(8,128)S(1)} %convert_bitcast_fusion) | data formatting | bytes 4718592 | tf_op jit(solution)/shard_map/convert_element_type | solution.py:59
  167.1 0.0 copy-start
  167.1 3.3 %reshape.76 = f32[1,128,4608]{2,1,0:T(8,128)S(1)} reshape(f32[128,2,2304]{2,1,0:T(2,128)} %copy.17) | data formatting | bytes 4718592 | tf_op jit(solution)/shard_map/convert_element_type | solution.py:59
  170.4 0.0 copy-done
  170.4 2.2 %add_convert_fusion = bf16[1,128,4608]{2,1,0:T(8,128)(2,1)} fusion(f32[1,128,4608]{2,1,0:T(8,128)S(1)} %reshape.76, bf16[1,128,4608]{2,1,0:T(8,128)(2,1)S(1)} %copy-done, f32[4608]{0:T(1024)} %param.12, f32[128]{0:T(128)S(1)} %add_rsqrt_fusion), kind=kLoop, calls=%fused_computation.4 | loop fusion | flops 2949120 | bytes 4737536 | tf_op jit(solution)/shard_map/convert_element_type | solution.py:65
  (1 shorter events, 0.0 us)
Async XLA Ops:
  6.5 23.1 %copy-start.2 = (s32[1,128]{1,0:T(1,128)S(1)}, s32[1,128]{1,0:T(1,128)}, u32[]{:S(2)}) copy-start(s32[1,128]{1,0:T(1,128)} %param.11) | copy-start | bytes 1540
  6.5 15.9 %copy-start.1 = (bf16[1,128,1024]{2,1,0:T(8,128)(2,1)S(1)}, bf16[1,128,1024]{2,1,0:T(8,128)(2,1)}, u32[]{:S(2)}) copy-start(bf16[1,128,1024]{2,1,0:T(8,128)(2,1)} %param.10) | copy-start | bytes 786436
  6.5 48.2 %all-gather.3.cloned.1.call-start = ((), (), s32[]{:S(2)}) async-start(), calls=%async_computation.1 | async-start | bytes 1572864 | tf_op jit(solution)/shard_map/all_gather | solution.py:52
  31.9 106.6 %all-gather.5.cloned.1.call-start = ((), (), s32[]{:S(2)}) async-start(), calls=%async_computation.2 | async-start | bytes 10027008 | tf_op jit(solution)/shard_map/all_gather | solution.py:36
  167.1 3.3 %copy-start = (bf16[1,128,4608]{2,1,0:T(8,128)(2,1)S(1)}, bf16[1,128,4608]{2,1,0:T(8,128)(2,1)}, u32[]{:S(2)}) copy-start(bf16[1,128,4608]{2,1,0:T(8,128)(2,1)} %param.7) | copy-start | bytes 3538948
Sparse Core Ops, SparseCore 0:
  32.0 22.7 all-gather.2
  57.0 81.4 all-gather.4
where the time goes:
time: 180 us; the launch traced here: 179 us
  waiting for transfers between devices  107 us (59%)
  blocking collectives  38.6 us (21%)
  between operations  13.5 us (8%)
  local copies, waits for them, and re-layouts  9.25 us (5%)
  matrix products  8.7 us (5%)
  other arithmetic  2.74 us (2%)
    all_gather x1, waiting for transfers between devices, shards(): weight_block = lax.all_gather(out_weight, 'fsdp', axis=0, tiled=True)  83.8 us
    all_gather x1, waiting for transfers between devices, shards(): lax.all_gather(attended, 'ctx', axis=1, tiled=True)[0]  22.1 us
    all_to_all x1, blocking collectives, shards(): lax.all_to_all(projected.astype(jnp.bfloat16), 'ctx', split_axis=0, conca...  18.2 us
    all_gather x1, blocking collectives, shards(): key_piece = lax.all_gather(key_proj, 'ctx', axis=1, tiled=True)  7.88 us
    all_gather x1, blocking collectives, shards(): value_piece = lax.all_gather(value_proj, 'ctx', axis=1, tiled=True)  7.05 us
    dot_general x1, matrix products, shards(): jnp.dot(lax.all_gather(attended, 'ctx', axis=1, tiled=True)[0], weight_bl...  6.65 us
    convert_element_type x2, local copies, waits for them, and re-layouts, shards(): widened = token_rows.astype(jnp.float32)  6.52 us
    all_gather x1, blocking collectives, shards(): all_positions = lax.all_gather(order_pos, 'ctx', axis=1, tiled=True)[0]  5.46 us
  transfers between devices with their start and end apart: 2, of which 2 were waited for; matrix products, arithmetic and copies ran while one was open for 0% of the time, Pallas kernels for 0%

commit v1 on v0

v1 whole, which is shorter than its diff:
```python
import functools

import jax
import jax.numpy as jnp
import numpy as np
from jax import lax
from jax.experimental import pallas as pl
from jax.experimental.pallas import tpu as pltpu
from jax.sharding import Mesh
from jax.sharding import PartitionSpec as P

HQ = 16
HK = 8
DH = 128

score_scale = 1.0 / 12.0
soft_cap = 50.0
norm_eps = 1e-06

CHUNKS = (640, 512)
VMEM_LIMIT = 56 * 2**20
VMEM = pl.BlockSpec(memory_space=pltpu.VMEM)
ANY = pl.BlockSpec(memory_space=pl.ANY)


def params():
    return pltpu.CompilerParams(vmem_limit_bytes=VMEM_LIMIT)


def bf16(*dims):
    return jax.ShapeDtypeStruct(dims, jnp.bfloat16)


def ring_of(n):
    return list(range(0, 2, 1))[:1] + list(range(1, n, 2)) + list(range(2, n, 2))[::-1]


def cut_weight(w_ref, *rest):
    outs, sems = rest[:-1], rest[-1]
    quarter = w_ref.shape[1] // 2
    me = lax.axis_index("x")
    copies = []
    start = 0
    for i, (out, side) in enumerate(zip(outs, (me, 1 - me, 1 - me))):
        if i == 2:
            start = outs[1].shape[1]
        at = pl.multiple_of(side * quarter + start, 128)
        copies.append(
            pltpu.make_async_copy(w_ref.at[:, pl.ds(at, out.shape[1])], out, sems.at[i])
        )
    for copy in copies:
        copy.start()
    for copy in copies:
        copy.wait()


def attend(q_ref, k_own, k_far, v_own, v_far, pos_own, pos_far, *outs):
    tokens = q_ref.shape[0]
    groups = HQ // HK
    own = pos_own[...].astype(jnp.float32)
    far = pos_far[...].astype(jnp.float32)
    mine = jnp.transpose(jnp.broadcast_to(own, (tokens, tokens)))[:, :1]
    visible = jnp.concatenate([own, far], axis=1) <= mine
    visible = jnp.concatenate([visible] * groups, axis=0)
    for head in range(HK):
        at = pl.ds(head * DH, DH)
        query = jnp.concatenate(
            [q_ref[:, pl.ds((head * groups + g) * DH, DH)] for g in range(groups)], axis=0
        )
        keys = jnp.concatenate([k_own[:, at], k_far[:, at]], axis=0)
        values = jnp.concatenate([v_own[:, at], v_far[:, at]], axis=0)
        scores = lax.dot_general(
            query, keys, (((1,), (1,)), ((), ())), preferred_element_type=jnp.float32
        )
        capped = soft_cap * jnp.tanh(scores * (score_scale / soft_cap))
        weights = jnp.where(visible, jnp.exp(capped), 0.0)
        total = jnp.sum(weights, axis=-1, keepdims=True)
        mixed = jnp.dot(weights.astype(jnp.bfloat16), values, preferred_element_type=jnp.float32)
        mixed = (mixed / total).astype(jnp.bfloat16)
        for g in range(groups):
            h = head * groups + g
            per = HQ // len(outs)
            outs[h // per][:, pl.ds((h % per) * DH, DH)] = mixed[g * tokens : (g + 1) * tokens]


def head_of(step, same_x, same_core, ring):
    z, x, core = (lax.axis_index(name) for name in ("z", "x", "core"))
    n = len(ring)
    source = 0
    for i, stop in enumerate(ring):
        source = source + jnp.where(z == stop, ring[(i - step) % n], 0)
    x = x if same_x else 1 - x
    core = core if same_core else 1 - core
    return (source * 2 + x) * 2 + core


def project(ring, first, groups, halves, *refs):
    n = len(ring)
    acts = refs[: groups * halves]
    near = refs[groups * halves : groups * halves + 2 * n]
    away = refs[groups * halves + 2 * n : groups * halves + 4 * n]
    outs = refs[groups * halves + 4 * n : groups * halves + 4 * n + groups]
    a_all, w_all = refs[-2:]
    tokens, columns = outs[0].shape
    wide = acts[0].shape[1]
    for g in range(groups):
        for half in range(halves):
            a_all[pl.ds(g * tokens, tokens), pl.ds(half * wide, wide)] = acts[g * halves + half][...]
    for same_x, bufs, at in ((True, near, first), (False, away, 0)):
        for step in range(n):
            for other, same_core in enumerate((True, False)):
                head = head_of(step, same_x, same_core, ring)
                w_all[pl.ds(pl.multiple_of(head * DH, DH), DH), :] = bufs[step * 2 + other][
                    :, pl.ds(at, columns)
                ]
    for g in range(groups // 2):
        rows = jnp.dot(
            a_all[pl.ds(g * 2 * tokens, 2 * tokens), :], w_all[...], preferred_element_type=jnp.float32
        ).astype(jnp.bfloat16)
        outs[2 * g][...] = rows[:tokens]
        outs[2 * g + 1][...] = rows[tokens:]


def finish(chunks, hidden_ref, gain_ref, *refs):
    pieces, out_ref = refs[:-1], refs[-1]
    width = hidden_ref.shape[1]
    x, y = lax.axis_index("x"), lax.axis_index("ctx")
    owners = ((x, y), (1 - x, y), (x, 1 - y), (1 - x, 1 - y))
    total = 0.0
    for piece in pieces:
        value = piece[...].astype(jnp.float32)
        total = total + jnp.sum(value * value, axis=-1, keepdims=True)
    scale = lax.rsqrt(total / width + norm_eps)
    start = 0
    for c, columns in enumerate(chunks):
        for i, (px, py) in enumerate(owners):
            at = pl.ds(pl.multiple_of((py * 2 + px) * (width // 4) + start, 128), columns)
            normed = pieces[c * 4 + i][...].astype(jnp.float32) * scale * gain_ref[:, at]
            out_ref[:, at] = (hidden_ref[:, at].astype(jnp.float32) + normed).astype(jnp.bfloat16)
        start += columns


def shards(ring, chunks, hidden_rows, query_proj, key_proj, value_proj, order_pos, post_gain, out_weight):
    n = len(ring)
    tokens = query_proj.shape[1]
    width = hidden_rows.shape[2]
    swap = [(0, 1), (1, 0)]
    along = [(ring[i], ring[(i + 1) % n]) for i in range(n)]

    def over(value, axis):
        if axis == "diag":
            return lax.ppermute(value, ("ctx", "x"), [(i, 3 - i) for i in range(4)])
        return lax.ppermute(value, axis, along if axis == "z" else swap)

    query, key, value = query_proj[0], key_proj[0], value_proj[0]
    pos_far = over(order_pos, "ctx")
    key_far = over(key, "ctx")
    value_far = over(value, "ctx")

    quarter = out_weight.shape[1] // 2
    rows = out_weight.shape[0]
    near, *sent = pl.pallas_call(
        cut_weight,
        out_shape=[bf16(rows, quarter)] + [bf16(rows, c) for c in chunks],
        in_specs=[ANY],
        out_specs=[VMEM] * 3,
        scratch_shapes=[pltpu.SemaphoreType.DMA((3,))],
        compiler_params=params(),
        name="cut_weight",
    )(out_weight)
    away = [over(piece, "x") for piece in sent]

    def gather(piece):
        held = [piece]
        for _ in range(n - 1):
            held.append(over(held[-1], "z"))
        both = []
        for piece in held:
            both += [piece, over(piece, "core")]
        return both

    near = gather(near)
    away = [gather(piece) for piece in away]

    halves = 2
    acts = pl.pallas_call(
        attend,
        out_shape=[bf16(tokens, HQ * DH // halves)] * halves,
        in_specs=[VMEM] * 7,
        out_specs=[VMEM] * halves,
        compiler_params=params(),
        cost_estimate=pl.CostEstimate(flops=2**28, bytes_accessed=2**21, transcendentals=2**20),
        name="attend",
    )(query, key, key_far, value, value_far, order_pos, pos_far)
    acts_x = [over(a, "x") for a in acts]
    acts_y = [over(a, "ctx") for a in acts]
    acts_d = [over(acts_y[0], "x"), over(acts_x[1], "ctx")]
    all_acts = [*acts, *acts_x, *acts_y, *acts_d]

    pieces = []
    start = 0
    for columns, far in zip(chunks, away):
        out = pl.pallas_call(
            functools.partial(project, ring, start, 4, halves),
            out_shape=[bf16(tokens, columns)] * 4,
            in_specs=[VMEM] * (4 * halves + 4 * n),
            out_specs=[VMEM] * 4,
            scratch_shapes=[
                pltpu.VMEM((4 * tokens, HQ * DH), jnp.bfloat16),
                pltpu.VMEM((HQ * DH, columns), jnp.bfloat16),
            ],
            compiler_params=params(),
            cost_estimate=pl.CostEstimate(
                flops=8 * tokens * HQ * DH * columns, bytes_accessed=2**22, transcendentals=0
            ),
            name="project",
        )(*all_acts, *near, *far)
        pieces += [out[0], over(out[1], "x"), over(out[2], "ctx"), over(out[3], "diag")]
        start += columns

    out = pl.pallas_call(
        functools.partial(finish, chunks),
        out_shape=bf16(tokens, width),
        in_specs=[VMEM] * (2 + len(pieces)),
        out_specs=VMEM,
        compiler_params=params(),
        name="finish",
    )(hidden_rows[0], post_gain.reshape(1, width), *pieces)
    return out[None]


def plain_shards(hidden_rows, query_proj, key_proj, value_proj, order_pos, post_gain, out_weight):
    tokens = query_proj.shape[1]
    groups = HQ // HK
    positions = lax.all_gather(order_pos, "ctx", axis=1, tiled=True)[0]
    weight_block = lax.all_gather(out_weight, "fsdp", axis=0, tiled=True)
    query = query_proj[0].reshape(tokens, HK, groups, DH)
    keys = lax.all_gather(key_proj, "ctx", axis=1, tiled=True)[0].reshape(-1, HK, DH)
    values = lax.all_gather(value_proj, "ctx", axis=1, tiled=True)[0].reshape(-1, HK, DH)
    scores = jnp.einsum("thgd,nhd->hgtn", query, keys, preferred_element_type=jnp.float32)
    capped = soft_cap * jnp.tanh(scores * score_scale / soft_cap)
    visible = positions[None, :] <= order_pos[0][:, None]
    weights = jnp.where(visible, jnp.exp(capped), 0.0)
    numerator = jnp.einsum(
        "hgtn,nhd->thgd", weights.astype(jnp.bfloat16), values, preferred_element_type=jnp.float32
    )
    denominator = jnp.transpose(jnp.sum(weights, axis=-1), (2, 0, 1))
    attended = (numerator / denominator[..., None]).astype(jnp.bfloat16).reshape(1, tokens, HQ * DH)
    projected = jnp.dot(
        lax.all_gather(attended, "ctx", axis=1, tiled=True)[0],
        weight_block,
        preferred_element_type=jnp.float32,
    )
    token_rows = lax.all_to_all(
        projected.astype(jnp.bfloat16), "ctx", split_axis=0, concat_axis=1, tiled=True
    ).astype(jnp.float32)
    mean = jnp.mean(token_rows * token_rows, axis=-1, keepdims=True)
    normed = token_rows * lax.rsqrt(mean + norm_eps) * post_gain
    return (hidden_rows[0].astype(jnp.float32) + normed).astype(jnp.bfloat16)[None]


def solution(mesh):
    ctx, fsdp = mesh.shape["ctx"], mesh.shape["fsdp"]
    rows = "fsdp"
    body = plain_shards
    if ctx == 2 and fsdp % 4 == 0 and fsdp == HQ:
        mesh = Mesh(np.asarray(mesh.devices).reshape(ctx, fsdp // 4, 2, 2), ("ctx", "z", "x", "core"))
        rows = ("z", "x", "core")
        body = functools.partial(shards, ring_of(fsdp // 4), CHUNKS)
    placed = (
        P(rows, "ctx", None),
        P(rows, "ctx", None),
        P(rows, "ctx", None),
        P(rows, "ctx", None),
        P(rows, "ctx"),
        P(),
        P(rows, "ctx"),
    )
    return jax.shard_map(
        body, mesh=mesh, in_specs=placed, out_specs=P(rows, "ctx", None), check_vma=False
    )
```

time: 180 us -> 105 us (0.58)
  waiting for transfers between devices: 107 us -> 52.1 us
  blocking collectives: 38.6 us -> 0 us
  starting transfers between devices: 0.04 us -> 29.8 us
  Pallas kernels: 0 us -> 18.5 us
  between operations: 13.5 us -> 0.39 us
  matrix products: 8.7 us -> 0 us
  local copies, waits for them, and re-layouts: 9.25 us -> 4 us
  other arithmetic: 2.74 us -> 0 us
    all_gather x2 -> x0, waiting for transfers between devices: 106 us -> none  [the longest x1 83.8 us: shards(): weight_block = lax.all_gather(out_weight, 'fsdp', axis=0, tiled=True)]
    ppermute x0 -> x38, waiting for transfers between devices: none -> 52.1 us  [the longest x36 52 us: over(): return lax.ppermute(value, axis, along if axis == 'z' else swap)]
    ppermute x0 -> x38, starting transfers between devices: none -> 29.8 us  [the longest x36 25.8 us: over(): return lax.ppermute(value, axis, along if axis == 'z' else swap)]
    all_gather x3 -> x0, blocking collectives: 20.4 us -> none  [the longest x1 7.88 us: shards(): key_piece = lax.all_gather(key_proj, 'ctx', axis=1, tiled=True)]
    pallas_call x0 -> x5, Pallas kernels: none -> 18.5 us  [the longest x2 9.91 us: shards(): pl.pallas_call(functools.partial(project, ring, start, 4, halves), out_sh...]
    all_to_all x1 -> x0, blocking collectives: 18.2 us -> none  [shards(): lax.all_to_all(projected.astype(jnp.bfloat16), 'ctx', split_axis=0, conca...]
    dot_general x3 -> x0, matrix products: 8.7 us -> none  [the longest x1 6.65 us: shards(): jnp.dot(lax.all_gather(attended, 'ctx', axis=1, tiled=True)[0], weight_bl...]
    convert_element_type x2 -> x0, local copies, waits for them, and re-layouts: 6.52 us -> none  [shards(): widened = token_rows.astype(jnp.float32)]
  transfers between devices with their start and end apart: 2 -> 38, of which waited for: 2 -> 13; matrix products, arithmetic and copies ran while one was open for 0% -> 1% of each run, Pallas kernels for 0% -> 12%
where the time goes in v1:
time: 105 us
  waiting for transfers between devices  52.1 us (50%)
  starting transfers between devices  29.8 us (28%)
  Pallas kernels  18.5 us (18%)
  local copies, waits for them, and re-layouts  4 us (4%)
    ppermute x36, waiting for transfers between devices, over(): return lax.ppermute(value, axis, along if axis == 'z' else swap)  52 us
    ppermute x36, starting transfers between devices, over(): return lax.ppermute(value, axis, along if axis == 'z' else swap)  25.8 us
    pallas_call x2, Pallas kernels, shards(): pl.pallas_call(functools.partial(project, ring, start, 4, halves), out_sh...  9.91 us
    ppermute x2, starting transfers between devices, over(): return lax.ppermute(value, ('ctx', 'x'), [(i, 3 - i) for i in range(4)])  4 us
    pallas_call x1, Pallas kernels, shards(): pl.pallas_call(functools.partial(finish, chunks), out_shape=bf16(tokens,...  3.54 us
    unnamed x82, local copies, waits for them, and re-layouts  3.4 us
    pallas_call x1, Pallas kernels, shards(): pl.pallas_call(attend, out_shape=[bf16(tokens, HQ * DH // halves)] * halv...  3.17 us
  transfers between devices with their start and end apart: 38, of which 13 were waited for; matrix products, arithmetic and copies ran while one was open for 1% of the time, Pallas kernels for 12%

profile of v1, /device:TPU:0, one launch (start us, length us, event | category | flops | bytes accessed | tf_op | source)
XLA Modules:
  0.0 104.8 jit_solution(9432153008887454007)
XLA Ops:
  0.0 1.9 %cut_weight.1 = (bf16[128,1152]{1,0:T(8,128)(2,1)}, bf16[128,640]{1,0:T(8,128)(2,1)}, bf16[128,512]{1,0:T(8,128)(2,1)}) custom-call(bf16[128,2304]{1,0:T(8,128)(2,1)} %w_ref.1), custom_call_target="tpu_custom_call" | custom-call | tf_op jit(solution)/shard_map/cut_weight/pallas_call | solution.py:162
  1.9 3.0 %collective-permute-start.27 = (bf16[128,512]{1,0:T(8,128)(2,1)}, bf16[128,512]{1,0:T(8,128)(2,1)S(1)}, u32[]{:S(2)}, u32[]{:S(2)}) collective-permute-start(bf16[128,512]{1,0:T(8,128)(2,1)} %get-tuple-element.26), channel_id=1, source_target_pairs={{0,2},{2,0},{1,3},{3,1},{4,6},{6,4},{5,7},{7,5},{8,10},{10,8},{9,1... | collective-permute-start | bytes 393224 | tf_op jit(solution)/shard_map/ppermute | solution.py:153
  4.9 1.5 %collective-permute-start = (bf16[128,1024]{1,0:T(8,128)(2,1)}, bf16[128,1024]{1,0:T(8,128)(2,1)S(1)}, u32[]{:S(2)}, u32[]{:S(2)}) collective-permute-start(bf16[128,1024]{1,0:T(8,128)(2,1)} %bitcast.7), channel_id=1, source_target_pairs={{0,16},{16,0},{1,17},{17,1},{2,18},{18,2},{3,19},{19,3},{4,20},{20... | collective-permute-start | bytes 786440 | tf_op jit(solution)/shard_map/ppermute | solution.py:153
  6.4 0.5 collective-permute-start.1
  6.9 1.6 %collective-permute-start.10 = (bf16[128,1152]{1,0:T(8,128)(2,1)}, bf16[128,1152]{1,0:T(8,128)(2,1)S(1)}, u32[]{:S(2)}, u32[]{:S(2)}) collective-permute-start(bf16[128,1152]{1,0:T(8,128)(2,1)} %get-tuple-element.20.refs_8_), channel_id=1, source_target_pairs={{0,4},{4,12},{12,8},{8,0},{1,5},{5,13},{13,9},{9,1},{2,6},{6,14},{... | collective-permute-start | bytes 884744 | tf_op jit(solution)/shard_map/ppermute | solution.py:153
  8.5 1.5 %collective-permute-start.2 = (s32[1,128]{1,0:T(1,128)}, s32[1,128]{1,0:T(1,128)S(1)}, u32[]{:S(2)}, u32[]{:S(2)}) collective-permute-start(s32[1,128]{1,0:T(1,128)} %pos_own.1), channel_id=1, source_target_pairs={{0,16},{16,0},{1,17},{17,1},{2,18},{18,2},{3,19},{19,3},{4,20},{20... | collective-permute-start | bytes 1544 | tf_op jit(solution)/shard_map/ppermute | solution.py:153
  10.0 8.5 %collective-permute-done.2.pos_far = s32[1,128]{1,0:T(1,128)S(1)} collective-permute-done((s32[1,128]{1,0:T(1,128)}, s32[1,128]{1,0:T(1,128)S(1)}, u32[]{:S(2)}, u32[]{:S(2)}) %collective-permute-start.2) | collective-permute-done | bytes 544 | tf_op jit(solution)/shard_map/ppermute | solution.py:153
  18.6 0.4 collective-permute-start.16
  18.9 5.2 %collective-permute-done.16.refs_16_ = bf16[128,640]{1,0:T(8,128)(2,1)S(1)} collective-permute-done((bf16[128,640]{1,0:T(8,128)(2,1)}, bf16[128,640]{1,0:T(8,128)(2,1)S(1)}, u32[]{:S(2)}, u32[]{:S(2)}) %collective-permute-start.16) | collective-permute-done | bytes 163872 | tf_op jit(solution)/shard_map/ppermute | solution.py:153
  24.1 1.6 %collective-permute-start.29 = (bf16[128,512]{1,0:T(8,128)(2,1)S(1)}, bf16[128,512]{1,0:T(8,128)(2,1)S(1)}, u32[]{:S(2)}, u32[]{:S(2)}) collective-permute-start(bf16[128,512]{1,0:T(8,128)(2,1)S(1)} %collective-permute-done.27.refs_16_), channel_id=1, source_target_pairs={{0,4},{4,12},{12,8},{8,0},{1,5},{5,13},{13,9},{9,1},{2,6},{6,14},{... | collective-permute-start | bytes 393224 | tf_op jit(solution)/shard_map/ppermute | solution.py:153
  25.8 2.6 %collective-permute-start.18 = (bf16[128,640]{1,0:T(8,128)(2,1)S(1)}, bf16[128,640]{1,0:T(8,128)(2,1)S(1)}, u32[]{:S(2)}, u32[]{:S(2)}) collective-permute-start(bf16[128,640]{1,0:T(8,128)(2,1)S(1)} %collective-permute-done.16.refs_16_), channel_id=1, source_target_pairs={{0,4},{4,12},{12,8},{8,0},{1,5},{5,13},{13,9},{9,1},{2,6},{6,14},{... | collective-permute-start | bytes 491528 | tf_op jit(solution)/shard_map/ppermute | solution.py:153
  28.3 0.5 collective-permute-start.12
  28.8 3.2 %attend.1 = (bf16[128,1024]{1,0:T(8,128)(2,1)}, bf16[128,1024]{1,0:T(8,128)(2,1)}) custom-call(bf16[128,2048]{1,0:T(8,128)(2,1)} %bitcast.6, bf16[128,1024]{1,0:T(8,128)(2,1)} %bitcast.8, bf16[128,1024]{1,0:T(8,128)(2,1)} %copy-done.36, bf16[128,1024]{1,0:T(8,128)(2,1)} %bitcast.10, bf16[128,1024]{1,0:T(8,128)(2,1)} %copy-done.37, s32[1,128]{1,0:T(1,128)} %pos_own.1, ...), custom_call_target="tpu_custom_call" | custom-call | flops 268435456 | bytes 2097152 | tf_op jit(solution)/shard_map/attend/pallas_call | solution.py:186
  32.0 0.6 collective-permute-start.3
  32.6 0.3 collective-permute-start.31
  32.9 2.0 %collective-permute-done.18.refs_18_ = bf16[128,640]{1,0:T(8,128)(2,1)S(1)} collective-permute-done((bf16[128,640]{1,0:T(8,128)(2,1)S(1)}, bf16[128,640]{1,0:T(8,128)(2,1)S(1)}, u32[]{:S(2)}, u32[]{:S(2)}) %collective-permute-start.18) | collective-permute-done | bytes 163872 | tf_op jit(solution)/shard_map/ppermute | solution.py:153
  34.9 0.8 collective-permute-start.20
  35.7 0.5 collective-permute-start.4
  36.2 7.8 %collective-permute-done.31.refs_20_ = bf16[128,512]{1,0:T(8,128)(2,1)S(1)} collective-permute-done((bf16[128,512]{1,0:T(8,128)(2,1)S(1)}, bf16[128,512]{1,0:T(8,128)(2,1)S(1)}, u32[]{:S(2)}, u32[]{:S(2)}) %collective-permute-start.31) | collective-permute-done | bytes 131104 | tf_op jit(solution)/shard_map/ppermute | solution.py:153
  44.0 1.5 %collective-permute-start.5 = (bf16[128,1024]{1,0:T(8,128)(2,1)}, bf16[128,1024]{1,0:T(8,128)(2,1)S(1)}, u32[]{:S(2)}, u32[]{:S(2)}) collective-permute-start(bf16[128,1024]{1,0:T(8,128)(2,1)} %get-tuple-element.18.refs_0_), channel_id=1, source_target_pairs={{0,16},{16,0},{1,17},{17,1},{2,18},{18,2},{3,19},{19,3},{4,20},{20... | collective-permute-start | bytes 786440 | tf_op jit(solution)/shard_map/ppermute | solution.py:153
  45.5 1.5 %collective-permute-done.20.refs_20_ = bf16[128,640]{1,0:T(8,128)(2,1)S(1)} collective-permute-done((bf16[128,640]{1,0:T(8,128)(2,1)S(1)}, bf16[128,640]{1,0:T(8,128)(2,1)S(1)}, u32[]{:S(2)}, u32[]{:S(2)}) %collective-permute-start.20) | collective-permute-done | bytes 163872 | tf_op jit(solution)/shard_map/ppermute | solution.py:153
  47.1 1.5 %collective-permute-start.6 = (bf16[128,1024]{1,0:T(8,128)(2,1)}, bf16[128,1024]{1,0:T(8,128)(2,1)S(1)}, u32[]{:S(2)}, u32[]{:S(2)}) collective-permute-start(bf16[128,1024]{1,0:T(8,128)(2,1)} %get-tuple-element.19.refs_1_), channel_id=1, source_target_pairs={{0,16},{16,0},{1,17},{17,1},{2,18},{18,2},{3,19},{19,3},{4,20},{20... | collective-permute-start | bytes 786440 | tf_op jit(solution)/shard_map/ppermute | solution.py:153
  48.6 0.8 collective-permute-start.14
  49.6 3.8 %collective-permute-done.5.refs_4_ = bf16[128,1024]{1,0:T(8,128)(2,1)S(1)} collective-permute-done((bf16[128,1024]{1,0:T(8,128)(2,1)}, bf16[128,1024]{1,0:T(8,128)(2,1)S(1)}, u32[]{:S(2)}, u32[]{:S(2)}) %collective-permute-start.5) | collective-permute-done | bytes 262176 | tf_op jit(solution)/shard_map/ppermute | solution.py:153
  53.5 0.8 collective-permute-start.33
  54.3 3.0 %collective-permute-done.6.refs_5_ = bf16[128,1024]{1,0:T(8,128)(2,1)S(1)} collective-permute-done((bf16[128,1024]{1,0:T(8,128)(2,1)}, bf16[128,1024]{1,0:T(8,128)(2,1)S(1)}, u32[]{:S(2)}, u32[]{:S(2)}) %collective-permute-start.6) | collective-permute-done | bytes 262176 | tf_op jit(solution)/shard_map/ppermute | solution.py:153
  57.3 0.8 collective-permute-start.22
  58.1 4.1 %collective-permute-done.33.refs_22_ = bf16[128,512]{1,0:T(8,128)(2,1)S(1)} collective-permute-done((bf16[128,512]{1,0:T(8,128)(2,1)S(1)}, bf16[128,512]{1,0:T(8,128)(2,1)S(1)}, u32[]{:S(2)}, u32[]{:S(2)}) %collective-permute-start.33) | collective-permute-done | bytes 131104 | tf_op jit(solution)/shard_map/ppermute | solution.py:153
  62.2 0.5 collective-permute-start.7
  62.7 0.5 collective-permute-start.8
  63.2 2.0 %collective-permute-done.22.refs_22_ = bf16[128,640]{1,0:T(8,128)(2,1)S(1)} collective-permute-done((bf16[128,640]{1,0:T(8,128)(2,1)S(1)}, bf16[128,640]{1,0:T(8,128)(2,1)S(1)}, u32[]{:S(2)}, u32[]{:S(2)}) %collective-permute-start.22) | collective-permute-done | bytes 163872 | tf_op jit(solution)/shard_map/ppermute | solution.py:153
  65.3 1.3 %collective-permute-done.34.refs_23_ = bf16[128,512]{1,0:T(8,128)(2,1)S(1)} collective-permute-done((bf16[128,512]{1,0:T(8,128)(2,1)S(1)}, bf16[128,512]{1,0:T(8,128)(2,1)S(1)}, u32[]{:S(2)}, u32[]{:S(2)}) %collective-permute-start.34) | collective-permute-done | bytes 131104 | tf_op jit(solution)/shard_map/ppermute | solution.py:153
  66.7 2.8 %collective-permute-done.7.refs_6_ = bf16[128,1024]{1,0:T(8,128)(2,1)S(1)} collective-permute-done((bf16[128,1024]{1,0:T(8,128)(2,1)S(1)}, bf16[128,1024]{1,0:T(8,128)(2,1)S(1)}, u32[]{:S(2)}, u32[]{:S(2)}) %collective-permute-start.7) | collective-permute-done | bytes 262176 | tf_op jit(solution)/shard_map/ppermute | solution.py:153
  70.8 0.7 copy-done.6
  71.6 4.6 %project.3 = (bf16[128,512]{1,0:T(8,128)(2,1)}, bf16[128,512]{1,0:T(8,128)(2,1)}, bf16[128,512]{1,0:T(8,128)(2,1)}, bf16[128,512]{1,0:T(8,128)(2,1)}) custom-call(bf16[128,1024]{1,0:T(8,128)(2,1)} %get-tuple-element.18.refs_0_, bf16[128,1024]{1,0:T(8,128)(2,1)} %get-tuple-element.19.refs_1_, bf16[128,1024]{1,0:T(8,128)(2,1)} %copy-done.7, ...), custom_call_target="tpu_custom_call" | custom-call | flops 1073741824 | bytes 4194304 | tf_op jit(solution)/shard_map/project/pallas_call | solution.py:203
  76.2 1.4 %collective-permute-start.35 = (bf16[128,512]{1,0:T(8,128)(2,1)}, bf16[128,512]{1,0:T(8,128)(2,1)S(1)}, u32[]{:S(2)}, u32[]{:S(2)}) collective-permute-start(bf16[128,512]{1,0:T(8,128)(2,1)} %get-tuple-element.28), channel_id=1, source_target_pairs={{0,2},{2,0},{1,3},{3,1},{4,6},{6,4},{5,7},{7,5},{8,10},{10,8},{9,1... | collective-permute-start | bytes 393224 | tf_op jit(solution)/shard_map/ppermute | solution.py:153
  77.7 0.6 copy-done.17
  78.4 0.7 copy-done.20
  79.1 5.3 %project.2 = (bf16[128,640]{1,0:T(8,128)(2,1)}, bf16[128,640]{1,0:T(8,128)(2,1)}, bf16[128,640]{1,0:T(8,128)(2,1)}, bf16[128,640]{1,0:T(8,128)(2,1)}) custom-call(bf16[128,1024]{1,0:T(8,128)(2,1)} %get-tuple-element.18.refs_0_, bf16[128,1024]{1,0:T(8,128)(2,1)} %get-tuple-element.19.refs_1_, bf16[128,1024]{1,0:T(8,128)(2,1)} %copy-done.7, ...), custom_call_target="tpu_custom_call" | custom-call | flops 1342177280 | bytes 4194304 | tf_op jit(solution)/shard_map/project/pallas_call | solution.py:203
  84.4 0.8 collective-permute-start.24
  85.2 0.5 collective-permute-start.25
  85.7 2.3 %collective-permute-start.26 = (bf16[128,640]{1,0:T(8,128)(2,1)}, bf16[128,640]{1,0:T(8,128)(2,1)S(1)}, u32[]{:S(2)}, u32[]{:S(2)}) collective-permute-start(bf16[128,640]{1,0:T(8,128)(2,1)} %get-tuple-element.25), channel_id=1, source_target_pairs={{0,18},{2,16},{16,2},{18,0},{1,19},{3,17},{17,3},{19,1},{4,22},{6,... | collective-permute-start | bytes 491528 | tf_op jit(solution)/shard_map/ppermute | solution.py:152
  87.9 0.5 collective-permute-start.36
  88.5 1.7 %collective-permute-start.37 = (bf16[128,512]{1,0:T(8,128)(2,1)S(1)}, bf16[128,512]{1,0:T(8,128)(2,1)S(1)}, u32[]{:S(2)}, u32[]{:S(2)}) collective-permute-start(bf16[128,512]{1,0:T(8,128)(2,1)S(1)} %copy-done.38), channel_id=1, source_target_pairs={{0,18},{2,16},{16,2},{18,0},{1,19},{3,17},{17,3},{19,1},{4,22},{6,... | collective-permute-start | bytes 393224 | tf_op jit(solution)/shard_map/ppermute | solution.py:152
  90.2 0.6 reshape.3.gain_ref
  90.8 9.5 %collective-permute-done.36.refs_6_ = bf16[128,512]{1,0:T(8,128)(2,1)S(1)} collective-permute-done((bf16[128,512]{1,0:T(8,128)(2,1)S(1)}, bf16[128,512]{1,0:T(8,128)(2,1)S(1)}, u32[]{:S(2)}, u32[]{:S(2)}) %collective-permute-start.36) | collective-permute-done | bytes 131104 | tf_op jit(solution)/shard_map/ppermute | solution.py:153
  100.4 0.6 copy-done.33
  101.2 3.5 %finish.1 = bf16[128,4608]{1,0:T(8,128)(2,1)} custom-call(bf16[128,4608]{1,0:T(8,128)(2,1)} %bitcast.5, f32[1,4608]{1,0:T(1,128)} %reshape.3.gain_ref, bf16[128,640]{1,0:T(8,128)(2,1)} %get-tuple-element.22.refs_0_, bf16[128,640]{1,0:T(8,128)(2,1)} %copy-done.21, bf16[128,640]{1,0:T(8,128)(2,1)} %copy-done.22, bf16[128,640]{1,0:T(8,128)(2,1)} %copy-done.23, ...), custom_call_target="tpu_custom_call" | custom-call | tf_op jit(solution)/shard_map/finish/pallas_call | solution.py:221
  (116 shorter events, 2.0 us)
Async XLA Ops:
  1.9 17.0 %collective-permute-start.27 = (bf16[128,512]{1,0:T(8,128)(2,1)}, bf16[128,512]{1,0:T(8,128)(2,1)S(1)}, u32[]{:S(2)}, u32[]{:S(2)}) collective-permute-start(bf16[128,512]{1,0:T(8,128)(2,1)} %get-tuple-element.26), channel_id=1, source_target_pairs={{0,2},{2,0},{1,3},{3,1},{4,6},{6,4},{5,7},{7,5},{8,10},{10,8},{9,1... | collective-permute-start | bytes 393224 | tf_op jit(solution)/shard_map/ppermute | solution.py:153
  4.9 19.2 %collective-permute-start = (bf16[128,1024]{1,0:T(8,128)(2,1)}, bf16[128,1024]{1,0:T(8,128)(2,1)S(1)}, u32[]{:S(2)}, u32[]{:S(2)}) collective-permute-start(bf16[128,1024]{1,0:T(8,128)(2,1)} %bitcast.7), channel_id=1, source_target_pairs={{0,16},{16,0},{1,17},{17,1},{2,18},{18,2},{3,19},{19,3},{4,20},{20... | collective-permute-start | bytes 786440 | tf_op jit(solution)/shard_map/ppermute | solution.py:153
  6.4 19.3 %collective-permute-start.1 = (bf16[128,1024]{1,0:T(8,128)(2,1)}, bf16[128,1024]{1,0:T(8,128)(2,1)S(1)}, u32[]{:S(2)}, u32[]{:S(2)}) collective-permute-start(bf16[128,1024]{1,0:T(8,128)(2,1)} %bitcast.9), channel_id=1, source_target_pairs={{0,16},{16,0},{1,17},{17,1},{2,18},{18,2},{3,19},{19,3},{4,20},{20... | collective-permute-start | bytes 786440 | tf_op jit(solution)/shard_map/ppermute | solution.py:153
  6.9 21.4 %collective-permute-start.10 = (bf16[128,1152]{1,0:T(8,128)(2,1)}, bf16[128,1152]{1,0:T(8,128)(2,1)S(1)}, u32[]{:S(2)}, u32[]{:S(2)}) collective-permute-start(bf16[128,1152]{1,0:T(8,128)(2,1)} %get-tuple-element.20.refs_8_), channel_id=1, source_target_pairs={{0,4},{4,12},{12,8},{8,0},{1,5},{5,13},{13,9},{9,1},{2,6},{6,14},{... | collective-permute-start | bytes 884744 | tf_op jit(solution)/shard_map/ppermute | solution.py:153
  8.5 10.1 %collective-permute-start.2 = (s32[1,128]{1,0:T(1,128)}, s32[1,128]{1,0:T(1,128)S(1)}, u32[]{:S(2)}, u32[]{:S(2)}) collective-permute-start(s32[1,128]{1,0:T(1,128)} %pos_own.1), channel_id=1, source_target_pairs={{0,16},{16,0},{1,17},{17,1},{2,18},{18,2},{3,19},{19,3},{4,20},{20... | collective-permute-start | bytes 1544 | tf_op jit(solution)/shard_map/ppermute | solution.py:153
  18.6 5.5 %collective-permute-start.16 = (bf16[128,640]{1,0:T(8,128)(2,1)}, bf16[128,640]{1,0:T(8,128)(2,1)S(1)}, u32[]{:S(2)}, u32[]{:S(2)}) collective-permute-start(bf16[128,640]{1,0:T(8,128)(2,1)} %get-tuple-element.21), channel_id=1, source_target_pairs={{0,2},{2,0},{1,3},{3,1},{4,6},{6,4},{5,7},{7,5},{8,10},{10,8},{9,1... | collective-permute-start | bytes 491528 | tf_op jit(solution)/shard_map/ppermute | solution.py:153
  18.9 51.5 %copy-start.24 = (bf16[128,512]{1,0:T(8,128)(2,1)}, bf16[128,512]{1,0:T(8,128)(2,1)S(1)}, u32[]{:S(2)}) copy-start(bf16[128,512]{1,0:T(8,128)(2,1)S(1)} %collective-permute-done.27.refs_16_) | copy-start | bytes 393220
  18.9 13.7 %collective-permute-start.9 = (bf16[128,1152]{1,0:T(8,128)(2,1)}, bf16[128,1152]{1,0:T(8,128)(2,1)S(1)}, u32[]{:S(2)}, u32[]{:S(2)}) collective-permute-start(bf16[128,1152]{1,0:T(8,128)(2,1)} %get-tuple-element.20.refs_8_), channel_id=1, source_target_pairs={{0,1},{1,0},{2,3},{3,2},{4,5},{5,4},{6,7},{7,6},{8,9},{9,8},{10,11... | collective-permute-start | bytes 884744 | tf_op jit(solution)/shard_map/ppermute | solution.py:153
  24.1 52.1 %copy-start.13 = (bf16[128,640]{1,0:T(8,128)(2,1)}, bf16[128,640]{1,0:T(8,128)(2,1)S(1)}, u32[]{:S(2)}) copy-start(bf16[128,640]{1,0:T(8,128)(2,1)S(1)} %collective-permute-done.16.refs_16_) | copy-start | bytes 491524
  24.1 7.9 %collective-permute-start.28 = (bf16[128,512]{1,0:T(8,128)(2,1)S(1)}, bf16[128,512]{1,0:T(8,128)(2,1)S(1)}, u32[]{:S(2)}, u32[]{:S(2)}) collective-permute-start(bf16[128,512]{1,0:T(8,128)(2,1)S(1)} %collective-permute-done.27.refs_16_), channel_id=1, source_target_pairs={{0,1},{1,0},{2,3},{3,2},{4,5},{5,4},{6,7},{7,6},{8,9},{9,8},{10,11... | collective-permute-start | bytes 393224 | tf_op jit(solution)/shard_map/ppermute | solution.py:153
  24.1 8.5 %collective-permute-start.29 = (bf16[128,512]{1,0:T(8,128)(2,1)S(1)}, bf16[128,512]{1,0:T(8,128)(2,1)S(1)}, u32[]{:S(2)}, u32[]{:S(2)}) collective-permute-start(bf16[128,512]{1,0:T(8,128)(2,1)S(1)} %collective-permute-done.27.refs_16_), channel_id=1, source_target_pairs={{0,4},{4,12},{12,8},{8,0},{1,5},{5,13},{13,9},{9,1},{2,6},{6,14},{... | collective-permute-start | bytes 393224 | tf_op jit(solution)/shard_map/ppermute | solution.py:153
  25.8 9.1 %collective-permute-start.18 = (bf16[128,640]{1,0:T(8,128)(2,1)S(1)}, bf16[128,640]{1,0:T(8,128)(2,1)S(1)}, u32[]{:S(2)}, u32[]{:S(2)}) collective-permute-start(bf16[128,640]{1,0:T(8,128)(2,1)S(1)} %collective-permute-done.16.refs_16_), channel_id=1, source_target_pairs={{0,4},{4,12},{12,8},{8,0},{1,5},{5,13},{13,9},{9,1},{2,6},{6,14},{... | collective-permute-start | bytes 491528 | tf_op jit(solution)/shard_map/ppermute | solution.py:153
  28.3 42.0 %copy-start = (bf16[128,1152]{1,0:T(8,128)(2,1)}, bf16[128,1152]{1,0:T(8,128)(2,1)S(1)}, u32[]{:S(2)}) copy-start(bf16[128,1152]{1,0:T(8,128)(2,1)S(1)} %collective-permute-done.10.refs_10_) | copy-start | bytes 884740
  28.3 20.3 %collective-permute-start.12 = (bf16[128,1152]{1,0:T(8,128)(2,1)S(1)}, bf16[128,1152]{1,0:T(8,128)(2,1)S(1)}, u32[]{:S(2)}, u32[]{:S(2)}) collective-permute-start(bf16[128,1152]{1,0:T(8,128)(2,1)S(1)} %collective-permute-done.10.refs_10_), channel_id=1, source_target_pairs={{0,4},{4,12},{12,8},{8,0},{1,5},{5,13},{13,9},{9,1},{2,6},{6,14},{... | collective-permute-start | bytes 884744 | tf_op jit(solution)/shard_map/ppermute | solution.py:153
  32.0 38.4 %copy-start.25 = (bf16[128,512]{1,0:T(8,128)(2,1)}, bf16[128,512]{1,0:T(8,128)(2,1)S(1)}, u32[]{:S(2)}) copy-start(bf16[128,512]{1,0:T(8,128)(2,1)S(1)} %collective-permute-done.28.refs_17_) | copy-start | bytes 393220
  32.0 16.6 %collective-permute-start.3 = (bf16[128,1024]{1,0:T(8,128)(2,1)}, bf16[128,1024]{1,0:T(8,128)(2,1)S(1)}, u32[]{:S(2)}, u32[]{:S(2)}) collective-permute-start(bf16[128,1024]{1,0:T(8,128)(2,1)} %get-tuple-element.18.refs_0_), channel_id=1, source_target_pairs={{0,2},{2,0},{1,3},{3,1},{4,6},{6,4},{5,7},{7,5},{8,10},{10,8},{9,1... | collective-permute-start | bytes 786440 | tf_op jit(solution)/shard_map/ppermute | solution.py:153
  32.6 37.8 %copy-start.26 = (bf16[128,512]{1,0:T(8,128)(2,1)}, bf16[128,512]{1,0:T(8,128)(2,1)S(1)}, u32[]{:S(2)}) copy-start(bf16[128,512]{1,0:T(8,128)(2,1)S(1)} %collective-permute-done.29.refs_18_) | copy-start | bytes 393220
  32.6 3.1 %collective-permute-start.30 = (bf16[128,512]{1,0:T(8,128)(2,1)S(1)}, bf16[128,512]{1,0:T(8,128)(2,1)S(1)}, u32[]{:S(2)}, u32[]{:S(2)}) collective-permute-start(bf16[128,512]{1,0:T(8,128)(2,1)S(1)} %collective-permute-done.29.refs_18_), channel_id=1, source_target_pairs={{0,1},{1,0},{2,3},{3,2},{4,5},{5,4},{6,7},{7,6},{8,9},{9,8},{10,11... | collective-permute-start | bytes 393224 | tf_op jit(solution)/shard_map/ppermute | solution.py:153
  32.6 37.8 %copy-start.1 = (bf16[128,1152]{1,0:T(8,128)(2,1)}, bf16[128,1152]{1,0:T(8,128)(2,1)S(1)}, u32[]{:S(2)}) copy-start(bf16[128,1152]{1,0:T(8,128)(2,1)S(1)} %collective-permute-done.9.refs_9_) | copy-start | bytes 884740
  32.6 11.4 %collective-permute-start.31 = (bf16[128,512]{1,0:T(8,128)(2,1)S(1)}, bf16[128,512]{1,0:T(8,128)(2,1)S(1)}, u32[]{:S(2)}, u32[]{:S(2)}) collective-permute-start(bf16[128,512]{1,0:T(8,128)(2,1)S(1)} %collective-permute-done.29.refs_18_), channel_id=1, source_target_pairs={{0,4},{4,12},{12,8},{8,0},{1,5},{5,13},{13,9},{9,1},{2,6},{6,14},{... | collective-permute-start | bytes 393224 | tf_op jit(solution)/shard_map/ppermute | solution.py:153
  34.9 42.8 %copy-start.14 = (bf16[128,640]{1,0:T(8,128)(2,1)}, bf16[128,640]{1,0:T(8,128)(2,1)S(1)}, u32[]{:S(2)}) copy-start(bf16[128,640]{1,0:T(8,128)(2,1)S(1)} %collective-permute-done.18.refs_18_) | copy-start | bytes 491524
  34.9 12.2 %collective-permute-start.20 = (bf16[128,640]{1,0:T(8,128)(2,1)S(1)}, bf16[128,640]{1,0:T(8,128)(2,1)S(1)}, u32[]{:S(2)}, u32[]{:S(2)}) collective-permute-start(bf16[128,640]{1,0:T(8,128)(2,1)S(1)} %collective-permute-done.18.refs_18_), channel_id=1, source_target_pairs={{0,4},{4,12},{12,8},{8,0},{1,5},{5,13},{13,9},{9,1},{2,6},{6,14},{... | collective-permute-start | bytes 491528 | tf_op jit(solution)/shard_map/ppermute | solution.py:153
  35.7 34.8 %copy-start.27 = (bf16[128,512]{1,0:T(8,128)(2,1)}, bf16[128,512]{1,0:T(8,128)(2,1)S(1)}, u32[]{:S(2)}) copy-start(bf16[128,512]{1,0:T(8,128)(2,1)S(1)} %collective-permute-done.30.refs_19_) | copy-start | bytes 393220
  35.7 13.8 %collective-permute-start.4 = (bf16[128,1024]{1,0:T(8,128)(2,1)}, bf16[128,1024]{1,0:T(8,128)(2,1)S(1)}, u32[]{:S(2)}, u32[]{:S(2)}) collective-permute-start(bf16[128,1024]{1,0:T(8,128)(2,1)} %get-tuple-element.19.refs_1_), channel_id=1, source_target_pairs={{0,2},{2,0},{1,3},{3,1},{4,6},{6,4},{5,7},{7,5},{8,10},{10,8},{9,1... | collective-permute-start | bytes 786440 | tf_op jit(solution)/shard_map/ppermute | solution.py:153
  44.0 26.4 %copy-start.28 = (bf16[128,512]{1,0:T(8,128)(2,1)}, bf16[128,512]{1,0:T(8,128)(2,1)S(1)}, u32[]{:S(2)}) copy-start(bf16[128,512]{1,0:T(8,128)(2,1)S(1)} %collective-permute-done.31.refs_20_) | copy-start | bytes 393220
  44.0 9.5 %collective-permute-start.5 = (bf16[128,1024]{1,0:T(8,128)(2,1)}, bf16[128,1024]{1,0:T(8,128)(2,1)S(1)}, u32[]{:S(2)}, u32[]{:S(2)}) collective-permute-start(bf16[128,1024]{1,0:T(8,128)(2,1)} %get-tuple-element.18.refs_0_), channel_id=1, source_target_pairs={{0,16},{16,0},{1,17},{17,1},{2,18},{18,2},{3,19},{19,3},{4,20},{20... | collective-permute-start | bytes 786440 | tf_op jit(solution)/shard_map/ppermute | solution.py:153
  47.1 30.6 %copy-start.15 = (bf16[128,640]{1,0:T(8,128)(2,1)}, bf16[128,640]{1,0:T(8,128)(2,1)S(1)}, u32[]{:S(2)}) copy-start(bf16[128,640]{1,0:T(8,128)(2,1)S(1)} %collective-permute-done.20.refs_20_) | copy-start | bytes 491524
  47.1 10.2 %collective-permute-start.6 = (bf16[128,1024]{1,0:T(8,128)(2,1)}, bf16[128,1024]{1,0:T(8,128)(2,1)S(1)}, u32[]{:S(2)}, u32[]{:S(2)}) collective-permute-start(bf16[128,1024]{1,0:T(8,128)(2,1)} %get-tuple-element.19.refs_1_), channel_id=1, source_target_pairs={{0,16},{16,0},{1,17},{17,1},{2,18},{18,2},{3,19},{19,3},{4,20},{20... | collective-permute-start | bytes 786440 | tf_op jit(solution)/shard_map/ppermute | solution.py:153
  48.6 14.1 %collective-permute-start.11 = (bf16[128,1152]{1,0:T(8,128)(2,1)S(1)}, bf16[128,1152]{1,0:T(8,128)(2,1)S(1)}, u32[]{:S(2)}, u32[]{:S(2)}) collective-permute-start(bf16[128,1152]{1,0:T(8,128)(2,1)S(1)} %collective-permute-done.10.refs_10_), channel_id=1, source_target_pairs={{0,1},{1,0},{2,3},{3,2},{4,5},{5,4},{6,7},{7,6},{8,9},{9,8},{10,11... | collective-permute-start | bytes 884744 | tf_op jit(solution)/shard_map/ppermute | solution.py:153
  48.6 14.6 %collective-permute-start.14 = (bf16[128,1152]{1,0:T(8,128)(2,1)S(1)}, bf16[128,1152]{1,0:T(8,128)(2,1)S(1)}, u32[]{:S(2)}, u32[]{:S(2)}) collective-permute-start(bf16[128,1152]{1,0:T(8,128)(2,1)S(1)} %collective-permute-done.12.refs_12_), channel_id=1, source_target_pairs={{0,4},{4,12},{12,8},{8,0},{1,5},{5,13},{13,9},{9,1},{2,6},{6,14},{... | collective-permute-start | bytes 884744 | tf_op jit(solution)/shard_map/ppermute | solution.py:153
  49.5 8.6 %collective-permute-start.32 = (bf16[128,512]{1,0:T(8,128)(2,1)S(1)}, bf16[128,512]{1,0:T(8,128)(2,1)S(1)}, u32[]{:S(2)}, u32[]{:S(2)}) collective-permute-start(bf16[128,512]{1,0:T(8,128)(2,1)S(1)} %collective-permute-done.31.refs_20_), channel_id=1, source_target_pairs={{0,1},{1,0},{2,3},{3,2},{4,5},{5,4},{6,7},{7,6},{8,9},{9,8},{10,11... | collective-permute-start | bytes 393224 | tf_op jit(solution)/shard_map/ppermute | solution.py:153
  53.5 8.7 %collective-permute-start.33 = (bf16[128,512]{1,0:T(8,128)(2,1)S(1)}, bf16[128,512]{1,0:T(8,128)(2,1)S(1)}, u32[]{:S(2)}, u32[]{:S(2)}) collective-permute-start(bf16[128,512]{1,0:T(8,128)(2,1)S(1)} %collective-permute-done.31.refs_20_), channel_id=1, source_target_pairs={{0,4},{4,12},{12,8},{8,0},{1,5},{5,13},{13,9},{9,1},{2,6},{6,14},{... | collective-permute-start | bytes 393224 | tf_op jit(solution)/shard_map/ppermute | solution.py:153
  57.3 8.0 %collective-permute-start.22 = (bf16[128,640]{1,0:T(8,128)(2,1)S(1)}, bf16[128,640]{1,0:T(8,128)(2,1)S(1)}, u32[]{:S(2)}, u32[]{:S(2)}) collective-permute-start(bf16[128,640]{1,0:T(8,128)(2,1)S(1)} %collective-permute-done.20.refs_20_), channel_id=1, source_target_pairs={{0,4},{4,12},{12,8},{8,0},{1,5},{5,13},{13,9},{9,1},{2,6},{6,14},{... | collective-permute-start | bytes 491528 | tf_op jit(solution)/shard_map/ppermute | solution.py:153
  58.1 12.1 %collective-permute-start.13 = (bf16[128,1152]{1,0:T(8,128)(2,1)S(1)}, bf16[128,1152]{1,0:T(8,128)(2,1)S(1)}, u32[]{:S(2)}, u32[]{:S(2)}) collective-permute-start(bf16[128,1152]{1,0:T(8,128)(2,1)S(1)} %collective-permute-done.12.refs_12_), channel_id=1, source_target_pairs={{0,1},{1,0},{2,3},{3,2},{4,5},{5,4},{6,7},{7,6},{8,9},{9,8},{10,11... | collective-permute-start | bytes 884744 | tf_op jit(solution)/shard_map/ppermute | solution.py:153
  62.2 7.4 %collective-permute-start.7 = (bf16[128,1024]{1,0:T(8,128)(2,1)S(1)}, bf16[128,1024]{1,0:T(8,128)(2,1)S(1)}, u32[]{:S(2)}, u32[]{:S(2)}) collective-permute-start(bf16[128,1024]{1,0:T(8,128)(2,1)S(1)} %collective-permute-done.5.refs_4_), channel_id=1, source_target_pairs={{0,2},{2,0},{1,3},{3,1},{4,6},{6,4},{5,7},{7,5},{8,10},{10,8},{9,1... | collective-permute-start | bytes 786440 | tf_op jit(solution)/shard_map/ppermute | solution.py:153
  62.7 7.1 %collective-permute-start.8 = (bf16[128,1024]{1,0:T(8,128)(2,1)S(1)}, bf16[128,1024]{1,0:T(8,128)(2,1)S(1)}, u32[]{:S(2)}, u32[]{:S(2)}) collective-permute-start(bf16[128,1024]{1,0:T(8,128)(2,1)S(1)} %collective-permute-done.4.refs_3_), channel_id=1, source_target_pairs={{0,16},{16,0},{1,17},{17,1},{2,18},{18,2},{3,19},{19,3},{4,20},{20... | collective-permute-start | bytes 786440 | tf_op jit(solution)/shard_map/ppermute | solution.py:153
  63.2 7.2 %collective-permute-start.15 = (bf16[128,1152]{1,0:T(8,128)(2,1)S(1)}, bf16[128,1152]{1,0:T(8,128)(2,1)S(1)}, u32[]{:S(2)}, u32[]{:S(2)}) collective-permute-start(bf16[128,1152]{1,0:T(8,128)(2,1)S(1)} %collective-permute-done.14.refs_14_), channel_id=1, source_target_pairs={{0,1},{1,0},{2,3},{3,2},{4,5},{5,4},{6,7},{7,6},{8,9},{9,8},{10,11... | collective-permute-start | bytes 884744 | tf_op jit(solution)/shard_map/ppermute | solution.py:153
  65.2 1.3 %collective-permute-start.34 = (bf16[128,512]{1,0:T(8,128)(2,1)S(1)}, bf16[128,512]{1,0:T(8,128)(2,1)S(1)}, u32[]{:S(2)}, u32[]{:S(2)}) collective-permute-start(bf16[128,512]{1,0:T(8,128)(2,1)S(1)} %collective-permute-done.33.refs_22_), channel_id=1, source_target_pairs={{0,1},{1,0},{2,3},{3,2},{4,5},{5,4},{6,7},{7,6},{8,9},{9,8},{10,11... | collective-permute-start | bytes 393224 | tf_op jit(solution)/shard_map/ppermute | solution.py:153
  66.6 11.0 %collective-permute-start.17 = (bf16[128,640]{1,0:T(8,128)(2,1)S(1)}, bf16[128,640]{1,0:T(8,128)(2,1)S(1)}, u32[]{:S(2)}, u32[]{:S(2)}) collective-permute-start(bf16[128,640]{1,0:T(8,128)(2,1)S(1)} %collective-permute-done.16.refs_16_), channel_id=1, source_target_pairs={{0,1},{1,0},{2,3},{3,2},{4,5},{5,4},{6,7},{7,6},{8,9},{9,8},{10,11... | collective-permute-start | bytes 491528 | tf_op jit(solution)/shard_map/ppermute | solution.py:153
  69.6 8.0 %collective-permute-start.19 = (bf16[128,640]{1,0:T(8,128)(2,1)S(1)}, bf16[128,640]{1,0:T(8,128)(2,1)S(1)}, u32[]{:S(2)}, u32[]{:S(2)}) collective-permute-start(bf16[128,640]{1,0:T(8,128)(2,1)S(1)} %collective-permute-done.18.refs_18_), channel_id=1, source_target_pairs={{0,1},{1,0},{2,3},{3,2},{4,5},{5,4},{6,7},{7,6},{8,9},{9,8},{10,11... | collective-permute-start | bytes 491528 | tf_op jit(solution)/shard_map/ppermute | solution.py:153
  69.9 7.8 %collective-permute-start.21 = (bf16[128,640]{1,0:T(8,128)(2,1)S(1)}, bf16[128,640]{1,0:T(8,128)(2,1)S(1)}, u32[]{:S(2)}, u32[]{:S(2)}) collective-permute-start(bf16[128,640]{1,0:T(8,128)(2,1)S(1)} %collective-permute-done.20.refs_20_), channel_id=1, source_target_pairs={{0,1},{1,0},{2,3},{3,2},{4,5},{5,4},{6,7},{7,6},{8,9},{9,8},{10,11... | collective-permute-start | bytes 491528 | tf_op jit(solution)/shard_map/ppermute | solution.py:153
  70.1 7.5 %collective-permute-start.23 = (bf16[128,640]{1,0:T(8,128)(2,1)S(1)}, bf16[128,640]{1,0:T(8,128)(2,1)S(1)}, u32[]{:S(2)}, u32[]{:S(2)}) collective-permute-start(bf16[128,640]{1,0:T(8,128)(2,1)S(1)} %collective-permute-done.22.refs_22_), channel_id=1, source_target_pairs={{0,1},{1,0},{2,3},{3,2},{4,5},{5,4},{6,7},{7,6},{8,9},{9,8},{10,11... | collective-permute-start | bytes 491528 | tf_op jit(solution)/shard_map/ppermute | solution.py:153
  76.2 12.2 %collective-permute-start.35 = (bf16[128,512]{1,0:T(8,128)(2,1)}, bf16[128,512]{1,0:T(8,128)(2,1)S(1)}, u32[]{:S(2)}, u32[]{:S(2)}) collective-permute-start(bf16[128,512]{1,0:T(8,128)(2,1)} %get-tuple-element.28), channel_id=1, source_target_pairs={{0,2},{2,0},{1,3},{3,1},{4,6},{6,4},{5,7},{7,5},{8,10},{10,8},{9,1... | collective-permute-start | bytes 393224 | tf_op jit(solution)/shard_map/ppermute | solution.py:153
  84.4 15.9 %collective-permute-start.24 = (bf16[128,640]{1,0:T(8,128)(2,1)}, bf16[128,640]{1,0:T(8,128)(2,1)S(1)}, u32[]{:S(2)}, u32[]{:S(2)}) collective-permute-start(bf16[128,640]{1,0:T(8,128)(2,1)} %get-tuple-element.23), channel_id=1, source_target_pairs={{0,2},{2,0},{1,3},{3,1},{4,6},{6,4},{5,7},{7,5},{8,10},{10,8},{9,1... | collective-permute-start | bytes 491528 | tf_op jit(solution)/shard_map/ppermute | solution.py:153
  85.2 15.2 %collective-permute-start.25 = (bf16[128,640]{1,0:T(8,128)(2,1)}, bf16[128,640]{1,0:T(8,128)(2,1)S(1)}, u32[]{:S(2)}, u32[]{:S(2)}) collective-permute-start(bf16[128,640]{1,0:T(8,128)(2,1)} %get-tuple-element.24), channel_id=1, source_target_pairs={{0,16},{16,0},{1,17},{17,1},{2,18},{18,2},{3,19},{19,3},{4,20},{20... | collective-permute-start | bytes 491528 | tf_op jit(solution)/shard_map/ppermute | solution.py:153
  85.7 14.7 %collective-permute-start.26 = (bf16[128,640]{1,0:T(8,128)(2,1)}, bf16[128,640]{1,0:T(8,128)(2,1)S(1)}, u32[]{:S(2)}, u32[]{:S(2)}) collective-permute-start(bf16[128,640]{1,0:T(8,128)(2,1)} %get-tuple-element.25), channel_id=1, source_target_pairs={{0,18},{2,16},{16,2},{18,0},{1,19},{3,17},{17,3},{19,1},{4,22},{6,... | collective-permute-start | bytes 491528 | tf_op jit(solution)/shard_map/ppermute | solution.py:152
  87.9 12.3 %collective-permute-start.36 = (bf16[128,512]{1,0:T(8,128)(2,1)S(1)}, bf16[128,512]{1,0:T(8,128)(2,1)S(1)}, u32[]{:S(2)}, u32[]{:S(2)}) collective-permute-start(bf16[128,512]{1,0:T(8,128)(2,1)S(1)} %copy-done.39), channel_id=1, source_target_pairs={{0,16},{16,0},{1,17},{17,1},{2,18},{18,2},{3,19},{19,3},{4,20},{20... | collective-permute-start | bytes 393224 | tf_op jit(solution)/shard_map/ppermute | solution.py:153
  88.5 11.8 %collective-permute-start.37 = (bf16[128,512]{1,0:T(8,128)(2,1)S(1)}, bf16[128,512]{1,0:T(8,128)(2,1)S(1)}, u32[]{:S(2)}, u32[]{:S(2)}) collective-permute-start(bf16[128,512]{1,0:T(8,128)(2,1)S(1)} %copy-done.38), channel_id=1, source_target_pairs={{0,18},{2,16},{16,2},{18,0},{1,19},{3,17},{17,3},{19,1},{4,22},{6,... | collective-permute-start | bytes 393224 | tf_op jit(solution)/shard_map/ppermute | solution.py:152
  (31 other events, 224.8 us)

commit v2 on v1

--- a/solution.py
+++ b/solution.py
@@ -18,9 +18,15 @@
 norm_eps = 1e-06
 
 CHUNKS = (640, 512)
-VMEM_LIMIT = 56 * 2**20
+TIES = {'rd2': ('rd1',), 'd1': ('B1',), 'cB0': ('y2',), 'cB1': ('B2',), 'ca0': ('cB0',)}
+COSTS = {'att': 3000, 'cut': 1500, 'stage': 9000, 'finish': 1500, 'proj1': 6000}
+PER_CYCLE = 524288
+FIRST = ()
+ACTS = 2
+WHOLE = 2
+VMEM_LIMIT = 14 * 2**20
 VMEM = pl.BlockSpec(memory_space=pltpu.VMEM)
-ANY = pl.BlockSpec(memory_space=pl.ANY)
+HBM = pl.BlockSpec(memory_space=pl.ANY)
 
 
 def params():
@@ -35,28 +41,30 @@
     return list(range(0, 2, 1))[:1] + list(range(1, n, 2)) + list(range(2, n, 2))[::-1]
 
 
-def cut_weight(w_ref, *rest):
-    outs, sems = rest[:-1], rest[-1]
-    quarter = w_ref.shape[1] // 2
+def cut(w_ref, near, away):
+    quarter = near.shape[1]
     me = lax.axis_index("x")
-    copies = []
+    near[...] = w_ref[:, pl.ds(pl.multiple_of(me * quarter, 128), quarter)]
+    away[...] = w_ref[:, pl.ds(pl.multiple_of((1 - me) * quarter, 128), quarter)]
+
+
+def stage(*refs):
+    half = len(refs) // 2
+    for ref, out in zip(refs[:half], refs[half:]):
+        out[...] = ref[...]
+
+
+def split(ref, *outs):
     start = 0
-    for i, (out, side) in enumerate(zip(outs, (me, 1 - me, 1 - me))):
-        if i == 2:
-            start = outs[1].shape[1]
-        at = pl.multiple_of(side * quarter + start, 128)
-        copies.append(
-            pltpu.make_async_copy(w_ref.at[:, pl.ds(at, out.shape[1])], out, sems.at[i])
-        )
-    for copy in copies:
-        copy.start()
-    for copy in copies:
-        copy.wait()
+    for out in outs:
+        out[...] = ref[:, pl.ds(start, out.shape[1])]
+        start += out.shape[1]
 
 
 def attend(q_ref, k_own, k_far, v_own, v_far, pos_own, pos_far, *outs):
     tokens = q_ref.shape[0]
     groups = HQ // HK
+    per = HQ // len(outs)
     own = pos_own[...].astype(jnp.float32)
     far = pos_far[...].astype(jnp.float32)
     mine = jnp.transpose(jnp.broadcast_to(own, (tokens, tokens)))[:, :1]
@@ -64,9 +72,8 @@
     visible = jnp.concatenate([visible] * groups, axis=0)
     for head in range(HK):
         at = pl.ds(head * DH, DH)
-        query = jnp.concatenate(
-            [q_ref[:, pl.ds((head * groups + g) * DH, DH)] for g in range(groups)], axis=0
-        )
+        q_at = [pl.ds((head * groups + g) * DH, DH) for g in range(groups)]
+        query = jnp.concatenate([q_ref[:, each] for each in q_at], axis=0)
         keys = jnp.concatenate([k_own[:, at], k_far[:, at]], axis=0)
         values = jnp.concatenate([v_own[:, at], v_far[:, at]], axis=0)
         scores = lax.dot_general(
@@ -79,7 +86,6 @@
         mixed = (mixed / total).astype(jnp.bfloat16)
         for g in range(groups):
             h = head * groups + g
-            per = HQ // len(outs)
             outs[h // per][:, pl.ds((h % per) * DH, DH)] = mixed[g * tokens : (g + 1) * tokens]
 
 
@@ -94,31 +100,30 @@
     return (source * 2 + x) * 2 + core
 
 
-def project(ring, first, groups, halves, *refs):
+def project(ring, first, sizes, *refs):
     n = len(ring)
-    acts = refs[: groups * halves]
-    near = refs[groups * halves : groups * halves + 2 * n]
-    away = refs[groups * halves + 2 * n : groups * halves + 4 * n]
-    outs = refs[groups * halves + 4 * n : groups * halves + 4 * n + groups]
+    count = sum(sizes)
+    acts, bufs, outs = refs[:count], refs[count : count + 4 * n], refs[count + 4 * n : -2]
     a_all, w_all = refs[-2:]
     tokens, columns = outs[0].shape
-    wide = acts[0].shape[1]
-    for g in range(groups):
-        for half in range(halves):
-            a_all[pl.ds(g * tokens, tokens), pl.ds(half * wide, wide)] = acts[g * halves + half][...]
-    for same_x, bufs, at in ((True, near, first), (False, away, 0)):
-        for step in range(n):
-            for other, same_core in enumerate((True, False)):
-                head = head_of(step, same_x, same_core, ring)
-                w_all[pl.ds(pl.multiple_of(head * DH, DH), DH), :] = bufs[step * 2 + other][
-                    :, pl.ds(at, columns)
-                ]
-    for g in range(groups // 2):
+    taken = 0
+    for g, parts in enumerate(sizes):
+        at = 0
+        for act in acts[taken : taken + parts]:
+            a_all[pl.ds(g * tokens, tokens), pl.ds(at, act.shape[1])] = act[...]
+            at += act.shape[1]
+        taken += parts
+    for i, buf in enumerate(bufs):
+        same_x, step, same_core = i < 2 * n, i // 2 % n, i % 2 == 0
+        head = head_of(step, same_x, same_core, ring)
+        at = 0 if buf.shape[1] == columns else first
+        w_all[pl.ds(pl.multiple_of(head * DH, DH), DH), :] = buf[:, pl.ds(at, columns)]
+    for g in range(0, len(outs), 2):
         rows = jnp.dot(
-            a_all[pl.ds(g * 2 * tokens, 2 * tokens), :], w_all[...], preferred_element_type=jnp.float32
+            a_all[pl.ds(g * tokens, 2 * tokens), :], w_all[...], preferred_element_type=jnp.float32
         ).astype(jnp.bfloat16)
-        outs[2 * g][...] = rows[:tokens]
-        outs[2 * g + 1][...] = rows[tokens:]
+        outs[g][...] = rows[:tokens]
+        outs[g + 1][...] = rows[tokens:]
 
 
 def finish(chunks, hidden_ref, gain_ref, *refs):
@@ -152,71 +157,124 @@
             return lax.ppermute(value, ("ctx", "x"), [(i, 3 - i) for i in range(4)])
         return lax.ppermute(value, axis, along if axis == "z" else swap)
 
-    query, key, value = query_proj[0], key_proj[0], value_proj[0]
-    pos_far = over(order_pos, "ctx")
-    key_far = over(key, "ctx")
-    value_far = over(value, "ctx")
-
-    quarter = out_weight.shape[1] // 2
-    rows = out_weight.shape[0]
-    near, *sent = pl.pallas_call(
-        cut_weight,
-        out_shape=[bf16(rows, quarter)] + [bf16(rows, c) for c in chunks],
-        in_specs=[ANY],
-        out_specs=[VMEM] * 3,
-        scratch_shapes=[pltpu.SemaphoreType.DMA((3,))],
-        compiler_params=params(),
-        name="cut_weight",
-    )(out_weight)
-    away = [over(piece, "x") for piece in sent]
-
-    def gather(piece):
-        held = [piece]
-        for _ in range(n - 1):
-            held.append(over(held[-1], "z"))
-        both = []
-        for piece in held:
-            both += [piece, over(piece, "core")]
-        return both
-
-    near = gather(near)
-    away = [gather(piece) for piece in away]
-
-    halves = 2
-    acts = pl.pallas_call(
-        attend,
-        out_shape=[bf16(tokens, HQ * DH // halves)] * halves,
-        in_specs=[VMEM] * 7,
-        out_specs=[VMEM] * halves,
-        compiler_params=params(),
-        cost_estimate=pl.CostEstimate(flops=2**28, bytes_accessed=2**21, transcendentals=2**20),
-        name="attend",
-    )(query, key, key_far, value, value_far, order_pos, pos_far)
-    acts_x = [over(a, "x") for a in acts]
-    acts_y = [over(a, "ctx") for a in acts]
-    acts_d = [over(acts_y[0], "x"), over(acts_x[1], "ctx")]
-    all_acts = [*acts, *acts_x, *acts_y, *acts_d]
-
-    pieces = []
-    start = 0
-    for columns, far in zip(chunks, away):
-        out = pl.pallas_call(
-            functools.partial(project, ring, start, 4, halves),
-            out_shape=[bf16(tokens, columns)] * 4,
-            in_specs=[VMEM] * (4 * halves + 4 * n),
-            out_specs=[VMEM] * 4,
-            scratch_shapes=[
+    rows, block = out_weight.shape
+    quarter = block // 2
+
+    def call(body, outs, ins, name, scratch=(), label=None):
+        return pl.pallas_call(
+            body,
+            out_shape=outs,
+            in_specs=[VMEM] * ins,
+            out_specs=[VMEM] * len(outs),
+            scratch_shapes=scratch,
+            compiler_params=params(),
+            cost_estimate=pl.CostEstimate(
+                flops=int(COSTS.get(label or name, 0) * PER_CYCLE) + 1, bytes_accessed=0, transcendentals=0
+            ),
+            name=name,
+        )
+
+    def project_chunk(c, sizes, count):
+        columns = chunks[c]
+        return call(
+            functools.partial(project, ring, sum(chunks[:c]), sizes),
+            [bf16(tokens, columns)] * 4,
+            count,
+            "project",
+            [
                 pltpu.VMEM((4 * tokens, HQ * DH), jnp.bfloat16),
                 pltpu.VMEM((HQ * DH, columns), jnp.bfloat16),
             ],
-            compiler_params=params(),
-            cost_estimate=pl.CostEstimate(
-                flops=8 * tokens * HQ * DH * columns, bytes_accessed=2**22, transcendentals=0
-            ),
-            name="project",
-        )(*all_acts, *near, *far)
-        pieces += [out[0], over(out[1], "x"), over(out[2], "ctx"), over(out[3], "diag")]
-        start += columns
+            label="proj" + str(c + 1),
+        )
+
+    moves, kernels = {}, {}
+    kernels["cut"] = (call(cut, [bf16(rows, quarter)] * 2, 1, "cut"), ("w",), ("a0", "awayo"))
+    kernels["stage"] = (
+        call(
+            stage,
+            [bf16(tokens, a.shape[2]) for a in (query_proj, key_proj, value_proj)]
+            + [jax.ShapeDtypeStruct(order_pos.shape, jnp.int32)],
+            4,
+            "stage",
+        ),
+        ("qo", "Ko", "Vo", "poso"),
+        ("q", "Kq", "Vq", "posq"),
+    )
+    wide = bf16(tokens, HQ * DH // ACTS)
+    halves = "12"[:ACTS]
+    for k, axis in (("K", "ctx"), ("V", "ctx"), ("pos", "ctx"), ("B0", "x")):
+        moves[k] = ({"B0": "awayo"}.get(k, k + "o"), axis)
+    kernels["att"] = (
+        call(attend, [wide] * ACTS, 7, "attend", label="att"),
+        ("q", "Kq", "K", "Vq", "V", "posq", "pos"),
+        tuple("h" + i for i in halves),
+    )
+    for i in halves:
+        moves["x" + i] = ("h" + i, "x")
+        moves["y" + i] = ("h" + i, "ctx")
+    if ACTS == 2:
+        moves["d1"], moves["d2"] = ("y1", "x"), ("x2", "ctx")
+        acts = ("h1", "h2", "x1", "x2", "y1", "y2", "d1", "d2")
+        sizes = (2, 2, 2, 2)
+    else:
+        half = bf16(tokens, HQ * DH // 2)
+        kernels["hy"] = (call(split, [half] * 2, 1, "halves", label="hy"), ("y1",), ("y1l", "y1r"))
+        kernels["hx"] = (call(split, [half] * 2, 1, "halves", label="hx"), ("x1",), ("x1l", "x1r"))
+        moves["d1"], moves["d2"] = ("y1l", "x"), ("x1r", "ctx")
+        acts, sizes = ("h1", "x1", "y1", "d1", "d2"), (1, 1, 1, 2)
+    for i in range(1, n):
+        moves["a%d" % i] = ("a%d" % (i - 1), "z")
+    for i in range(1, WHOLE + 1):
+        moves["B%d" % i] = ("B%d" % (i - 1), "z")
+    last = "B%d" % WHOLE
+    kernels["split"] = (
+        call(split, [bf16(rows, c) for c in chunks], 1, "split"),
+        (last,),
+        tuple("b%d%d" % (c + 1, WHOLE) for c in range(len(chunks))),
+    )
+    for c in range(len(chunks)):
+        j = str(c + 1)
+        for i in range(WHOLE + 1, n):
+            moves["b%s%d" % (j, i)] = ("b%s%d" % (j, i - 1), "z")
+        away = ["B%d" % i for i in range(WHOLE + 1)] + ["b%s%d" % (j, i) for i in range(WHOLE + 1, n)]
+        bufs = []
+        for name in ["a%d" % i for i in range(n)] + away:
+            moves["c" + name] = (name, "core")
+            bufs += [name, "c" + name]
+        operands = (*acts, *bufs)
+        results = tuple("p" + k + j for k in "oxyd")
+        kernels["proj" + j] = (project_chunk(c, sizes, len(operands)), operands, results)
+        for k, axis in zip("xyd", ("x", "ctx", "diag")):
+            moves["r" + k + j] = ("p" + k + j, axis)
+
+    held = dict(
+        w=out_weight, qo=query_proj[0], Ko=key_proj[0], Vo=value_proj[0], poso=order_pos
+    )
+
+    def after(value, deps):
+        for dep in deps:
+            token, held[dep] = lax.optimization_barrier((lax.create_token(), held[dep]))
+            token, value = lax.optimization_barrier((token, value))
+        return value
+
+    pending = list(kernels) + list(moves)
+    pending.sort(key=lambda name: FIRST.index(name) if name in FIRST else len(FIRST))
+    while pending:
+        for name in pending:
+            sources, results = (moves[name][:1], (name,)) if name in moves else kernels[name][1:]
+            deps = [d for d in TIES.get(name, ())]
+            if all(k in held for k in (*sources, *deps)):
+                break
+        pending.remove(name)
+        first = after(held[sources[0]], deps)
+        if name in moves:
+            held[name] = over(first, moves[name][1])
+        else:
+            out = kernels[name][0](first, *(held[k] for k in sources[1:]))
+            held.update(zip(results, out))
+
+    pieces = [held[("po" if k == "o" else "r" + k) + str(c + 1)] for c in range(len(chunks)) for k in "oxyd"]
 
     out = pl.pallas_call(
         functools.partial(finish, chunks),
@@ -224,6 +282,7 @@
         in_specs=[VMEM] * (2 + len(pieces)),
         out_specs=VMEM,
         compiler_params=params(),
+        cost_estimate=pl.CostEstimate(flops=1, bytes_accessed=0, transcendentals=0),
         name="finish",
     )(hidden_rows[0], post_gain.reshape(1, width), *pieces)
     return out[None]

time: 105 us -> 67.8 us (0.65)
  waiting for transfers between devices: 52.1 us -> 25.7 us
  Pallas kernels: 18.5 us -> 6.57 us
  starting transfers between devices: 29.8 us -> 34.2 us
  local copies, waits for them, and re-layouts: 4 us -> 1.1 us
    ppermute x36 -> x30, waiting for transfers between devices: 52 us -> 25.5 us  [over(): return lax.ppermute(value, axis, along if axis == 'z' else swap)]
    pallas_call x4 -> x6, Pallas kernels: 15 us -> 4.69 us  [shards(): out = kernels[name][0](first, *(held[k] for k in sources[1:]))]
    ppermute x36 -> x30, starting transfers between devices: 25.8 us -> 30.6 us  [over(): return lax.ppermute(value, axis, along if axis == 'z' else swap)]
    unnamed x82 -> x14, local copies, waits for them, and re-layouts: 3.4 us -> 1.09 us
    pallas_call x1, Pallas kernels: 3.54 us -> 1.88 us  [shards(): pl.pallas_call(functools.partial(finish, chunks), out_shape=bf16(tokens,...]
  transfers between devices with their start and end apart: 38 -> 32, of which waited for: 13 -> 14; matrix products, arithmetic and copies ran while one was open for 1% -> 0% of each run, Pallas kernels for 12% -> 7%
where the time goes in v2:
time: 67.8 us; the launch traced here: 67.7 us
  starting transfers between devices  34.2 us (50%)
  waiting for transfers between devices  25.7 us (38%)
  Pallas kernels  6.57 us (10%)
  local copies, waits for them, and re-layouts  1.1 us (2%)
    ppermute x30, starting transfers between devices, over(): return lax.ppermute(value, axis, along if axis == 'z' else swap)  30.6 us
    ppermute x30, waiting for transfers between devices, over(): return lax.ppermute(value, axis, along if axis == 'z' else swap)  25.5 us
    pallas_call x6, Pallas kernels, shards(): out = kernels[name][0](first, *(held[k] for k in sources[1:]))  4.69 us
    ppermute x2, starting transfers between devices, over(): return lax.ppermute(value, ('ctx', 'x'), [(i, 3 - i) for i in range(4)])  3.55 us
    pallas_call x1, Pallas kernels, shards(): pl.pallas_call(functools.partial(finish, chunks), out_shape=bf16(tokens,...  1.88 us
  transfers between devices with their start and end apart: 32, of which 14 were waited for; matrix products, arithmetic and copies ran while one was open for 0% of the time, Pallas kernels for 7%

profile of v2, /device:TPU:0, one launch (start us, length us, event | category | flops | bytes accessed | tf_op | source)
XLA Modules:
  0.0 67.7 jit_solution(1529245645016077508)
XLA Ops:
  0.0 3.0 %collective-permute-start = (bf16[128,1024]{1,0:T(8,128)(2,1)}, bf16[128,1024]{1,0:T(8,128)(2,1)S(1)}, u32[]{:S(2)}, u32[]{:S(2)}) collective-permute-start(bf16[128,1024]{1,0:T(8,128)(2,1)} %bitcast.7), channel_id=1, source_target_pairs={{0,16},{16,0},{1,17},{17,1},{2,18},{18,2},{3,19},{19,3},{4,20},{20... | collective-permute-start | bytes 786440 | tf_op jit(solution)/shard_map/ppermute | solution.py:158
  3.0 0.1 collective-permute-start.1
  3.0 2.0 %collective-permute-start.2 = (s32[1,128]{1,0:T(1,128)}, s32[1,128]{1,0:T(1,128)S(1)}, u32[]{:S(2)}, u32[]{:S(2)}) collective-permute-start(s32[1,128]{1,0:T(1,128)} %refs_3_.1), channel_id=1, source_target_pairs={{0,16},{16,0},{1,17},{17,1},{2,18},{18,2},{3,19},{19,3},{4,20},{20... | collective-permute-start | bytes 1544 | tf_op jit(solution)/shard_map/ppermute | solution.py:158
  5.0 1.1 %copy-done.1 = bf16[128,2304]{1,0:T(8,128)(2,1)S(1)} copy-done((bf16[128,2304]{1,0:T(8,128)(2,1)S(1)}, bf16[128,2304]{1,0:T(8,128)(2,1)}, u32[]{:S(2)}) %copy-start.1) | copy-done | bytes 589848
  6.1 1.6 %collective-permute-start.7 = (bf16[128,1152]{1,0:T(8,128)(2,1)S(1)}, bf16[128,1152]{1,0:T(8,128)(2,1)S(1)}, u32[]{:S(2)}, u32[]{:S(2)}) collective-permute-start(bf16[128,1152]{1,0:T(8,128)(2,1)S(1)} %get-tuple-element.45), channel_id=1, source_target_pairs={{0,2},{2,0},{1,3},{3,1},{4,6},{6,4},{5,7},{7,5},{8,10},{10,8},{9,1... | collective-permute-start | bytes 884744 | tf_op jit(solution)/shard_map/ppermute | solution.py:158
  7.7 1.6 %collective-permute-start.13 = (bf16[128,1152]{1,0:T(8,128)(2,1)S(1)}, bf16[128,1152]{1,0:T(8,128)(2,1)S(1)}, u32[]{:S(2)}, u32[]{:S(2)}) collective-permute-start(bf16[128,1152]{1,0:T(8,128)(2,1)S(1)} %get-tuple-element.52.refs_8_), channel_id=1, source_target_pairs={{0,4},{4,12},{12,8},{8,0},{1,5},{5,13},{13,9},{9,1},{2,6},{6,14},{... | collective-permute-start | bytes 884744 | tf_op jit(solution)/shard_map/ppermute | solution.py:158
  9.3 0.1 stage.1
  9.3 4.7 %collective-permute-done.7.refs_16_ = bf16[128,1152]{1,0:T(8,128)(2,1)S(1)} collective-permute-done((bf16[128,1152]{1,0:T(8,128)(2,1)S(1)}, bf16[128,1152]{1,0:T(8,128)(2,1)S(1)}, u32[]{:S(2)}, u32[]{:S(2)}) %collective-permute-start.7) | collective-permute-done | bytes 294944 | tf_op jit(solution)/shard_map/ppermute | solution.py:158
  14.1 1.6 %collective-permute-start.8 = (bf16[128,1152]{1,0:T(8,128)(2,1)S(1)}, bf16[128,1152]{1,0:T(8,128)(2,1)S(1)}, u32[]{:S(2)}, u32[]{:S(2)}) collective-permute-start(bf16[128,1152]{1,0:T(8,128)(2,1)S(1)} %collective-permute-done.7.refs_16_), channel_id=1, source_target_pairs={{0,4},{4,12},{12,8},{8,0},{1,5},{5,13},{13,9},{9,1},{2,6},{6,14},{... | collective-permute-start | bytes 884744 | tf_op jit(solution)/shard_map/ppermute | solution.py:158
  15.7 0.0 collective-permute-done.2.pos_far
  15.7 0.0 collective-permute-done.k_far
  15.7 0.0 collective-permute-done.1.v_far
  15.7 1.1 %attend.1 = (bf16[128,1024]{1,0:T(8,128)(2,1)S(1)}, bf16[128,1024]{1,0:T(8,128)(2,1)S(1)}) custom-call(bf16[128,2048]{1,0:T(8,128)(2,1)S(1)} %get-tuple-element.38.q_ref, bf16[128,1024]{1,0:T(8,128)(2,1)S(1)} %get-tuple-element.39.k_own, bf16[128,1024]{1,0:T(8,128)(2,1)S(1)} %collective-permute-done.k_far, bf16[128,1024]{1,0:T(8,128)(2,1)S(1)} %get-tuple-element.40.v_own, ...), custom_call_target="tpu_custom_call" | custom-call | flops 1572864000 | tf_op jit(solution)/shard_map/attend/pallas_call | solution.py:274
  16.8 1.6 %collective-permute-start.3 = (bf16[128,1024]{1,0:T(8,128)(2,1)S(1)}, bf16[128,1024]{1,0:T(8,128)(2,1)S(1)}, u32[]{:S(2)}, u32[]{:S(2)}) collective-permute-start(bf16[128,1024]{1,0:T(8,128)(2,1)S(1)} %get-tuple-element.42.refs_0_), channel_id=1, source_target_pairs={{0,2},{2,0},{1,3},{3,1},{4,6},{6,4},{5,7},{7,5},{8,10},{10,8},{9,1... | collective-permute-start | bytes 786440 | tf_op jit(solution)/shard_map/ppermute | solution.py:158
  18.4 1.2 %collective-permute-start.6 = (bf16[128,1024]{1,0:T(8,128)(2,1)S(1)}, bf16[128,1024]{1,0:T(8,128)(2,1)S(1)}, u32[]{:S(2)}, u32[]{:S(2)}) collective-permute-start(bf16[128,1024]{1,0:T(8,128)(2,1)S(1)} %get-tuple-element.43.refs_1_), channel_id=1, source_target_pairs={{0,16},{16,0},{1,17},{17,1},{2,18},{18,2},{3,19},{19,3},{4,20},{20... | collective-permute-start | bytes 786440 | tf_op jit(solution)/shard_map/ppermute | solution.py:158
  19.6 1.9 %collective-permute-start.15 = (bf16[128,1152]{1,0:T(8,128)(2,1)S(1)}, bf16[128,1152]{1,0:T(8,128)(2,1)S(1)}, u32[]{:S(2)}, u32[]{:S(2)}) collective-permute-start(bf16[128,1152]{1,0:T(8,128)(2,1)S(1)} %collective-permute-done.13.refs_10_), channel_id=1, source_target_pairs={{0,4},{4,12},{12,8},{8,0},{1,5},{5,13},{13,9},{9,1},{2,6},{6,14},{... | collective-permute-start | bytes 884744 | tf_op jit(solution)/shard_map/ppermute | solution.py:158
  21.5 0.5 collective-permute-start.4
  22.0 1.5 %collective-permute-done.8.refs_18_ = bf16[128,1152]{1,0:T(8,128)(2,1)S(1)} collective-permute-done((bf16[128,1152]{1,0:T(8,128)(2,1)S(1)}, bf16[128,1152]{1,0:T(8,128)(2,1)S(1)}, u32[]{:S(2)}, u32[]{:S(2)}) %collective-permute-start.8) | collective-permute-done | bytes 294944 | tf_op jit(solution)/shard_map/ppermute | solution.py:158
  23.5 2.2 %collective-permute-done.3.refs_2_ = bf16[128,1024]{1,0:T(8,128)(2,1)S(1)} collective-permute-done((bf16[128,1024]{1,0:T(8,128)(2,1)S(1)}, bf16[128,1024]{1,0:T(8,128)(2,1)S(1)}, u32[]{:S(2)}, u32[]{:S(2)}) %collective-permute-start.3) | collective-permute-done | bytes 262176 | tf_op jit(solution)/shard_map/ppermute | solution.py:158
  25.7 1.6 %collective-permute-start.19 = (bf16[128,1152]{1,0:T(8,128)(2,1)S(1)}, bf16[128,1152]{1,0:T(8,128)(2,1)S(1)}, u32[]{:S(2)}, u32[]{:S(2)}) collective-permute-start(bf16[128,1152]{1,0:T(8,128)(2,1)S(1)} %collective-permute-done.8.refs_18_), channel_id=1, source_target_pairs={{0,4},{4,12},{12,8},{8,0},{1,5},{5,13},{13,9},{9,1},{2,6},{6,14},{... | collective-permute-start | bytes 884744 | tf_op jit(solution)/shard_map/ppermute | solution.py:158
  27.3 1.3 %collective-permute-start.5 = (bf16[128,1024]{1,0:T(8,128)(2,1)S(1)}, bf16[128,1024]{1,0:T(8,128)(2,1)S(1)}, u32[]{:S(2)}, u32[]{:S(2)}) collective-permute-start(bf16[128,1024]{1,0:T(8,128)(2,1)S(1)} %get-tuple-element.42.refs_0_), channel_id=1, source_target_pairs={{0,16},{16,0},{1,17},{17,1},{2,18},{18,2},{3,19},{19,3},{4,20},{20... | collective-permute-start | bytes 786440 | tf_op jit(solution)/shard_map/ppermute | solution.py:158
  28.6 0.8 %collective-permute-done.4.refs_3_ = bf16[128,1024]{1,0:T(8,128)(2,1)S(1)} collective-permute-done((bf16[128,1024]{1,0:T(8,128)(2,1)S(1)}, bf16[128,1024]{1,0:T(8,128)(2,1)S(1)}, u32[]{:S(2)}, u32[]{:S(2)}) %collective-permute-start.4) | collective-permute-done | bytes 262176 | tf_op jit(solution)/shard_map/ppermute | solution.py:158
  29.4 0.7 collective-permute-done.15.refs_12_
  30.1 1.5 %collective-permute-start.17 = (bf16[128,1152]{1,0:T(8,128)(2,1)S(1)}, bf16[128,1152]{1,0:T(8,128)(2,1)S(1)}, u32[]{:S(2)}, u32[]{:S(2)}) collective-permute-start(bf16[128,1152]{1,0:T(8,128)(2,1)S(1)} %collective-permute-done.15.refs_12_), channel_id=1, source_target_pairs={{0,4},{4,12},{12,8},{8,0},{1,5},{5,13},{13,9},{9,1},{2,6},{6,14},{... | collective-permute-start | bytes 884744 | tf_op jit(solution)/shard_map/ppermute | solution.py:158
  31.6 2.1 %collective-permute-done.5.refs_4_ = bf16[128,1024]{1,0:T(8,128)(2,1)S(1)} collective-permute-done((bf16[128,1024]{1,0:T(8,128)(2,1)S(1)}, bf16[128,1024]{1,0:T(8,128)(2,1)S(1)}, u32[]{:S(2)}, u32[]{:S(2)}) %collective-permute-start.5) | collective-permute-done | bytes 262176 | tf_op jit(solution)/shard_map/ppermute | solution.py:158
  33.7 1.3 %collective-permute-start.10 = (bf16[128,1024]{1,0:T(8,128)(2,1)S(1)}, bf16[128,1024]{1,0:T(8,128)(2,1)S(1)}, u32[]{:S(2)}, u32[]{:S(2)}) collective-permute-start(bf16[128,1024]{1,0:T(8,128)(2,1)S(1)} %collective-permute-done.4.refs_3_), channel_id=1, source_target_pairs={{0,16},{16,0},{1,17},{17,1},{2,18},{18,2},{3,19},{19,3},{4,20},{20... | collective-permute-start | bytes 786440 | tf_op jit(solution)/shard_map/ppermute | solution.py:158
  35.0 1.6 %collective-permute-done.19.ref.refs_20_ = bf16[128,1152]{1,0:T(8,128)(2,1)S(1)} collective-permute-done((bf16[128,1152]{1,0:T(8,128)(2,1)S(1)}, bf16[128,1152]{1,0:T(8,128)(2,1)S(1)}, u32[]{:S(2)}, u32[]{:S(2)}) %collective-permute-start.19) | collective-permute-done | bytes 294944 | tf_op jit(solution)/shard_map/ppermute | solution.py:158
  36.5 0.8 %collective-permute-start.9 = (bf16[128,1024]{1,0:T(8,128)(2,1)S(1)}, bf16[128,1024]{1,0:T(8,128)(2,1)S(1)}, u32[]{:S(2)}, u32[]{:S(2)}) collective-permute-start(bf16[128,1024]{1,0:T(8,128)(2,1)S(1)} %collective-permute-done.5.refs_4_), channel_id=1, source_target_pairs={{0,2},{2,0},{1,3},{3,1},{4,6},{6,4},{5,7},{7,5},{8,10},{10,8},{9,1... | collective-permute-start | bytes 786440 | tf_op jit(solution)/shard_map/ppermute | solution.py:158
  37.4 2.1 %collective-permute-start.22 = (bf16[128,640]{1,0:T(8,128)(2,1)S(1)}, bf16[128,640]{1,0:T(8,128)(2,1)S(1)}, u32[]{:S(2)}, u32[]{:S(2)}) collective-permute-start(bf16[128,640]{1,0:T(8,128)(2,1)S(1)} %get-tuple-element.58), channel_id=1, source_target_pairs={{0,4},{4,12},{12,8},{8,0},{1,5},{5,13},{13,9},{9,1},{2,6},{6,14},{... | collective-permute-start | bytes 491528 | tf_op jit(solution)/shard_map/ppermute | solution.py:158
  39.5 2.9 %collective-permute-done.10.refs_7_ = bf16[128,1024]{1,0:T(8,128)(2,1)S(1)} collective-permute-done((bf16[128,1024]{1,0:T(8,128)(2,1)S(1)}, bf16[128,1024]{1,0:T(8,128)(2,1)S(1)}, u32[]{:S(2)}, u32[]{:S(2)}) %collective-permute-start.10) | collective-permute-done | bytes 262176 | tf_op jit(solution)/shard_map/ppermute | solution.py:158
  42.4 1.4 %collective-permute-done.9.refs_6_ = bf16[128,1024]{1,0:T(8,128)(2,1)S(1)} collective-permute-done((bf16[128,1024]{1,0:T(8,128)(2,1)S(1)}, bf16[128,1024]{1,0:T(8,128)(2,1)S(1)}, u32[]{:S(2)}, u32[]{:S(2)}) %collective-permute-start.9) | collective-permute-done | bytes 262176 | tf_op jit(solution)/shard_map/ppermute | solution.py:158
  43.8 0.5 collective-permute-start.18
  44.3 0.1 collective-permute-start.21
  44.4 0.6 collective-permute-done.22.refs_22_
  45.0 2.4 %collective-permute-start.27 = (bf16[128,512]{1,0:T(8,128)(2,1)S(1)}, bf16[128,512]{1,0:T(8,128)(2,1)S(1)}, u32[]{:S(2)}, u32[]{:S(2)}) collective-permute-start(bf16[128,512]{1,0:T(8,128)(2,1)S(1)} %get-tuple-element.64), channel_id=1, source_target_pairs={{0,4},{4,12},{12,8},{8,0},{1,5},{5,13},{13,9},{9,1},{2,6},{6,14},{... | collective-permute-start | bytes 393224 | tf_op jit(solution)/shard_map/ppermute | solution.py:158
  47.4 2.0 %project.2 = (bf16[128,640]{1,0:T(8,128)(2,1)S(1)}, bf16[128,640]{1,0:T(8,128)(2,1)S(1)}, bf16[128,640]{1,0:T(8,128)(2,1)S(1)}, bf16[128,640]{1,0:T(8,128)(2,1)S(1)}) custom-call(bf16[128,1024]{1,0:T(8,128)(2,1)S(1)} %get-tuple-element.42.refs_0_, bf16[128,1024]{1,0:T(8,128)(2,1)S(1)} %get-tuple-element.43.refs_1_, ...), custom_call_target="tpu_custom_call" | custom-call | flops 3145728000 | tf_op jit(solution)/shard_map/project/pallas_call | solution.py:274
  49.5 1.8 %collective-permute-start.26 = (bf16[128,640]{1,0:T(8,128)(2,1)S(1)}, bf16[128,640]{1,0:T(8,128)(2,1)S(1)}, u32[]{:S(2)}, u32[]{:S(2)}) collective-permute-start(bf16[128,640]{1,0:T(8,128)(2,1)S(1)} %get-tuple-element.62), channel_id=1, source_target_pairs={{0,18},{2,16},{16,2},{18,0},{1,19},{3,17},{17,3},{19,1},{4,22},{6,... | collective-permute-start | bytes 491528 | tf_op jit(solution)/shard_map/ppermute | solution.py:157
  51.3 0.5 collective-permute-done.27.refs_22_
  51.8 1.1 %collective-permute-start.24 = (bf16[128,640]{1,0:T(8,128)(2,1)S(1)}, bf16[128,640]{1,0:T(8,128)(2,1)S(1)}, u32[]{:S(2)}, u32[]{:S(2)}) collective-permute-start(bf16[128,640]{1,0:T(8,128)(2,1)S(1)} %get-tuple-element.60), channel_id=1, source_target_pairs={{0,2},{2,0},{1,3},{3,1},{4,6},{6,4},{5,7},{7,5},{8,10},{10,8},{9,1... | collective-permute-start | bytes 491528 | tf_op jit(solution)/shard_map/ppermute | solution.py:158
  52.9 1.1 %collective-permute-start.25 = (bf16[128,640]{1,0:T(8,128)(2,1)S(1)}, bf16[128,640]{1,0:T(8,128)(2,1)S(1)}, u32[]{:S(2)}, u32[]{:S(2)}) collective-permute-start(bf16[128,640]{1,0:T(8,128)(2,1)S(1)} %get-tuple-element.61), channel_id=1, source_target_pairs={{0,16},{16,0},{1,17},{17,1},{2,18},{18,2},{3,19},{19,3},{4,20},{20... | collective-permute-start | bytes 491528 | tf_op jit(solution)/shard_map/ppermute | solution.py:158
  54.0 1.4 %project.3 = (bf16[128,512]{1,0:T(8,128)(2,1)S(1)}, bf16[128,512]{1,0:T(8,128)(2,1)S(1)}, bf16[128,512]{1,0:T(8,128)(2,1)S(1)}, bf16[128,512]{1,0:T(8,128)(2,1)S(1)}) custom-call(bf16[128,1024]{1,0:T(8,128)(2,1)S(1)} %get-tuple-element.42.refs_0_, bf16[128,1024]{1,0:T(8,128)(2,1)S(1)} %get-tuple-element.43.refs_1_, ...), custom_call_target="tpu_custom_call" | custom-call | flops 1 | tf_op jit(solution)/shard_map/project/pallas_call | solution.py:274
  55.4 0.5 collective-permute-start.29
  56.0 1.4 %collective-permute-start.30 = (bf16[128,512]{1,0:T(8,128)(2,1)S(1)}, bf16[128,512]{1,0:T(8,128)(2,1)S(1)}, u32[]{:S(2)}, u32[]{:S(2)}) collective-permute-start(bf16[128,512]{1,0:T(8,128)(2,1)S(1)} %get-tuple-element.67), channel_id=1, source_target_pairs={{0,16},{16,0},{1,17},{17,1},{2,18},{18,2},{3,19},{19,3},{4,20},{20... | collective-permute-start | bytes 393224 | tf_op jit(solution)/shard_map/ppermute | solution.py:158
  57.3 0.2 collective-permute-done.26.refs_3_
  57.5 1.7 %collective-permute-start.31 = (bf16[128,512]{1,0:T(8,128)(2,1)S(1)}, bf16[128,512]{1,0:T(8,128)(2,1)S(1)}, u32[]{:S(2)}, u32[]{:S(2)}) collective-permute-start(bf16[128,512]{1,0:T(8,128)(2,1)S(1)} %get-tuple-element.70), channel_id=1, source_target_pairs={{0,18},{2,16},{16,2},{18,0},{1,19},{3,17},{17,3},{19,1},{4,22},{6,... | collective-permute-start | bytes 393224 | tf_op jit(solution)/shard_map/ppermute | solution.py:157
  59.3 3.6 %collective-permute-done.29.refs_5_ = bf16[128,512]{1,0:T(8,128)(2,1)S(1)} collective-permute-done((bf16[128,512]{1,0:T(8,128)(2,1)S(1)}, bf16[128,512]{1,0:T(8,128)(2,1)S(1)}, u32[]{:S(2)}, u32[]{:S(2)}) %collective-permute-start.29) | collective-permute-done | bytes 131104 | tf_op jit(solution)/shard_map/ppermute | solution.py:158
  62.8 2.9 %collective-permute-done.30.refs_6_ = bf16[128,512]{1,0:T(8,128)(2,1)S(1)} collective-permute-done((bf16[128,512]{1,0:T(8,128)(2,1)S(1)}, bf16[128,512]{1,0:T(8,128)(2,1)S(1)}, u32[]{:S(2)}, u32[]{:S(2)}) %collective-permute-start.30) | collective-permute-done | bytes 131104 | tf_op jit(solution)/shard_map/ppermute | solution.py:158
  65.8 1.9 %finish.1 = bf16[128,4608]{1,0:T(8,128)(2,1)} custom-call(bf16[128,4608]{1,0:T(8,128)(2,1)S(1)} %bitcast.5, f32[1,4608]{1,0:T(1,128)S(1)} %reshape.3.gain_ref, bf16[128,640]{1,0:T(8,128)(2,1)S(1)} %get-tuple-element.59.refs_0_, bf16[128,640]{1,0:T(8,128)(2,1)S(1)} %collective-permute-done.24.refs_1_, bf16[128,640]{1,0:T(8,128)(2,1)S(1)} %collective-permute-done.25.refs_2_, ...), custom_call_target="tpu_custom_call" | custom-call | flops 1 | tf_op jit(solution)/shard_map/finish/pallas_call | solution.py:279
  (38 shorter events, 0.2 us)
Async XLA Ops:
  0.0 15.7 %collective-permute-start = (bf16[128,1024]{1,0:T(8,128)(2,1)}, bf16[128,1024]{1,0:T(8,128)(2,1)S(1)}, u32[]{:S(2)}, u32[]{:S(2)}) collective-permute-start(bf16[128,1024]{1,0:T(8,128)(2,1)} %bitcast.7), channel_id=1, source_target_pairs={{0,16},{16,0},{1,17},{17,1},{2,18},{18,2},{3,19},{19,3},{4,20},{20... | collective-permute-start | bytes 786440 | tf_op jit(solution)/shard_map/ppermute | solution.py:158
  3.0 6.3 %copy-start.5 = (s32[1,128]{1,0:T(1,128)S(1)}, s32[1,128]{1,0:T(1,128)}, u32[]{:S(2)}) copy-start(s32[1,128]{1,0:T(1,128)} %refs_3_.1) | copy-start | bytes 1540
  3.0 12.7 %collective-permute-start.1 = (bf16[128,1024]{1,0:T(8,128)(2,1)}, bf16[128,1024]{1,0:T(8,128)(2,1)S(1)}, u32[]{:S(2)}, u32[]{:S(2)}) collective-permute-start(bf16[128,1024]{1,0:T(8,128)(2,1)} %bitcast.9), channel_id=1, source_target_pairs={{0,16},{16,0},{1,17},{17,1},{2,18},{18,2},{3,19},{19,3},{4,20},{20... | collective-permute-start | bytes 786440 | tf_op jit(solution)/shard_map/ppermute | solution.py:158
  3.0 12.6 %collective-permute-start.2 = (s32[1,128]{1,0:T(1,128)}, s32[1,128]{1,0:T(1,128)S(1)}, u32[]{:S(2)}, u32[]{:S(2)}) collective-permute-start(s32[1,128]{1,0:T(1,128)} %refs_3_.1), channel_id=1, source_target_pairs={{0,16},{16,0},{1,17},{17,1},{2,18},{18,2},{3,19},{19,3},{4,20},{20... | collective-permute-start | bytes 1544 | tf_op jit(solution)/shard_map/ppermute | solution.py:158
  5.0 1.1 %copy-start.1 = (bf16[128,2304]{1,0:T(8,128)(2,1)S(1)}, bf16[128,2304]{1,0:T(8,128)(2,1)}, u32[]{:S(2)}) copy-start(bf16[128,2304]{1,0:T(8,128)(2,1)} %w_ref.1) | copy-start | bytes 1769476
  6.1 3.2 %copy-start.2 = (bf16[1,128,2048]{2,1,0:T(8,128)(2,1)S(1)}, bf16[1,128,2048]{2,1,0:T(8,128)(2,1)}, u32[]{:S(2)}) copy-start(bf16[1,128,2048]{2,1,0:T(8,128)(2,1)} %param.8) | copy-start | bytes 1572868
  6.1 3.2 %copy-start.3 = (bf16[1,128,1024]{2,1,0:T(8,128)(2,1)S(1)}, bf16[1,128,1024]{2,1,0:T(8,128)(2,1)}, u32[]{:S(2)}) copy-start(bf16[1,128,1024]{2,1,0:T(8,128)(2,1)} %param.9) | copy-start | bytes 786436
  6.1 3.2 %copy-start.4 = (bf16[1,128,1024]{2,1,0:T(8,128)(2,1)S(1)}, bf16[1,128,1024]{2,1,0:T(8,128)(2,1)}, u32[]{:S(2)}) copy-start(bf16[1,128,1024]{2,1,0:T(8,128)(2,1)} %param.10) | copy-start | bytes 786436
  6.1 8.0 %collective-permute-start.7 = (bf16[128,1152]{1,0:T(8,128)(2,1)S(1)}, bf16[128,1152]{1,0:T(8,128)(2,1)S(1)}, u32[]{:S(2)}, u32[]{:S(2)}) collective-permute-start(bf16[128,1152]{1,0:T(8,128)(2,1)S(1)} %get-tuple-element.45), channel_id=1, source_target_pairs={{0,2},{2,0},{1,3},{3,1},{4,6},{6,4},{5,7},{7,5},{8,10},{10,8},{9,1... | collective-permute-start | bytes 884744 | tf_op jit(solution)/shard_map/ppermute | solution.py:158
  7.7 11.9 %collective-permute-start.13 = (bf16[128,1152]{1,0:T(8,128)(2,1)S(1)}, bf16[128,1152]{1,0:T(8,128)(2,1)S(1)}, u32[]{:S(2)}, u32[]{:S(2)}) collective-permute-start(bf16[128,1152]{1,0:T(8,128)(2,1)S(1)} %get-tuple-element.52.refs_8_), channel_id=1, source_target_pairs={{0,4},{4,12},{12,8},{8,0},{1,5},{5,13},{13,9},{9,1},{2,6},{6,14},{... | collective-permute-start | bytes 884744 | tf_op jit(solution)/shard_map/ppermute | solution.py:158
  14.1 9.4 %collective-permute-start.8 = (bf16[128,1152]{1,0:T(8,128)(2,1)S(1)}, bf16[128,1152]{1,0:T(8,128)(2,1)S(1)}, u32[]{:S(2)}, u32[]{:S(2)}) collective-permute-start(bf16[128,1152]{1,0:T(8,128)(2,1)S(1)} %collective-permute-done.7.refs_16_), channel_id=1, source_target_pairs={{0,4},{4,12},{12,8},{8,0},{1,5},{5,13},{13,9},{9,1},{2,6},{6,14},{... | collective-permute-start | bytes 884744 | tf_op jit(solution)/shard_map/ppermute | solution.py:158
  16.8 8.9 %collective-permute-start.3 = (bf16[128,1024]{1,0:T(8,128)(2,1)S(1)}, bf16[128,1024]{1,0:T(8,128)(2,1)S(1)}, u32[]{:S(2)}, u32[]{:S(2)}) collective-permute-start(bf16[128,1024]{1,0:T(8,128)(2,1)S(1)} %get-tuple-element.42.refs_0_), channel_id=1, source_target_pairs={{0,2},{2,0},{1,3},{3,1},{4,6},{6,4},{5,7},{7,5},{8,10},{10,8},{9,1... | collective-permute-start | bytes 786440 | tf_op jit(solution)/shard_map/ppermute | solution.py:158
  18.4 8.9 %collective-permute-start.6 = (bf16[128,1024]{1,0:T(8,128)(2,1)S(1)}, bf16[128,1024]{1,0:T(8,128)(2,1)S(1)}, u32[]{:S(2)}, u32[]{:S(2)}) collective-permute-start(bf16[128,1024]{1,0:T(8,128)(2,1)S(1)} %get-tuple-element.43.refs_1_), channel_id=1, source_target_pairs={{0,16},{16,0},{1,17},{17,1},{2,18},{18,2},{3,19},{19,3},{4,20},{20... | collective-permute-start | bytes 786440 | tf_op jit(solution)/shard_map/ppermute | solution.py:158
  19.6 10.5 %collective-permute-start.15 = (bf16[128,1152]{1,0:T(8,128)(2,1)S(1)}, bf16[128,1152]{1,0:T(8,128)(2,1)S(1)}, u32[]{:S(2)}, u32[]{:S(2)}) collective-permute-start(bf16[128,1152]{1,0:T(8,128)(2,1)S(1)} %collective-permute-done.13.refs_10_), channel_id=1, source_target_pairs={{0,4},{4,12},{12,8},{8,0},{1,5},{5,13},{13,9},{9,1},{2,6},{6,14},{... | collective-permute-start | bytes 884744 | tf_op jit(solution)/shard_map/ppermute | solution.py:158
  21.5 7.9 %collective-permute-start.4 = (bf16[128,1024]{1,0:T(8,128)(2,1)S(1)}, bf16[128,1024]{1,0:T(8,128)(2,1)S(1)}, u32[]{:S(2)}, u32[]{:S(2)}) collective-permute-start(bf16[128,1024]{1,0:T(8,128)(2,1)S(1)} %get-tuple-element.43.refs_1_), channel_id=1, source_target_pairs={{0,2},{2,0},{1,3},{3,1},{4,6},{6,4},{5,7},{7,5},{8,10},{10,8},{9,1... | collective-permute-start | bytes 786440 | tf_op jit(solution)/shard_map/ppermute | solution.py:158
  23.5 10.1 %collective-permute-start.14 = (bf16[128,1152]{1,0:T(8,128)(2,1)S(1)}, bf16[128,1152]{1,0:T(8,128)(2,1)S(1)}, u32[]{:S(2)}, u32[]{:S(2)}) collective-permute-start(bf16[128,1152]{1,0:T(8,128)(2,1)S(1)} %collective-permute-done.13.refs_10_), channel_id=1, source_target_pairs={{0,1},{1,0},{2,3},{3,2},{4,5},{5,4},{6,7},{7,6},{8,9},{9,8},{10,11... | collective-permute-start | bytes 884744 | tf_op jit(solution)/shard_map/ppermute | solution.py:158
  25.7 10.8 %collective-permute-start.19 = (bf16[128,1152]{1,0:T(8,128)(2,1)S(1)}, bf16[128,1152]{1,0:T(8,128)(2,1)S(1)}, u32[]{:S(2)}, u32[]{:S(2)}) collective-permute-start(bf16[128,1152]{1,0:T(8,128)(2,1)S(1)} %collective-permute-done.8.refs_18_), channel_id=1, source_target_pairs={{0,4},{4,12},{12,8},{8,0},{1,5},{5,13},{13,9},{9,1},{2,6},{6,14},{... | collective-permute-start | bytes 884744 | tf_op jit(solution)/shard_map/ppermute | solution.py:158
  27.3 6.4 %collective-permute-start.5 = (bf16[128,1024]{1,0:T(8,128)(2,1)S(1)}, bf16[128,1024]{1,0:T(8,128)(2,1)S(1)}, u32[]{:S(2)}, u32[]{:S(2)}) collective-permute-start(bf16[128,1024]{1,0:T(8,128)(2,1)S(1)} %get-tuple-element.42.refs_0_), channel_id=1, source_target_pairs={{0,16},{16,0},{1,17},{17,1},{2,18},{18,2},{3,19},{19,3},{4,20},{20... | collective-permute-start | bytes 786440 | tf_op jit(solution)/shard_map/ppermute | solution.py:158
  29.4 7.9 %collective-permute-start.11 = (bf16[128,1152]{1,0:T(8,128)(2,1)S(1)}, bf16[128,1152]{1,0:T(8,128)(2,1)S(1)}, u32[]{:S(2)}, u32[]{:S(2)}) collective-permute-start(bf16[128,1152]{1,0:T(8,128)(2,1)S(1)} %collective-permute-done.7.refs_16_), channel_id=1, source_target_pairs={{0,1},{1,0},{2,3},{3,2},{4,5},{5,4},{6,7},{7,6},{8,9},{9,8},{10,11... | collective-permute-start | bytes 884744 | tf_op jit(solution)/shard_map/ppermute | solution.py:158
  30.1 13.7 %collective-permute-start.17 = (bf16[128,1152]{1,0:T(8,128)(2,1)S(1)}, bf16[128,1152]{1,0:T(8,128)(2,1)S(1)}, u32[]{:S(2)}, u32[]{:S(2)}) collective-permute-start(bf16[128,1152]{1,0:T(8,128)(2,1)S(1)} %collective-permute-done.15.refs_12_), channel_id=1, source_target_pairs={{0,4},{4,12},{12,8},{8,0},{1,5},{5,13},{13,9},{9,1},{2,6},{6,14},{... | collective-permute-start | bytes 884744 | tf_op jit(solution)/shard_map/ppermute | solution.py:158
  33.7 10.6 %collective-permute-start.16 = (bf16[128,1152]{1,0:T(8,128)(2,1)S(1)}, bf16[128,1152]{1,0:T(8,128)(2,1)S(1)}, u32[]{:S(2)}, u32[]{:S(2)}) collective-permute-start(bf16[128,1152]{1,0:T(8,128)(2,1)S(1)} %collective-permute-done.15.refs_12_), channel_id=1, source_target_pairs={{0,1},{1,0},{2,3},{3,2},{4,5},{5,4},{6,7},{7,6},{8,9},{9,8},{10,11... | collective-permute-start | bytes 884744 | tf_op jit(solution)/shard_map/ppermute | solution.py:158
  33.7 8.7 %collective-permute-start.10 = (bf16[128,1024]{1,0:T(8,128)(2,1)S(1)}, bf16[128,1024]{1,0:T(8,128)(2,1)S(1)}, u32[]{:S(2)}, u32[]{:S(2)}) collective-permute-start(bf16[128,1024]{1,0:T(8,128)(2,1)S(1)} %collective-permute-done.4.refs_3_), channel_id=1, source_target_pairs={{0,16},{16,0},{1,17},{17,1},{2,18},{18,2},{3,19},{19,3},{4,20},{20... | collective-permute-start | bytes 786440 | tf_op jit(solution)/shard_map/ppermute | solution.py:158
  36.5 7.2 %collective-permute-start.9 = (bf16[128,1024]{1,0:T(8,128)(2,1)S(1)}, bf16[128,1024]{1,0:T(8,128)(2,1)S(1)}, u32[]{:S(2)}, u32[]{:S(2)}) collective-permute-start(bf16[128,1024]{1,0:T(8,128)(2,1)S(1)} %collective-permute-done.5.refs_4_), channel_id=1, source_target_pairs={{0,2},{2,0},{1,3},{3,1},{4,6},{6,4},{5,7},{7,5},{8,10},{10,8},{9,1... | collective-permute-start | bytes 786440 | tf_op jit(solution)/shard_map/ppermute | solution.py:158
  37.4 7.6 %collective-permute-start.22 = (bf16[128,640]{1,0:T(8,128)(2,1)S(1)}, bf16[128,640]{1,0:T(8,128)(2,1)S(1)}, u32[]{:S(2)}, u32[]{:S(2)}) collective-permute-start(bf16[128,640]{1,0:T(8,128)(2,1)S(1)} %get-tuple-element.58), channel_id=1, source_target_pairs={{0,4},{4,12},{12,8},{8,0},{1,5},{5,13},{13,9},{9,1},{2,6},{6,14},{... | collective-permute-start | bytes 491528 | tf_op jit(solution)/shard_map/ppermute | solution.py:158
  42.4 2.6 %collective-permute-start.12 = (bf16[128,1152]{1,0:T(8,128)(2,1)S(1)}, bf16[128,1152]{1,0:T(8,128)(2,1)S(1)}, u32[]{:S(2)}, u32[]{:S(2)}) collective-permute-start(bf16[128,1152]{1,0:T(8,128)(2,1)S(1)} %get-tuple-element.52.refs_8_), channel_id=1, source_target_pairs={{0,1},{1,0},{2,3},{3,2},{4,5},{5,4},{6,7},{7,6},{8,9},{9,8},{10,11... | collective-permute-start | bytes 884744 | tf_op jit(solution)/shard_map/ppermute | solution.py:158
  43.8 3.6 %collective-permute-start.20 = (bf16[128,1152]{1,0:T(8,128)(2,1)S(1)}, bf16[128,1152]{1,0:T(8,128)(2,1)S(1)}, u32[]{:S(2)}, u32[]{:S(2)}) collective-permute-start(bf16[128,1152]{1,0:T(8,128)(2,1)S(1)} %collective-permute-done.8.refs_18_), channel_id=1, source_target_pairs={{0,1},{1,0},{2,3},{3,2},{4,5},{5,4},{6,7},{7,6},{8,9},{9,8},{10,11... | collective-permute-start | bytes 884744 | tf_op jit(solution)/shard_map/ppermute | solution.py:158
  43.8 3.6 %collective-permute-start.18 = (bf16[128,1152]{1,0:T(8,128)(2,1)S(1)}, bf16[128,1152]{1,0:T(8,128)(2,1)S(1)}, u32[]{:S(2)}, u32[]{:S(2)}) collective-permute-start(bf16[128,1152]{1,0:T(8,128)(2,1)S(1)} %collective-permute-done.17.refs_14_), channel_id=1, source_target_pairs={{0,1},{1,0},{2,3},{3,2},{4,5},{5,4},{6,7},{7,6},{8,9},{9,8},{10,11... | collective-permute-start | bytes 884744 | tf_op jit(solution)/shard_map/ppermute | solution.py:158
  44.3 3.1 %collective-permute-start.21 = (bf16[128,1152]{1,0:T(8,128)(2,1)S(1)}, bf16[128,1152]{1,0:T(8,128)(2,1)S(1)}, u32[]{:S(2)}, u32[]{:S(2)}) collective-permute-start(bf16[128,1152]{1,0:T(8,128)(2,1)S(1)} %collective-permute-done.19.ref.refs_20_), channel_id=1, source_target_pairs={{0,1},{1,0},{2,3},{3,2},{4,5},{5,4},{6,7},{7,6},{8,9},{9,8},{10,11... | collective-permute-start | bytes 884744 | tf_op jit(solution)/shard_map/ppermute | solution.py:158
  45.0 2.4 %collective-permute-start.23 = (bf16[128,640]{1,0:T(8,128)(2,1)S(1)}, bf16[128,640]{1,0:T(8,128)(2,1)S(1)}, u32[]{:S(2)}, u32[]{:S(2)}) collective-permute-start(bf16[128,640]{1,0:T(8,128)(2,1)S(1)} %collective-permute-done.22.refs_22_), channel_id=1, source_target_pairs={{0,1},{1,0},{2,3},{3,2},{4,5},{5,4},{6,7},{7,6},{8,9},{9,8},{10,11... | collective-permute-start | bytes 491528 | tf_op jit(solution)/shard_map/ppermute | solution.py:158
  45.0 6.8 %collective-permute-start.27 = (bf16[128,512]{1,0:T(8,128)(2,1)S(1)}, bf16[128,512]{1,0:T(8,128)(2,1)S(1)}, u32[]{:S(2)}, u32[]{:S(2)}) collective-permute-start(bf16[128,512]{1,0:T(8,128)(2,1)S(1)} %get-tuple-element.64), channel_id=1, source_target_pairs={{0,4},{4,12},{12,8},{8,0},{1,5},{5,13},{13,9},{9,1},{2,6},{6,14},{... | collective-permute-start | bytes 393224 | tf_op jit(solution)/shard_map/ppermute | solution.py:158
  49.5 8.1 %collective-permute-start.26 = (bf16[128,640]{1,0:T(8,128)(2,1)S(1)}, bf16[128,640]{1,0:T(8,128)(2,1)S(1)}, u32[]{:S(2)}, u32[]{:S(2)}) collective-permute-start(bf16[128,640]{1,0:T(8,128)(2,1)S(1)} %get-tuple-element.62), channel_id=1, source_target_pairs={{0,18},{2,16},{16,2},{18,0},{1,19},{3,17},{17,3},{19,1},{4,22},{6,... | collective-permute-start | bytes 491528 | tf_op jit(solution)/shard_map/ppermute | solution.py:157
  51.8 2.2 %collective-permute-start.28 = (bf16[128,512]{1,0:T(8,128)(2,1)S(1)}, bf16[128,512]{1,0:T(8,128)(2,1)S(1)}, u32[]{:S(2)}, u32[]{:S(2)}) collective-permute-start(bf16[128,512]{1,0:T(8,128)(2,1)S(1)} %collective-permute-done.27.refs_22_), channel_id=1, source_target_pairs={{0,1},{1,0},{2,3},{3,2},{4,5},{5,4},{6,7},{7,6},{8,9},{9,8},{10,11... | collective-permute-start | bytes 393224 | tf_op jit(solution)/shard_map/ppermute | solution.py:158
  51.8 14.0 %collective-permute-start.24 = (bf16[128,640]{1,0:T(8,128)(2,1)S(1)}, bf16[128,640]{1,0:T(8,128)(2,1)S(1)}, u32[]{:S(2)}, u32[]{:S(2)}) collective-permute-start(bf16[128,640]{1,0:T(8,128)(2,1)S(1)} %get-tuple-element.60), channel_id=1, source_target_pairs={{0,2},{2,0},{1,3},{3,1},{4,6},{6,4},{5,7},{7,5},{8,10},{10,8},{9,1... | collective-permute-start | bytes 491528 | tf_op jit(solution)/shard_map/ppermute | solution.py:158
  52.9 6.3 %copy-start.6 = (f32[4608]{0:T(1024)S(1)}, f32[4608]{0:T(1024)}, u32[]{:S(2)}) copy-start(f32[4608]{0:T(1024)} %param.12) | copy-start | bytes 55300
  52.9 12.8 %copy-start = (bf16[1,128,4608]{2,1,0:T(8,128)(2,1)S(1)}, bf16[1,128,4608]{2,1,0:T(8,128)(2,1)}, u32[]{:S(2)}) copy-start(bf16[1,128,4608]{2,1,0:T(8,128)(2,1)} %param.7) | copy-start | bytes 3538948
  52.9 12.8 %collective-permute-start.25 = (bf16[128,640]{1,0:T(8,128)(2,1)S(1)}, bf16[128,640]{1,0:T(8,128)(2,1)S(1)}, u32[]{:S(2)}, u32[]{:S(2)}) collective-permute-start(bf16[128,640]{1,0:T(8,128)(2,1)S(1)} %get-tuple-element.61), channel_id=1, source_target_pairs={{0,16},{16,0},{1,17},{17,1},{2,18},{18,2},{3,19},{19,3},{4,20},{20... | collective-permute-start | bytes 491528 | tf_op jit(solution)/shard_map/ppermute | solution.py:158
  55.4 7.4 %collective-permute-start.29 = (bf16[128,512]{1,0:T(8,128)(2,1)S(1)}, bf16[128,512]{1,0:T(8,128)(2,1)S(1)}, u32[]{:S(2)}, u32[]{:S(2)}) collective-permute-start(bf16[128,512]{1,0:T(8,128)(2,1)S(1)} %get-tuple-element.66), channel_id=1, source_target_pairs={{0,2},{2,0},{1,3},{3,1},{4,6},{6,4},{5,7},{7,5},{8,10},{10,8},{9,1... | collective-permute-start | bytes 393224 | tf_op jit(solution)/shard_map/ppermute | solution.py:158
  56.0 9.8 %collective-permute-start.30 = (bf16[128,512]{1,0:T(8,128)(2,1)S(1)}, bf16[128,512]{1,0:T(8,128)(2,1)S(1)}, u32[]{:S(2)}, u32[]{:S(2)}) collective-permute-start(bf16[128,512]{1,0:T(8,128)(2,1)S(1)} %get-tuple-element.67), channel_id=1, source_target_pairs={{0,16},{16,0},{1,17},{17,1},{2,18},{18,2},{3,19},{19,3},{4,20},{20... | collective-permute-start | bytes 393224 | tf_op jit(solution)/shard_map/ppermute | solution.py:158
  57.5 8.3 %collective-permute-start.31 = (bf16[128,512]{1,0:T(8,128)(2,1)S(1)}, bf16[128,512]{1,0:T(8,128)(2,1)S(1)}, u32[]{:S(2)}, u32[]{:S(2)}) collective-permute-start(bf16[128,512]{1,0:T(8,128)(2,1)S(1)} %get-tuple-element.70), channel_id=1, source_target_pairs={{0,18},{2,16},{16,2},{18,0},{1,19},{3,17},{17,3},{19,1},{4,22},{6,... | collective-permute-start | bytes 393224 | tf_op jit(solution)/shard_map/ppermute | solution.py:157

commit v3 on v2

--- a/solution.py
+++ b/solution.py
@@ -18,13 +18,14 @@
 norm_eps = 1e-06
 
 CHUNKS = (640, 512)
-TIES = {'rd2': ('rd1',), 'd1': ('B1',), 'cB0': ('y2',), 'cB1': ('B2',), 'ca0': ('cB0',)}
-COSTS = {'att': 3000, 'cut': 1500, 'stage': 9000, 'finish': 1500, 'proj1': 6000}
+PACKS = (('a0', 'B0', 'a1', 'B1'), ('a2', 'B2'))
+WHOLE_STEPS = {'a': 3, 'B': 2}
+TIES = {'rx1': ('rd0',), 'B3_0': ('ck0',), 'a2': ('h1',), 'ry1': ('rd0',), 'd1': ('k1',)}
+COSTS = {'splitB': 9000, 'hy': 1500, 'proj0': 9000, 'pk0': 1500, 'cut': 9000, 'early': 9000, 'att': 3000, 'stage': 1500, 'pk1': 9000, 'hx': 6000}
 PER_CYCLE = 524288
 FIRST = ()
-ACTS = 2
-WHOLE = 2
-VMEM_LIMIT = 14 * 2**20
+ACTS = 1
+VMEM_LIMIT = 20 * 2**20
 VMEM = pl.BlockSpec(memory_space=pltpu.VMEM)
 HBM = pl.BlockSpec(memory_space=pl.ANY)
 
@@ -100,12 +101,18 @@
     return (source * 2 + x) * 2 + core
 
 
-def project(ring, first, sizes, *refs):
-    n = len(ring)
-    count = sum(sizes)
-    acts, bufs, outs = refs[:count], refs[count : count + 4 * n], refs[count + 4 * n : -2]
-    a_all, w_all = refs[-2:]
-    tokens, columns = outs[0].shape
+def part(which, ref, out):
+    out[...] = ref[:, pl.ds(which * out.shape[1], out.shape[1])]
+
+
+def stack(*refs):
+    bufs, out = refs[:-1], refs[-1]
+    for i, buf in enumerate(bufs):
+        out[pl.ds(i * buf.shape[0], buf.shape[0]), :] = buf[...]
+
+
+def stack_acts(sizes, acts, a_all):
+    tokens = a_all.shape[0] // len(sizes)
     taken = 0
     for g, parts in enumerate(sizes):
         at = 0
@@ -113,21 +120,51 @@
             a_all[pl.ds(g * tokens, tokens), pl.ds(at, act.shape[1])] = act[...]
             at += act.shape[1]
         taken += parts
-    for i, buf in enumerate(bufs):
-        same_x, step, same_core = i < 2 * n, i // 2 % n, i % 2 == 0
-        head = head_of(step, same_x, same_core, ring)
-        at = 0 if buf.shape[1] == columns else first
-        w_all[pl.ds(pl.multiple_of(head * DH, DH), DH), :] = buf[:, pl.ds(at, columns)]
-    for g in range(0, len(outs), 2):
-        rows = jnp.dot(
-            a_all[pl.ds(g * tokens, 2 * tokens), :], w_all[...], preferred_element_type=jnp.float32
-        ).astype(jnp.bfloat16)
-        outs[g][...] = rows[:tokens]
-        outs[g + 1][...] = rows[tokens:]
+
+
+def columns_of(a_all, heads):
+    return jnp.concatenate(
+        [a_all[:, pl.ds(pl.multiple_of(head * DH, DH), DH)] for head in heads], axis=1
+    )
+
+
+def early(ring, sizes, heads, *refs):
+    count = sum(sizes)
+    acts, bufs, (acc, a_all, w_all) = refs[:count], refs[count:-3], refs[-3:]
+    stack_acts(sizes, acts, a_all)
+    at = 0
+    for buf in bufs:
+        w_all[pl.ds(at, buf.shape[0]), :] = buf[...]
+        at += buf.shape[0]
+    heads = [head_of(*head, ring) for head in heads]
+    acc[...] = jnp.dot(columns_of(a_all, heads), w_all[...], preferred_element_type=jnp.float32)
+
+
+def project(ring, first, sizes, heads, acc, a_all, w_all, *refs):
+    count = sum(sizes)
+    acts, bufs, outs, a_last = refs[:count], refs[count:-5], refs[-5:-1], refs[-1]
+    tokens, columns = outs[0].shape
+    done = w_all.shape[0] // DH
+    stack_acts(sizes, acts, a_last)
+    heads = [head_of(*head, ring) for head in heads]
+    w_late = jnp.concatenate(
+        [buf[:, pl.ds(0 if buf.shape[1] == columns else first, columns)] for buf in bufs], axis=0
+    )
+    rows = acc[:, pl.ds(first, columns)] + jnp.dot(
+        columns_of(a_all, heads[done:]), w_late, preferred_element_type=jnp.float32
+    )
+    for g in range(3):
+        outs[g][...] = rows[g * tokens : (g + 1) * tokens].astype(jnp.bfloat16)
+    rows = jnp.dot(
+        columns_of(a_last, heads[:done]),
+        w_all[:, pl.ds(first, columns)],
+        preferred_element_type=jnp.float32,
+    ) + jnp.dot(columns_of(a_last, heads[done:]), w_late, preferred_element_type=jnp.float32)
+    outs[3][...] = rows.astype(jnp.bfloat16)
 
 
 def finish(chunks, hidden_ref, gain_ref, *refs):
-    pieces, out_ref = refs[:-1], refs[-1]
+    pieces, out_hbm, out_ref, sems = refs[:-3], refs[-3], refs[-2], refs[-1]
     width = hidden_ref.shape[1]
     x, y = lax.axis_index("x"), lax.axis_index("ctx")
     owners = ((x, y), (1 - x, y), (x, 1 - y), (1 - x, 1 - y))
@@ -137,12 +174,19 @@
         total = total + jnp.sum(value * value, axis=-1, keepdims=True)
     scale = lax.rsqrt(total / width + norm_eps)
     start = 0
+    copies = []
     for c, columns in enumerate(chunks):
         for i, (px, py) in enumerate(owners):
             at = pl.ds(pl.multiple_of((py * 2 + px) * (width // 4) + start, 128), columns)
             normed = pieces[c * 4 + i][...].astype(jnp.float32) * scale * gain_ref[:, at]
             out_ref[:, at] = (hidden_ref[:, at].astype(jnp.float32) + normed).astype(jnp.bfloat16)
+            copies.append(
+                pltpu.make_async_copy(out_ref.at[:, at], out_hbm.at[:, at], sems.at[c * 4 + i])
+            )
+            copies[-1].start()
         start += columns
+    for copy in copies:
+        copy.wait()
 
 
 def shards(ring, chunks, hidden_rows, query_proj, key_proj, value_proj, order_pos, post_gain, out_weight):
@@ -174,20 +218,6 @@
             name=name,
         )
 
-    def project_chunk(c, sizes, count):
-        columns = chunks[c]
-        return call(
-            functools.partial(project, ring, sum(chunks[:c]), sizes),
-            [bf16(tokens, columns)] * 4,
-            count,
-            "project",
-            [
-                pltpu.VMEM((4 * tokens, HQ * DH), jnp.bfloat16),
-                pltpu.VMEM((HQ * DH, columns), jnp.bfloat16),
-            ],
-            label="proj" + str(c + 1),
-        )
-
     moves, kernels = {}, {}
     kernels["cut"] = (call(cut, [bf16(rows, quarter)] * 2, 1, "cut"), ("w",), ("a0", "awayo"))
     kernels["stage"] = (
@@ -219,32 +249,76 @@
         sizes = (2, 2, 2, 2)
     else:
         half = bf16(tokens, HQ * DH // 2)
-        kernels["hy"] = (call(split, [half] * 2, 1, "halves", label="hy"), ("y1",), ("y1l", "y1r"))
-        kernels["hx"] = (call(split, [half] * 2, 1, "halves", label="hx"), ("x1",), ("x1l", "x1r"))
+        kernels["hy"] = (call(functools.partial(part, 0), [half], 1, "halves", label="hy"), ("y1",), ("y1l",))
+        kernels["hx"] = (call(functools.partial(part, 1), [half], 1, "halves", label="hx"), ("x1",), ("x1r",))
         moves["d1"], moves["d2"] = ("y1l", "x"), ("x1r", "ctx")
         acts, sizes = ("h1", "x1", "y1", "d1", "d2"), (1, 1, 1, 2)
-    for i in range(1, n):
-        moves["a%d" % i] = ("a%d" % (i - 1), "z")
-    for i in range(1, WHOLE + 1):
-        moves["B%d" % i] = ("B%d" % (i - 1), "z")
-    last = "B%d" % WHOLE
-    kernels["split"] = (
-        call(split, [bf16(rows, c) for c in chunks], 1, "split"),
-        (last,),
-        tuple("b%d%d" % (c + 1, WHOLE) for c in range(len(chunks))),
-    )
-    for c in range(len(chunks)):
-        j = str(c + 1)
-        for i in range(WHOLE + 1, n):
-            moves["b%s%d" % (j, i)] = ("b%s%d" % (j, i - 1), "z")
-        away = ["B%d" % i for i in range(WHOLE + 1)] + ["b%s%d" % (j, i) for i in range(WHOLE + 1, n)]
+    for chain, whole in WHOLE_STEPS.items():
+        for i in range(1, whole + 1):
+            moves[chain + str(i)] = (chain + str(i - 1), "z")
+        if whole < n - 1:
+            last = chain + str(whole)
+            kernels["split" + chain] = (
+                call(split, [bf16(rows, c) for c in chunks], 1, "split", label="split" + chain),
+                (last,),
+                tuple("%s_%d" % (last, c) for c in range(len(chunks))),
+            )
+    def spot(name):
+        return name[0], int(name[1:])
+
+    sure = [spot(name) for names in PACKS for name in names]
+    late = [(chain, i) for chain in WHOLE_STEPS for i in range(n) if (chain, i) not in sure]
+    order, bufs = [], []
+    for k, names in enumerate(PACKS):
+        kernels["pk%d" % k] = (
+            call(stack, [bf16(len(names) * rows, quarter)], len(names), "stack", label="pk%d" % k),
+            tuple(names),
+            ("k%d" % k,),
+        )
+        moves["ck%d" % k] = ("k%d" % k, "core")
+        bufs += ["k%d" % k, "ck%d" % k]
+        for same in (True, False):
+            order += [(spot(name)[1], name[0] == "a", same) for name in names]
+    done = len(order)
+    order += [(i, chain == "a", same) for chain, i in late for same in (True, False)]
+    three = (*acts[: 3 * ACTS],)
+    kernels["early"] = (
+        call(
+            functools.partial(early, ring, (ACTS,) * 3, order[:done]),
+            [
+                jax.ShapeDtypeStruct((3 * tokens, quarter), jnp.float32),
+                bf16(3 * tokens, HQ * DH),
+                bf16(done * DH, quarter),
+            ],
+            len(three) + len(bufs),
+            "early",
+        ),
+        (*three, *bufs),
+        ("acc", "aall", "wall"),
+    )
+    for c, columns in enumerate(chunks):
+        j = str(c)
         bufs = []
-        for name in ["a%d" % i for i in range(n)] + away:
+        for chain, i in late:
+            name = "%s%d" % (chain, i) if i <= WHOLE_STEPS[chain] else "%s%d_%d" % (chain, i, c)
+            if i > WHOLE_STEPS[chain]:
+                moves[name] = ("%s%d_%d" % (chain, i - 1, c), "z")
             moves["c" + name] = (name, "core")
             bufs += [name, "c" + name]
-        operands = (*acts, *bufs)
+        operands = ("acc", "aall", "wall", *acts[3 * ACTS :], *bufs)
         results = tuple("p" + k + j for k in "oxyd")
-        kernels["proj" + j] = (project_chunk(c, sizes, len(operands)), operands, results)
+        kernels["proj" + j] = (
+            call(
+                functools.partial(project, ring, sum(chunks[:c]), (2,), order),
+                [bf16(tokens, columns)] * 4,
+                len(operands),
+                "project",
+                [pltpu.VMEM((tokens, HQ * DH), jnp.bfloat16)],
+                label="proj" + j,
+            ),
+            operands,
+            results,
+        )
         for k, axis in zip("xyd", ("x", "ctx", "diag")):
             moves["r" + k + j] = ("p" + k + j, axis)
 
@@ -274,13 +348,17 @@
             out = kernels[name][0](first, *(held[k] for k in sources[1:]))
             held.update(zip(results, out))
 
-    pieces = [held[("po" if k == "o" else "r" + k) + str(c + 1)] for c in range(len(chunks)) for k in "oxyd"]
+    pieces = [held[("po" if k == "o" else "r" + k) + str(c)] for c in range(len(chunks)) for k in "oxyd"]
 
     out = pl.pallas_call(
         functools.partial(finish, chunks),
         out_shape=bf16(tokens, width),
         in_specs=[VMEM] * (2 + len(pieces)),
-        out_specs=VMEM,
+        out_specs=HBM,
+        scratch_shapes=[
+            pltpu.VMEM((tokens, width), jnp.bfloat16),
+            pltpu.SemaphoreType.DMA((len(pieces),)),
+        ],
         compiler_params=params(),
         cost_estimate=pl.CostEstimate(flops=1, bytes_accessed=0, transcendentals=0),
         name="finish",

time: 67.8 us -> 65.7 us (0.969)
  starting transfers between devices: 34.2 us -> 29.7 us
  waiting for transfers between devices: 25.7 us -> 27.9 us
    ppermute x2, waiting for transfers between devices: 0.19 us -> 6.89 us  [over(): return lax.ppermute(value, ('ctx', 'x'), [(i, 3 - i) for i in range(4)])]
    ppermute x30 -> x24, waiting for transfers between devices: 25.5 us -> 21 us  [over(): return lax.ppermute(value, axis, along if axis == 'z' else swap)]
    ppermute x30 -> x24, starting transfers between devices: 30.6 us -> 26.9 us  [over(): return lax.ppermute(value, axis, along if axis == 'z' else swap)]
    ppermute x2, starting transfers between devices: 3.55 us -> 2.82 us  [over(): return lax.ppermute(value, ('ctx', 'x'), [(i, 3 - i) for i in range(4)])]
    pallas_call x6 -> x11, Pallas kernels: 4.69 us -> 4.9 us  [shards(): out = kernels[name][0](first, *(held[k] for k in sources[1:]))]
  transfers between devices with their start and end apart: 32 -> 26, of which waited for: 14 -> 12; matrix products, arithmetic and copies ran while one was open for 0% -> 0% of each run, Pallas kernels for 7% -> 7%
where the time goes in v3:
time: 65.7 us; the launch traced here: 65.6 us
  starting transfers between devices  29.7 us (45%)
  waiting for transfers between devices  27.9 us (42%)
  Pallas kernels  6.73 us (10%)
  local copies, waits for them, and re-layouts  1.1 us (2%)
    ppermute x24, starting transfers between devices, over(): return lax.ppermute(value, axis, along if axis == 'z' else swap)  26.9 us
    ppermute x24, waiting for transfers between devices, over(): return lax.ppermute(value, axis, along if axis == 'z' else swap)  21 us
    ppermute x2, waiting for transfers between devices, over(): return lax.ppermute(value, ('ctx', 'x'), [(i, 3 - i) for i in range(4)])  6.89 us
    pallas_call x11, Pallas kernels, shards(): out = kernels[name][0](first, *(held[k] for k in sources[1:]))  4.9 us
    ppermute x2, starting transfers between devices, over(): return lax.ppermute(value, ('ctx', 'x'), [(i, 3 - i) for i in range(4)])  2.82 us
    pallas_call x1, Pallas kernels, shards(): pl.pallas_call(functools.partial(finish, chunks), out_shape=bf16(tokens,...  1.83 us
  transfers between devices with their start and end apart: 26, of which 12 were waited for; matrix products, arithmetic and copies ran while one was open for 0% of the time, Pallas kernels for 7%

profile of v3, /device:TPU:0, one launch (start us, length us, event | category | flops | bytes accessed | tf_op | source)
XLA Modules:
  0.0 65.6 jit_solution(11513455116389258425)
XLA Ops:
  0.0 1.1 %copy-done.1 = bf16[128,2304]{1,0:T(8,128)(2,1)S(1)} copy-done((bf16[128,2304]{1,0:T(8,128)(2,1)S(1)}, bf16[128,2304]{1,0:T(8,128)(2,1)}, u32[]{:S(2)}) %copy-start.1) | copy-done | bytes 589848
  1.1 0.1 cut.1
  1.1 3.0 %collective-permute-start.5 = (bf16[128,1152]{1,0:T(8,128)(2,1)S(1)}, bf16[128,1152]{1,0:T(8,128)(2,1)S(1)}, u32[]{:S(2)}, u32[]{:S(2)}) collective-permute-start(bf16[128,1152]{1,0:T(8,128)(2,1)S(1)} %get-tuple-element.44), channel_id=1, source_target_pairs={{0,2},{2,0},{1,3},{3,1},{4,6},{6,4},{5,7},{7,5},{8,10},{10,8},{9,1... | collective-permute-start | bytes 884744 | tf_op jit(solution)/shard_map/ppermute | solution.py:202
  4.1 1.5 %collective-permute-start = (bf16[128,1024]{1,0:T(8,128)(2,1)S(1)}, bf16[128,1024]{1,0:T(8,128)(2,1)S(1)}, u32[]{:S(2)}, u32[]{:S(2)}) collective-permute-start(bf16[128,1024]{1,0:T(8,128)(2,1)S(1)} %bitcast.7), channel_id=1, source_target_pairs={{0,16},{16,0},{1,17},{17,1},{2,18},{18,2},{3,19},{19,3},{4,20},{20... | collective-permute-start | bytes 786440 | tf_op jit(solution)/shard_map/ppermute | solution.py:202
  5.7 0.5 collective-permute-start.1
  6.2 1.6 %collective-permute-start.6 = (bf16[128,1152]{1,0:T(8,128)(2,1)S(1)}, bf16[128,1152]{1,0:T(8,128)(2,1)S(1)}, u32[]{:S(2)}, u32[]{:S(2)}) collective-permute-start(bf16[128,1152]{1,0:T(8,128)(2,1)S(1)} %get-tuple-element.43.refs_0_), channel_id=1, source_target_pairs={{0,4},{4,12},{12,8},{8,0},{1,5},{5,13},{13,9},{9,1},{2,6},{6,14},{... | collective-permute-start | bytes 884744 | tf_op jit(solution)/shard_map/ppermute | solution.py:202
  7.8 3.4 %collective-permute-done.5.refs_1_ = bf16[128,1152]{1,0:T(8,128)(2,1)S(1)} collective-permute-done((bf16[128,1152]{1,0:T(8,128)(2,1)S(1)}, bf16[128,1152]{1,0:T(8,128)(2,1)S(1)}, u32[]{:S(2)}, u32[]{:S(2)}) %collective-permute-start.5) | collective-permute-done | bytes 294944 | tf_op jit(solution)/shard_map/ppermute | solution.py:202
  11.2 1.8 %collective-permute-start.7 = (bf16[128,1152]{1,0:T(8,128)(2,1)S(1)}, bf16[128,1152]{1,0:T(8,128)(2,1)S(1)}, u32[]{:S(2)}, u32[]{:S(2)}) collective-permute-start(bf16[128,1152]{1,0:T(8,128)(2,1)S(1)} %collective-permute-done.5.refs_1_), channel_id=1, source_target_pairs={{0,4},{4,12},{12,8},{8,0},{1,5},{5,13},{13,9},{9,1},{2,6},{6,14},{... | collective-permute-start | bytes 884744 | tf_op jit(solution)/shard_map/ppermute | solution.py:202
  13.0 1.5 %collective-permute-start.2 = (s32[1,128]{1,0:T(1,128)S(1)}, s32[1,128]{1,0:T(1,128)S(1)}, u32[]{:S(2)}, u32[]{:S(2)}) collective-permute-start(s32[1,128]{1,0:T(1,128)S(1)} %copy-done.5), channel_id=1, source_target_pairs={{0,16},{16,0},{1,17},{17,1},{2,18},{18,2},{3,19},{19,3},{4,20},{20... | collective-permute-start | bytes 1544 | tf_op jit(solution)/shard_map/ppermute | solution.py:202
  14.5 0.1 stage.1
  14.6 3.0 %collective-permute-done.2.pos_far = s32[1,128]{1,0:T(1,128)S(1)} collective-permute-done((s32[1,128]{1,0:T(1,128)S(1)}, s32[1,128]{1,0:T(1,128)S(1)}, u32[]{:S(2)}, u32[]{:S(2)}) %collective-permute-start.2) | collective-permute-done | bytes 544 | tf_op jit(solution)/shard_map/ppermute | solution.py:202
  17.6 1.1 %attend.1.refs_0_ = bf16[128,2048]{1,0:T(8,128)(2,1)S(1)} custom-call(bf16[128,2048]{1,0:T(8,128)(2,1)S(1)} %get-tuple-element.38.q_ref, bf16[128,1024]{1,0:T(8,128)(2,1)S(1)} %get-tuple-element.39.k_own, bf16[128,1024]{1,0:T(8,128)(2,1)S(1)} %collective-permute-done.k_far, bf16[128,1024]{1,0:T(8,128)(2,1)S(1)} %get-tuple-element.40.v_own, ...), custom_call_target="tpu_custom_call" | custom-call | flops 1572864000 | tf_op jit(solution)/shard_map/attend/pallas_call | solution.py:348
  18.7 1.6 %collective-permute-start.9 = (bf16[128,1152]{1,0:T(8,128)(2,1)S(1)}, bf16[128,1152]{1,0:T(8,128)(2,1)S(1)}, u32[]{:S(2)}, u32[]{:S(2)}) collective-permute-start(bf16[128,1152]{1,0:T(8,128)(2,1)S(1)} %collective-permute-done.6.refs_2_), channel_id=1, source_target_pairs={{0,4},{4,12},{12,8},{8,0},{1,5},{5,13},{13,9},{9,1},{2,6},{6,14},{... | collective-permute-start | bytes 884744 | tf_op jit(solution)/shard_map/ppermute | solution.py:202
  20.4 1.3 %collective-permute-done.7.refs_3_ = bf16[128,1152]{1,0:T(8,128)(2,1)S(1)} collective-permute-done((bf16[128,1152]{1,0:T(8,128)(2,1)S(1)}, bf16[128,1152]{1,0:T(8,128)(2,1)S(1)}, u32[]{:S(2)}, u32[]{:S(2)}) %collective-permute-start.7) | collective-permute-done | bytes 294944 | tf_op jit(solution)/shard_map/ppermute | solution.py:202
  21.7 1.3 %collective-permute-start.10 = (bf16[128,1152]{1,0:T(8,128)(2,1)S(1)}, bf16[128,1152]{1,0:T(8,128)(2,1)S(1)}, u32[]{:S(2)}, u32[]{:S(2)}) collective-permute-start(bf16[128,1152]{1,0:T(8,128)(2,1)S(1)} %collective-permute-done.7.refs_3_), channel_id=1, source_target_pairs={{0,4},{4,12},{12,8},{8,0},{1,5},{5,13},{13,9},{9,1},{2,6},{6,14},{... | collective-permute-start | bytes 884744 | tf_op jit(solution)/shard_map/ppermute | solution.py:202
  23.0 0.1 stack.2.refs_3_
  23.0 0.1 collective-permute-start.8
  23.1 1.2 %collective-permute-start.3 = (bf16[128,2048]{1,0:T(8,128)(2,1)S(1)}, bf16[128,2048]{1,0:T(8,128)(2,1)S(1)}, u32[]{:S(2)}, u32[]{:S(2)}) collective-permute-start(bf16[128,2048]{1,0:T(8,128)(2,1)S(1)} %attend.1.refs_0_), channel_id=1, source_target_pairs={{0,2},{2,0},{1,3},{3,1},{4,6},{6,4},{5,7},{7,5},{8,10},{10,8},{9,1... | collective-permute-start | bytes 1572872 | tf_op jit(solution)/shard_map/ppermute | solution.py:202
  24.3 1.5 %collective-permute-start.4 = (bf16[128,2048]{1,0:T(8,128)(2,1)S(1)}, bf16[128,2048]{1,0:T(8,128)(2,1)S(1)}, u32[]{:S(2)}, u32[]{:S(2)}) collective-permute-start(bf16[128,2048]{1,0:T(8,128)(2,1)S(1)} %attend.1.refs_0_), channel_id=1, source_target_pairs={{0,16},{16,0},{1,17},{17,1},{2,18},{18,2},{3,19},{19,3},{4,20},{20... | collective-permute-start | bytes 1572872 | tf_op jit(solution)/shard_map/ppermute | solution.py:202
  25.8 3.8 %collective-permute-done.9.refs_0_ = bf16[128,1152]{1,0:T(8,128)(2,1)S(1)} collective-permute-done((bf16[128,1152]{1,0:T(8,128)(2,1)S(1)}, bf16[128,1152]{1,0:T(8,128)(2,1)S(1)}, u32[]{:S(2)}, u32[]{:S(2)}) %collective-permute-start.9) | collective-permute-done | bytes 294944 | tf_op jit(solution)/shard_map/ppermute | solution.py:202
  29.6 0.8 %collective-permute-start.14 = (bf16[128,1152]{1,0:T(8,128)(2,1)S(1)}, bf16[128,1152]{1,0:T(8,128)(2,1)S(1)}, u32[]{:S(2)}, u32[]{:S(2)}) collective-permute-start(bf16[128,1152]{1,0:T(8,128)(2,1)S(1)} %collective-permute-done.9.refs_0_), channel_id=1, source_target_pairs={{0,4},{4,12},{12,8},{8,0},{1,5},{5,13},{13,9},{9,1},{2,6},{6,14},{... | collective-permute-start | bytes 884744 | tf_op jit(solution)/shard_map/ppermute | solution.py:202
  30.4 5.5 %collective-permute-done.10.refs_1_.ref = bf16[128,1152]{1,0:T(8,128)(2,1)S(1)} collective-permute-done((bf16[128,1152]{1,0:T(8,128)(2,1)S(1)}, bf16[128,1152]{1,0:T(8,128)(2,1)S(1)}, u32[]{:S(2)}, u32[]{:S(2)}) %collective-permute-start.10) | collective-permute-done | bytes 294944 | tf_op jit(solution)/shard_map/ppermute | solution.py:202
  36.0 0.1 collective-permute-start.11
  36.1 0.8 %collective-permute-start.16 = (bf16[128,640]{1,0:T(8,128)(2,1)S(1)}, bf16[128,640]{1,0:T(8,128)(2,1)S(1)}, u32[]{:S(2)}, u32[]{:S(2)}) collective-permute-start(bf16[128,640]{1,0:T(8,128)(2,1)S(1)} %get-tuple-element.55), channel_id=1, source_target_pairs={{0,4},{4,12},{12,8},{8,0},{1,5},{5,13},{13,9},{9,1},{2,6},{6,14},{... | collective-permute-start | bytes 491528 | tf_op jit(solution)/shard_map/ppermute | solution.py:202
  37.0 0.5 collective-permute-done.3.refs_1_.ref
  37.5 1.6 %collective-permute-start.13 = (bf16[128,1024]{1,0:T(8,128)(2,1)S(1)}, bf16[128,1024]{1,0:T(8,128)(2,1)S(1)}, u32[]{:S(2)}, u32[]{:S(2)}) collective-permute-start(bf16[128,1024]{1,0:T(8,128)(2,1)S(1)} %halves.3), channel_id=1, source_target_pairs={{0,16},{16,0},{1,17},{17,1},{2,18},{18,2},{3,19},{19,3},{4,20},{20... | collective-permute-start | bytes 786440 | tf_op jit(solution)/shard_map/ppermute | solution.py:202
  39.1 0.0 collective-permute-done.4.refs_2_.ref
  39.1 1.2 %collective-permute-start.12 = (bf16[128,1024]{1,0:T(8,128)(2,1)S(1)}, bf16[128,1024]{1,0:T(8,128)(2,1)S(1)}, u32[]{:S(2)}, u32[]{:S(2)}) collective-permute-start(bf16[128,1024]{1,0:T(8,128)(2,1)S(1)} %halves.2), channel_id=1, source_target_pairs={{0,2},{2,0},{1,3},{3,1},{4,6},{6,4},{5,7},{7,5},{8,10},{10,8},{9,1... | collective-permute-start | bytes 786440 | tf_op jit(solution)/shard_map/ppermute | solution.py:202
  40.3 0.0 collective-permute-done.14.refs_2_
  40.3 2.8 %collective-permute-start.21 = (bf16[128,512]{1,0:T(8,128)(2,1)S(1)}, bf16[128,512]{1,0:T(8,128)(2,1)S(1)}, u32[]{:S(2)}, u32[]{:S(2)}) collective-permute-start(bf16[128,512]{1,0:T(8,128)(2,1)S(1)} %get-tuple-element.62), channel_id=1, source_target_pairs={{0,4},{4,12},{12,8},{8,0},{1,5},{5,13},{13,9},{9,1},{2,6},{6,14},{... | collective-permute-start | bytes 393224 | tf_op jit(solution)/shard_map/ppermute | solution.py:202
  43.1 0.0 collective-permute-start.15
  43.1 0.9 %collective-permute-done.16.refs_4_ = bf16[128,640]{1,0:T(8,128)(2,1)S(1)} collective-permute-done((bf16[128,640]{1,0:T(8,128)(2,1)S(1)}, bf16[128,640]{1,0:T(8,128)(2,1)S(1)}, u32[]{:S(2)}, u32[]{:S(2)}) %collective-permute-start.16) | collective-permute-done | bytes 163872 | tf_op jit(solution)/shard_map/ppermute | solution.py:202
  44.1 1.8 %early.1 = (f32[384,1152]{1,0:T(8,128)S(1)}, bf16[384,2048]{1,0:T(8,128)(2,1)S(1)}, bf16[1536,1152]{1,0:T(8,128)(2,1)S(1)}) custom-call(bf16[128,2048]{1,0:T(8,128)(2,1)S(1)} %attend.1.refs_0_, bf16[128,2048]{1,0:T(8,128)(2,1)S(1)} %collective-permute-done.3.refs_1_.ref, bf16[128,2048]{1,0:T(8,128)(2,1)S(1)} %collective-permute-done.4.refs_2_.ref, ...), custom_call_target="tpu_custom_call" | custom-call | flops 4718592000 | tf_op jit(solution)/shard_map/early/pallas_call | solution.py:348
  45.9 0.9 %collective-permute-done.12.refs_0_ = bf16[128,1024]{1,0:T(8,128)(2,1)S(1)} collective-permute-done((bf16[128,1024]{1,0:T(8,128)(2,1)S(1)}, bf16[128,1024]{1,0:T(8,128)(2,1)S(1)}, u32[]{:S(2)}, u32[]{:S(2)}) %collective-permute-start.12) | collective-permute-done | bytes 262176 | tf_op jit(solution)/shard_map/ppermute | solution.py:202
  46.8 1.0 %project.2 = (bf16[128,640]{1,0:T(8,128)(2,1)S(1)}, bf16[128,640]{1,0:T(8,128)(2,1)S(1)}, bf16[128,640]{1,0:T(8,128)(2,1)S(1)}, bf16[128,640]{1,0:T(8,128)(2,1)S(1)}) custom-call(f32[384,1152]{1,0:T(8,128)S(1)} %get-tuple-element.48.acc, bf16[384,2048]{1,0:T(8,128)(2,1)S(1)} %get-tuple-element.49.a_all, bf16[1536,1152]{1,0:T(8,128)(2,1)S(1)} %get-tuple-element.50.w_all, ...), custom_call_target="tpu_custom_call" | custom-call | flops 4718592000 | tf_op jit(solution)/shard_map/project/pallas_call | solution.py:348
  47.8 1.3 %collective-permute-start.20 = (bf16[128,640]{1,0:T(8,128)(2,1)S(1)}, bf16[128,640]{1,0:T(8,128)(2,1)S(1)}, u32[]{:S(2)}, u32[]{:S(2)}) collective-permute-start(bf16[128,640]{1,0:T(8,128)(2,1)S(1)} %get-tuple-element.59), channel_id=1, source_target_pairs={{0,18},{2,16},{16,2},{18,0},{1,19},{3,17},{17,3},{19,1},{4,22},{6,... | collective-permute-start | bytes 491528 | tf_op jit(solution)/shard_map/ppermute | solution.py:201
  49.1 0.2 collective-permute-start.22
  49.3 0.9 %collective-permute-start.18 = (bf16[128,640]{1,0:T(8,128)(2,1)S(1)}, bf16[128,640]{1,0:T(8,128)(2,1)S(1)}, u32[]{:S(2)}, u32[]{:S(2)}) collective-permute-start(bf16[128,640]{1,0:T(8,128)(2,1)S(1)} %get-tuple-element.57), channel_id=1, source_target_pairs={{0,2},{2,0},{1,3},{3,1},{4,6},{6,4},{5,7},{7,5},{8,10},{10,8},{9,1... | collective-permute-start | bytes 491528 | tf_op jit(solution)/shard_map/ppermute | solution.py:202
  50.2 1.1 %collective-permute-start.19 = (bf16[128,640]{1,0:T(8,128)(2,1)S(1)}, bf16[128,640]{1,0:T(8,128)(2,1)S(1)}, u32[]{:S(2)}, u32[]{:S(2)}) collective-permute-start(bf16[128,640]{1,0:T(8,128)(2,1)S(1)} %get-tuple-element.58), channel_id=1, source_target_pairs={{0,16},{16,0},{1,17},{17,1},{2,18},{18,2},{3,19},{19,3},{4,20},{20... | collective-permute-start | bytes 491528 | tf_op jit(solution)/shard_map/ppermute | solution.py:202
  51.3 0.7 %project.3 = (bf16[128,512]{1,0:T(8,128)(2,1)S(1)}, bf16[128,512]{1,0:T(8,128)(2,1)S(1)}, bf16[128,512]{1,0:T(8,128)(2,1)S(1)}, bf16[128,512]{1,0:T(8,128)(2,1)S(1)}) custom-call(f32[384,1152]{1,0:T(8,128)S(1)} %get-tuple-element.48.acc, bf16[384,2048]{1,0:T(8,128)(2,1)S(1)} %get-tuple-element.49.a_all, bf16[1536,1152]{1,0:T(8,128)(2,1)S(1)} %get-tuple-element.50.w_all, ...), custom_call_target="tpu_custom_call" | custom-call | flops 1 | tf_op jit(solution)/shard_map/project/pallas_call | solution.py:348
  52.0 1.5 %collective-permute-start.25 = (bf16[128,512]{1,0:T(8,128)(2,1)S(1)}, bf16[128,512]{1,0:T(8,128)(2,1)S(1)}, u32[]{:S(2)}, u32[]{:S(2)}) collective-permute-start(bf16[128,512]{1,0:T(8,128)(2,1)S(1)} %get-tuple-element.70), channel_id=1, source_target_pairs={{0,18},{2,16},{16,2},{18,0},{1,19},{3,17},{17,3},{19,1},{4,22},{6,... | collective-permute-start | bytes 393224 | tf_op jit(solution)/shard_map/ppermute | solution.py:201
  53.5 2.3 %collective-permute-done.20.refs_3_ = bf16[128,640]{1,0:T(8,128)(2,1)S(1)} collective-permute-done((bf16[128,640]{1,0:T(8,128)(2,1)S(1)}, bf16[128,640]{1,0:T(8,128)(2,1)S(1)}, u32[]{:S(2)}, u32[]{:S(2)}) %collective-permute-start.20) | collective-permute-done | bytes 163872 | tf_op jit(solution)/shard_map/ppermute | solution.py:201
  55.8 0.6 collective-permute-start.24
  56.4 1.2 %collective-permute-start.23 = (bf16[128,512]{1,0:T(8,128)(2,1)S(1)}, bf16[128,512]{1,0:T(8,128)(2,1)S(1)}, u32[]{:S(2)}, u32[]{:S(2)}) collective-permute-start(bf16[128,512]{1,0:T(8,128)(2,1)S(1)} %get-tuple-element.66), channel_id=1, source_target_pairs={{0,2},{2,0},{1,3},{3,1},{4,6},{6,4},{5,7},{7,5},{8,10},{10,8},{9,1... | collective-permute-start | bytes 393224 | tf_op jit(solution)/shard_map/ppermute | solution.py:202
  57.6 4.6 %collective-permute-done.25.refs_7_ = bf16[128,512]{1,0:T(8,128)(2,1)S(1)} collective-permute-done((bf16[128,512]{1,0:T(8,128)(2,1)S(1)}, bf16[128,512]{1,0:T(8,128)(2,1)S(1)}, u32[]{:S(2)}, u32[]{:S(2)}) %collective-permute-start.25) | collective-permute-done | bytes 131104 | tf_op jit(solution)/shard_map/ppermute | solution.py:201
  62.2 1.5 %collective-permute-done.24.refs_6_ = bf16[128,512]{1,0:T(8,128)(2,1)S(1)} collective-permute-done((bf16[128,512]{1,0:T(8,128)(2,1)S(1)}, bf16[128,512]{1,0:T(8,128)(2,1)S(1)}, u32[]{:S(2)}, u32[]{:S(2)}) %collective-permute-start.24) | collective-permute-done | bytes 131104 | tf_op jit(solution)/shard_map/ppermute | solution.py:202
  63.6 0.1 collective-permute-done.23.refs_5_
  63.7 1.8 %finish.1 = bf16[128,4608]{1,0:T(8,128)(2,1)} custom-call(bf16[128,4608]{1,0:T(8,128)(2,1)S(1)} %bitcast.5, f32[1,4608]{1,0:T(1,128)S(1)} %reshape.3.gain_ref, bf16[128,640]{1,0:T(8,128)(2,1)S(1)} %get-tuple-element.56.refs_0_, bf16[128,640]{1,0:T(8,128)(2,1)S(1)} %collective-permute-done.18.refs_1_, bf16[128,640]{1,0:T(8,128)(2,1)S(1)} %collective-permute-done.19.refs_2_, ...), custom_call_target="tpu_custom_call" | custom-call | flops 1 | tf_op jit(solution)/shard_map/finish/pallas_call | solution.py:353
  (31 shorter events, 0.2 us)
Async XLA Ops:
  0.0 1.1 %copy-start.1 = (bf16[128,2304]{1,0:T(8,128)(2,1)S(1)}, bf16[128,2304]{1,0:T(8,128)(2,1)}, u32[]{:S(2)}) copy-start(bf16[128,2304]{1,0:T(8,128)(2,1)} %w_ref.1) | copy-start | bytes 1769476
  1.1 3.1 %copy-start.3 = (bf16[1,128,1024]{2,1,0:T(8,128)(2,1)S(1)}, bf16[1,128,1024]{2,1,0:T(8,128)(2,1)}, u32[]{:S(2)}) copy-start(bf16[1,128,1024]{2,1,0:T(8,128)(2,1)} %param.9) | copy-start | bytes 786436
  1.1 4.6 %copy-start.4 = (bf16[1,128,1024]{2,1,0:T(8,128)(2,1)S(1)}, bf16[1,128,1024]{2,1,0:T(8,128)(2,1)}, u32[]{:S(2)}) copy-start(bf16[1,128,1024]{2,1,0:T(8,128)(2,1)} %param.10) | copy-start | bytes 786436
  1.1 11.9 %copy-start.5 = (s32[1,128]{1,0:T(1,128)S(1)}, s32[1,128]{1,0:T(1,128)}, u32[]{:S(2)}) copy-start(s32[1,128]{1,0:T(1,128)} %refs_3_.1) | copy-start | bytes 1540
  1.1 13.4 %copy-start.2 = (bf16[1,128,2048]{2,1,0:T(8,128)(2,1)S(1)}, bf16[1,128,2048]{2,1,0:T(8,128)(2,1)}, u32[]{:S(2)}) copy-start(bf16[1,128,2048]{2,1,0:T(8,128)(2,1)} %param.8) | copy-start | bytes 1572868
  1.1 10.0 %collective-permute-start.5 = (bf16[128,1152]{1,0:T(8,128)(2,1)S(1)}, bf16[128,1152]{1,0:T(8,128)(2,1)S(1)}, u32[]{:S(2)}, u32[]{:S(2)}) collective-permute-start(bf16[128,1152]{1,0:T(8,128)(2,1)S(1)} %get-tuple-element.44), channel_id=1, source_target_pairs={{0,2},{2,0},{1,3},{3,1},{4,6},{6,4},{5,7},{7,5},{8,10},{10,8},{9,1... | collective-permute-start | bytes 884744 | tf_op jit(solution)/shard_map/ppermute | solution.py:202
  4.1 13.5 %collective-permute-start = (bf16[128,1024]{1,0:T(8,128)(2,1)S(1)}, bf16[128,1024]{1,0:T(8,128)(2,1)S(1)}, u32[]{:S(2)}, u32[]{:S(2)}) collective-permute-start(bf16[128,1024]{1,0:T(8,128)(2,1)S(1)} %bitcast.7), channel_id=1, source_target_pairs={{0,16},{16,0},{1,17},{17,1},{2,18},{18,2},{3,19},{19,3},{4,20},{20... | collective-permute-start | bytes 786440 | tf_op jit(solution)/shard_map/ppermute | solution.py:202
  5.7 11.9 %collective-permute-start.1 = (bf16[128,1024]{1,0:T(8,128)(2,1)S(1)}, bf16[128,1024]{1,0:T(8,128)(2,1)S(1)}, u32[]{:S(2)}, u32[]{:S(2)}) collective-permute-start(bf16[128,1024]{1,0:T(8,128)(2,1)S(1)} %bitcast.9), channel_id=1, source_target_pairs={{0,16},{16,0},{1,17},{17,1},{2,18},{18,2},{3,19},{19,3},{4,20},{20... | collective-permute-start | bytes 786440 | tf_op jit(solution)/shard_map/ppermute | solution.py:202
  6.2 12.6 %collective-permute-start.6 = (bf16[128,1152]{1,0:T(8,128)(2,1)S(1)}, bf16[128,1152]{1,0:T(8,128)(2,1)S(1)}, u32[]{:S(2)}, u32[]{:S(2)}) collective-permute-start(bf16[128,1152]{1,0:T(8,128)(2,1)S(1)} %get-tuple-element.43.refs_0_), channel_id=1, source_target_pairs={{0,4},{4,12},{12,8},{8,0},{1,5},{5,13},{13,9},{9,1},{2,6},{6,14},{... | collective-permute-start | bytes 884744 | tf_op jit(solution)/shard_map/ppermute | solution.py:202
  11.2 10.5 %collective-permute-start.7 = (bf16[128,1152]{1,0:T(8,128)(2,1)S(1)}, bf16[128,1152]{1,0:T(8,128)(2,1)S(1)}, u32[]{:S(2)}, u32[]{:S(2)}) collective-permute-start(bf16[128,1152]{1,0:T(8,128)(2,1)S(1)} %collective-permute-done.5.refs_1_), channel_id=1, source_target_pairs={{0,4},{4,12},{12,8},{8,0},{1,5},{5,13},{13,9},{9,1},{2,6},{6,14},{... | collective-permute-start | bytes 884744 | tf_op jit(solution)/shard_map/ppermute | solution.py:202
  13.0 4.6 %collective-permute-start.2 = (s32[1,128]{1,0:T(1,128)S(1)}, s32[1,128]{1,0:T(1,128)S(1)}, u32[]{:S(2)}, u32[]{:S(2)}) collective-permute-start(s32[1,128]{1,0:T(1,128)S(1)} %copy-done.5), channel_id=1, source_target_pairs={{0,16},{16,0},{1,17},{17,1},{2,18},{18,2},{3,19},{19,3},{4,20},{20... | collective-permute-start | bytes 1544 | tf_op jit(solution)/shard_map/ppermute | solution.py:202
  18.7 10.9 %collective-permute-start.9 = (bf16[128,1152]{1,0:T(8,128)(2,1)S(1)}, bf16[128,1152]{1,0:T(8,128)(2,1)S(1)}, u32[]{:S(2)}, u32[]{:S(2)}) collective-permute-start(bf16[128,1152]{1,0:T(8,128)(2,1)S(1)} %collective-permute-done.6.refs_2_), channel_id=1, source_target_pairs={{0,4},{4,12},{12,8},{8,0},{1,5},{5,13},{13,9},{9,1},{2,6},{6,14},{... | collective-permute-start | bytes 884744 | tf_op jit(solution)/shard_map/ppermute | solution.py:202
  21.7 14.3 %collective-permute-start.10 = (bf16[128,1152]{1,0:T(8,128)(2,1)S(1)}, bf16[128,1152]{1,0:T(8,128)(2,1)S(1)}, u32[]{:S(2)}, u32[]{:S(2)}) collective-permute-start(bf16[128,1152]{1,0:T(8,128)(2,1)S(1)} %collective-permute-done.7.refs_3_), channel_id=1, source_target_pairs={{0,4},{4,12},{12,8},{8,0},{1,5},{5,13},{13,9},{9,1},{2,6},{6,14},{... | collective-permute-start | bytes 884744 | tf_op jit(solution)/shard_map/ppermute | solution.py:202
  23.0 13.1 %collective-permute-start.8 = (bf16[512,1152]{1,0:T(8,128)(2,1)S(1)}, bf16[512,1152]{1,0:T(8,128)(2,1)S(1)}, u32[]{:S(2)}, u32[]{:S(2)}) collective-permute-start(bf16[512,1152]{1,0:T(8,128)(2,1)S(1)} %stack.2.refs_3_), channel_id=1, source_target_pairs={{0,1},{1,0},{2,3},{3,2},{4,5},{5,4},{6,7},{7,6},{8,9},{9,8},{10,11... | collective-permute-start | bytes 3538952 | tf_op jit(solution)/shard_map/ppermute | solution.py:202
  23.1 14.3 %collective-permute-start.3 = (bf16[128,2048]{1,0:T(8,128)(2,1)S(1)}, bf16[128,2048]{1,0:T(8,128)(2,1)S(1)}, u32[]{:S(2)}, u32[]{:S(2)}) collective-permute-start(bf16[128,2048]{1,0:T(8,128)(2,1)S(1)} %attend.1.refs_0_), channel_id=1, source_target_pairs={{0,2},{2,0},{1,3},{3,1},{4,6},{6,4},{5,7},{7,5},{8,10},{10,8},{9,1... | collective-permute-start | bytes 1572872 | tf_op jit(solution)/shard_map/ppermute | solution.py:202
  24.3 14.8 %collective-permute-start.4 = (bf16[128,2048]{1,0:T(8,128)(2,1)S(1)}, bf16[128,2048]{1,0:T(8,128)(2,1)S(1)}, u32[]{:S(2)}, u32[]{:S(2)}) collective-permute-start(bf16[128,2048]{1,0:T(8,128)(2,1)S(1)} %attend.1.refs_0_), channel_id=1, source_target_pairs={{0,16},{16,0},{1,17},{17,1},{2,18},{18,2},{3,19},{19,3},{4,20},{20... | collective-permute-start | bytes 1572872 | tf_op jit(solution)/shard_map/ppermute | solution.py:202
  29.6 10.7 %collective-permute-start.14 = (bf16[128,1152]{1,0:T(8,128)(2,1)S(1)}, bf16[128,1152]{1,0:T(8,128)(2,1)S(1)}, u32[]{:S(2)}, u32[]{:S(2)}) collective-permute-start(bf16[128,1152]{1,0:T(8,128)(2,1)S(1)} %collective-permute-done.9.refs_0_), channel_id=1, source_target_pairs={{0,4},{4,12},{12,8},{8,0},{1,5},{5,13},{13,9},{9,1},{2,6},{6,14},{... | collective-permute-start | bytes 884744 | tf_op jit(solution)/shard_map/ppermute | solution.py:202
  36.0 7.1 %collective-permute-start.11 = (bf16[256,1152]{1,0:T(8,128)(2,1)S(1)}, bf16[256,1152]{1,0:T(8,128)(2,1)S(1)}, u32[]{:S(2)}, u32[]{:S(2)}) collective-permute-start(bf16[256,1152]{1,0:T(8,128)(2,1)S(1)} %stack.3.refs_5_), channel_id=1, source_target_pairs={{0,1},{1,0},{2,3},{3,2},{4,5},{5,4},{6,7},{7,6},{8,9},{9,8},{10,11... | collective-permute-start | bytes 1769480 | tf_op jit(solution)/shard_map/ppermute | solution.py:202
  36.1 7.9 %collective-permute-start.16 = (bf16[128,640]{1,0:T(8,128)(2,1)S(1)}, bf16[128,640]{1,0:T(8,128)(2,1)S(1)}, u32[]{:S(2)}, u32[]{:S(2)}) collective-permute-start(bf16[128,640]{1,0:T(8,128)(2,1)S(1)} %get-tuple-element.55), channel_id=1, source_target_pairs={{0,4},{4,12},{12,8},{8,0},{1,5},{5,13},{13,9},{9,1},{2,6},{6,14},{... | collective-permute-start | bytes 491528 | tf_op jit(solution)/shard_map/ppermute | solution.py:202
  37.5 8.4 %collective-permute-start.13 = (bf16[128,1024]{1,0:T(8,128)(2,1)S(1)}, bf16[128,1024]{1,0:T(8,128)(2,1)S(1)}, u32[]{:S(2)}, u32[]{:S(2)}) collective-permute-start(bf16[128,1024]{1,0:T(8,128)(2,1)S(1)} %halves.3), channel_id=1, source_target_pairs={{0,16},{16,0},{1,17},{17,1},{2,18},{18,2},{3,19},{19,3},{4,20},{20... | collective-permute-start | bytes 786440 | tf_op jit(solution)/shard_map/ppermute | solution.py:202
  39.1 7.7 %collective-permute-start.12 = (bf16[128,1024]{1,0:T(8,128)(2,1)S(1)}, bf16[128,1024]{1,0:T(8,128)(2,1)S(1)}, u32[]{:S(2)}, u32[]{:S(2)}) collective-permute-start(bf16[128,1024]{1,0:T(8,128)(2,1)S(1)} %halves.2), channel_id=1, source_target_pairs={{0,2},{2,0},{1,3},{3,1},{4,6},{6,4},{5,7},{7,5},{8,10},{10,8},{9,1... | collective-permute-start | bytes 786440 | tf_op jit(solution)/shard_map/ppermute | solution.py:202
  40.3 8.8 %collective-permute-start.21 = (bf16[128,512]{1,0:T(8,128)(2,1)S(1)}, bf16[128,512]{1,0:T(8,128)(2,1)S(1)}, u32[]{:S(2)}, u32[]{:S(2)}) collective-permute-start(bf16[128,512]{1,0:T(8,128)(2,1)S(1)} %get-tuple-element.62), channel_id=1, source_target_pairs={{0,4},{4,12},{12,8},{8,0},{1,5},{5,13},{13,9},{9,1},{2,6},{6,14},{... | collective-permute-start | bytes 393224 | tf_op jit(solution)/shard_map/ppermute | solution.py:202
  43.1 3.7 %collective-permute-start.15 = (bf16[128,1152]{1,0:T(8,128)(2,1)S(1)}, bf16[128,1152]{1,0:T(8,128)(2,1)S(1)}, u32[]{:S(2)}, u32[]{:S(2)}) collective-permute-start(bf16[128,1152]{1,0:T(8,128)(2,1)S(1)} %collective-permute-done.14.refs_2_), channel_id=1, source_target_pairs={{0,1},{1,0},{2,3},{3,2},{4,5},{5,4},{6,7},{7,6},{8,9},{9,8},{10,11... | collective-permute-start | bytes 884744 | tf_op jit(solution)/shard_map/ppermute | solution.py:202
  44.1 2.7 %collective-permute-start.17 = (bf16[128,640]{1,0:T(8,128)(2,1)S(1)}, bf16[128,640]{1,0:T(8,128)(2,1)S(1)}, u32[]{:S(2)}, u32[]{:S(2)}) collective-permute-start(bf16[128,640]{1,0:T(8,128)(2,1)S(1)} %collective-permute-done.16.refs_4_), channel_id=1, source_target_pairs={{0,1},{1,0},{2,3},{3,2},{4,5},{5,4},{6,7},{7,6},{8,9},{9,8},{10,11... | collective-permute-start | bytes 491528 | tf_op jit(solution)/shard_map/ppermute | solution.py:202
  47.8 8.1 %collective-permute-start.20 = (bf16[128,640]{1,0:T(8,128)(2,1)S(1)}, bf16[128,640]{1,0:T(8,128)(2,1)S(1)}, u32[]{:S(2)}, u32[]{:S(2)}) collective-permute-start(bf16[128,640]{1,0:T(8,128)(2,1)S(1)} %get-tuple-element.59), channel_id=1, source_target_pairs={{0,18},{2,16},{16,2},{18,0},{1,19},{3,17},{17,3},{19,1},{4,22},{6,... | collective-permute-start | bytes 491528 | tf_op jit(solution)/shard_map/ppermute | solution.py:201
  49.1 2.2 %collective-permute-start.22 = (bf16[128,512]{1,0:T(8,128)(2,1)S(1)}, bf16[128,512]{1,0:T(8,128)(2,1)S(1)}, u32[]{:S(2)}, u32[]{:S(2)}) collective-permute-start(bf16[128,512]{1,0:T(8,128)(2,1)S(1)} %collective-permute-done.21.refs_4_), channel_id=1, source_target_pairs={{0,1},{1,0},{2,3},{3,2},{4,5},{5,4},{6,7},{7,6},{8,9},{9,8},{10,11... | collective-permute-start | bytes 393224 | tf_op jit(solution)/shard_map/ppermute | solution.py:202
  49.3 12.9 %collective-permute-start.18 = (bf16[128,640]{1,0:T(8,128)(2,1)S(1)}, bf16[128,640]{1,0:T(8,128)(2,1)S(1)}, u32[]{:S(2)}, u32[]{:S(2)}) collective-permute-start(bf16[128,640]{1,0:T(8,128)(2,1)S(1)} %get-tuple-element.57), channel_id=1, source_target_pairs={{0,2},{2,0},{1,3},{3,1},{4,6},{6,4},{5,7},{7,5},{8,10},{10,8},{9,1... | collective-permute-start | bytes 491528 | tf_op jit(solution)/shard_map/ppermute | solution.py:202
  50.2 7.4 %copy-start.6 = (f32[4608]{0:T(1024)S(1)}, f32[4608]{0:T(1024)}, u32[]{:S(2)}) copy-start(f32[4608]{0:T(1024)} %param.12) | copy-start | bytes 55300
  50.2 13.5 %copy-start = (bf16[1,128,4608]{2,1,0:T(8,128)(2,1)S(1)}, bf16[1,128,4608]{2,1,0:T(8,128)(2,1)}, u32[]{:S(2)}) copy-start(bf16[1,128,4608]{2,1,0:T(8,128)(2,1)} %param.7) | copy-start | bytes 3538948
  50.2 12.0 %collective-permute-start.19 = (bf16[128,640]{1,0:T(8,128)(2,1)S(1)}, bf16[128,640]{1,0:T(8,128)(2,1)S(1)}, u32[]{:S(2)}, u32[]{:S(2)}) collective-permute-start(bf16[128,640]{1,0:T(8,128)(2,1)S(1)} %get-tuple-element.58), channel_id=1, source_target_pairs={{0,16},{16,0},{1,17},{17,1},{2,18},{18,2},{3,19},{19,3},{4,20},{20... | collective-permute-start | bytes 491528 | tf_op jit(solution)/shard_map/ppermute | solution.py:202
  52.0 10.1 %collective-permute-start.25 = (bf16[128,512]{1,0:T(8,128)(2,1)S(1)}, bf16[128,512]{1,0:T(8,128)(2,1)S(1)}, u32[]{:S(2)}, u32[]{:S(2)}) collective-permute-start(bf16[128,512]{1,0:T(8,128)(2,1)S(1)} %get-tuple-element.70), channel_id=1, source_target_pairs={{0,18},{2,16},{16,2},{18,0},{1,19},{3,17},{17,3},{19,1},{4,22},{6,... | collective-permute-start | bytes 393224 | tf_op jit(solution)/shard_map/ppermute | solution.py:201
  55.8 7.8 %collective-permute-start.24 = (bf16[128,512]{1,0:T(8,128)(2,1)S(1)}, bf16[128,512]{1,0:T(8,128)(2,1)S(1)}, u32[]{:S(2)}, u32[]{:S(2)}) collective-permute-start(bf16[128,512]{1,0:T(8,128)(2,1)S(1)} %get-tuple-element.69), channel_id=1, source_target_pairs={{0,16},{16,0},{1,17},{17,1},{2,18},{18,2},{3,19},{19,3},{4,20},{20... | collective-permute-start | bytes 393224 | tf_op jit(solution)/shard_map/ppermute | solution.py:202
  56.4 7.3 %collective-permute-start.23 = (bf16[128,512]{1,0:T(8,128)(2,1)S(1)}, bf16[128,512]{1,0:T(8,128)(2,1)S(1)}, u32[]{:S(2)}, u32[]{:S(2)}) collective-permute-start(bf16[128,512]{1,0:T(8,128)(2,1)S(1)} %get-tuple-element.66), channel_id=1, source_target_pairs={{0,2},{2,0},{1,3},{3,1},{4,6},{6,4},{5,7},{7,5},{8,10},{10,8},{9,1... | collective-permute-start | bytes 393224 | tf_op jit(solution)/shard_map/ppermute | solution.py:202

commit v4 on v3

--- a/solution.py
+++ b/solution.py
@@ -20,8 +20,8 @@
 CHUNKS = (640, 512)
 PACKS = (('a0', 'B0', 'a1', 'B1'), ('a2', 'B2'))
 WHOLE_STEPS = {'a': 3, 'B': 2}
-TIES = {'rx1': ('rd0',), 'B3_0': ('ck0',), 'a2': ('h1',), 'ry1': ('rd0',), 'd1': ('k1',)}
-COSTS = {'splitB': 9000, 'hy': 1500, 'proj0': 9000, 'pk0': 1500, 'cut': 9000, 'early': 9000, 'att': 3000, 'stage': 1500, 'pk1': 9000, 'hx': 6000}
+TIES = {'rd1': ('rd0',), 'ca3': ('ck0',), 'pos': ('a1',), 'hy': ('k1',)}
+COSTS = {'splitB': 9000, 'hy': 1500, 'proj0': 1500, 'pk0': 9000, 'cut': 3000, 'early': 6000, 'att': 3000, 'pk1': 6000, 'hx': 9000}
 PER_CYCLE = 524288
 FIRST = ()
 ACTS = 1

time: 65.7 us -> 64.7 us (0.985)
  waiting for transfers between devices: 27.9 us -> 22.2 us
  starting transfers between devices: 29.7 us -> 34.2 us
    ppermute x2, waiting for transfers between devices: 6.89 us -> 2.54 us  [over(): return lax.ppermute(value, ('ctx', 'x'), [(i, 3 - i) for i in range(4)])]
    ppermute x24, starting transfers between devices: 26.9 us -> 29.8 us  [over(): return lax.ppermute(value, axis, along if axis == 'z' else swap)]
    ppermute x2, starting transfers between devices: 2.82 us -> 4.41 us  [over(): return lax.ppermute(value, ('ctx', 'x'), [(i, 3 - i) for i in range(4)])]
    ppermute x24, waiting for transfers between devices: 21 us -> 19.7 us  [over(): return lax.ppermute(value, axis, along if axis == 'z' else swap)]
  transfers between devices with their start and end apart: 26 -> 26, of which waited for: 12 -> 13; matrix products, arithmetic and copies ran while one was open for 0% -> 0% of each run, Pallas kernels for 7% -> 8%
where the time goes in v4:
time: 64.7 us; the launch traced here: 64.5 us
  starting transfers between devices  34.2 us (53%)
  waiting for transfers between devices  22.2 us (34%)
  Pallas kernels  6.73 us (10%)
  local copies, waits for them, and re-layouts  1.18 us (2%)
    ppermute x24, starting transfers between devices, over(): return lax.ppermute(value, axis, along if axis == 'z' else swap)  29.8 us
    ppermute x24, waiting for transfers between devices, over(): return lax.ppermute(value, axis, along if axis == 'z' else swap)  19.7 us
    pallas_call x11, Pallas kernels, shards(): out = kernels[name][0](first, *(held[k] for k in sources[1:]))  4.89 us
    ppermute x2, starting transfers between devices, over(): return lax.ppermute(value, ('ctx', 'x'), [(i, 3 - i) for i in range(4)])  4.41 us
    ppermute x2, waiting for transfers between devices, over(): return lax.ppermute(value, ('ctx', 'x'), [(i, 3 - i) for i in range(4)])  2.54 us
    pallas_call x1, Pallas kernels, shards(): pl.pallas_call(functools.partial(finish, chunks), out_shape=bf16(tokens,...  1.83 us
  transfers between devices with their start and end apart: 26, of which 13 were waited for; matrix products, arithmetic and copies ran while one was open for 0% of the time, Pallas kernels for 8%

profile of v4, /device:TPU:0, one launch (start us, length us, event | category | flops | bytes accessed | tf_op | source)
XLA Modules:
  0.0 64.5 jit_solution(6053149816536002040)
XLA Ops:
  0.0 1.1 %copy-done.5 = bf16[128,2304]{1,0:T(8,128)(2,1)S(1)} copy-done((bf16[128,2304]{1,0:T(8,128)(2,1)S(1)}, bf16[128,2304]{1,0:T(8,128)(2,1)}, u32[]{:S(2)}) %copy-start.5) | copy-done | bytes 589848
  1.2 3.0 %collective-permute-start.6 = (bf16[128,1152]{1,0:T(8,128)(2,1)S(1)}, bf16[128,1152]{1,0:T(8,128)(2,1)S(1)}, u32[]{:S(2)}, u32[]{:S(2)}) collective-permute-start(bf16[128,1152]{1,0:T(8,128)(2,1)S(1)} %get-tuple-element.42), channel_id=1, source_target_pairs={{0,2},{2,0},{1,3},{3,1},{4,6},{6,4},{5,7},{7,5},{8,10},{10,8},{9,1... | collective-permute-start | bytes 884744 | tf_op jit(solution)/shard_map/ppermute | solution.py:202
  4.2 1.6 %collective-permute-start.2 = (bf16[128,1152]{1,0:T(8,128)(2,1)S(1)}, bf16[128,1152]{1,0:T(8,128)(2,1)S(1)}, u32[]{:S(2)}, u32[]{:S(2)}) collective-permute-start(bf16[128,1152]{1,0:T(8,128)(2,1)S(1)} %get-tuple-element.39.refs_0_), channel_id=1, source_target_pairs={{0,4},{4,12},{12,8},{8,0},{1,5},{5,13},{13,9},{9,1},{2,6},{6,14},{... | collective-permute-start | bytes 884744 | tf_op jit(solution)/shard_map/ppermute | solution.py:202
  5.8 1.5 %collective-permute-start = (bf16[128,1024]{1,0:T(8,128)(2,1)S(1)}, bf16[128,1024]{1,0:T(8,128)(2,1)S(1)}, u32[]{:S(2)}, u32[]{:S(2)}) collective-permute-start(bf16[128,1024]{1,0:T(8,128)(2,1)S(1)} %bitcast.7), channel_id=1, source_target_pairs={{0,16},{16,0},{1,17},{17,1},{2,18},{18,2},{3,19},{19,3},{4,20},{20... | collective-permute-start | bytes 786440 | tf_op jit(solution)/shard_map/ppermute | solution.py:202
  7.3 0.5 collective-permute-start.1
  7.8 3.4 %collective-permute-done.6.refs_1_ = bf16[128,1152]{1,0:T(8,128)(2,1)S(1)} collective-permute-done((bf16[128,1152]{1,0:T(8,128)(2,1)S(1)}, bf16[128,1152]{1,0:T(8,128)(2,1)S(1)}, u32[]{:S(2)}, u32[]{:S(2)}) %collective-permute-start.6) | collective-permute-done | bytes 294944 | tf_op jit(solution)/shard_map/ppermute | solution.py:202
  11.2 1.8 %collective-permute-start.7 = (bf16[128,1152]{1,0:T(8,128)(2,1)S(1)}, bf16[128,1152]{1,0:T(8,128)(2,1)S(1)}, u32[]{:S(2)}, u32[]{:S(2)}) collective-permute-start(bf16[128,1152]{1,0:T(8,128)(2,1)S(1)} %collective-permute-done.6.refs_1_), channel_id=1, source_target_pairs={{0,4},{4,12},{12,8},{8,0},{1,5},{5,13},{13,9},{9,1},{2,6},{6,14},{... | collective-permute-start | bytes 884744 | tf_op jit(solution)/shard_map/ppermute | solution.py:202
  13.1 0.5 collective-permute-done.2.refs_2_
  13.6 1.5 %collective-permute-start.3 = (s32[1,128]{1,0:T(1,128)S(1)}, s32[1,128]{1,0:T(1,128)S(1)}, u32[]{:S(2)}, u32[]{:S(2)}) collective-permute-start(s32[1,128]{1,0:T(1,128)S(1)} %copy-done.4), channel_id=1, source_target_pairs={{0,16},{16,0},{1,17},{17,1},{2,18},{18,2},{3,19},{19,3},{4,20},{20... | collective-permute-start | bytes 1544 | tf_op jit(solution)/shard_map/ppermute | solution.py:202
  15.1 0.1 stage.1
  15.2 2.1 %collective-permute-start.9 = (bf16[128,1152]{1,0:T(8,128)(2,1)S(1)}, bf16[128,1152]{1,0:T(8,128)(2,1)S(1)}, u32[]{:S(2)}, u32[]{:S(2)}) collective-permute-start(bf16[128,1152]{1,0:T(8,128)(2,1)S(1)} %collective-permute-done.2.refs_2_), channel_id=1, source_target_pairs={{0,4},{4,12},{12,8},{8,0},{1,5},{5,13},{13,9},{9,1},{2,6},{6,14},{... | collective-permute-start | bytes 884744 | tf_op jit(solution)/shard_map/ppermute | solution.py:202
  17.3 0.0 collective-permute-done.k_far
  17.3 1.6 %collective-permute-done.1.v_far = bf16[128,1024]{1,0:T(8,128)(2,1)S(1)} collective-permute-done((bf16[128,1024]{1,0:T(8,128)(2,1)S(1)}, bf16[128,1024]{1,0:T(8,128)(2,1)S(1)}, u32[]{:S(2)}, u32[]{:S(2)}) %collective-permute-start.1) | collective-permute-done | bytes 262176 | tf_op jit(solution)/shard_map/ppermute | solution.py:202
  18.9 0.1 collective-permute-done.3.pos_far
  19.0 1.1 %attend.1.refs_0_ = bf16[128,2048]{1,0:T(8,128)(2,1)S(1)} custom-call(bf16[128,2048]{1,0:T(8,128)(2,1)S(1)} %get-tuple-element.35.q_ref, bf16[128,1024]{1,0:T(8,128)(2,1)S(1)} %get-tuple-element.36.k_own, bf16[128,1024]{1,0:T(8,128)(2,1)S(1)} %collective-permute-done.k_far, bf16[128,1024]{1,0:T(8,128)(2,1)S(1)} %get-tuple-element.37.v_own, ...), custom_call_target="tpu_custom_call" | custom-call | flops 1572864000 | tf_op jit(solution)/shard_map/attend/pallas_call | solution.py:348
  20.1 0.6 collective-permute-start.4
  20.7 1.5 %collective-permute-start.5 = (bf16[128,2048]{1,0:T(8,128)(2,1)S(1)}, bf16[128,2048]{1,0:T(8,128)(2,1)S(1)}, u32[]{:S(2)}, u32[]{:S(2)}) collective-permute-start(bf16[128,2048]{1,0:T(8,128)(2,1)S(1)} %attend.1.refs_0_), channel_id=1, source_target_pairs={{0,16},{16,0},{1,17},{17,1},{2,18},{18,2},{3,19},{19,3},{4,20},{20... | collective-permute-start | bytes 1572872 | tf_op jit(solution)/shard_map/ppermute | solution.py:202
  22.2 0.0 collective-permute-done.7.refs_3_
  22.2 2.6 %collective-permute-start.10 = (bf16[128,1152]{1,0:T(8,128)(2,1)S(1)}, bf16[128,1152]{1,0:T(8,128)(2,1)S(1)}, u32[]{:S(2)}, u32[]{:S(2)}) collective-permute-start(bf16[128,1152]{1,0:T(8,128)(2,1)S(1)} %collective-permute-done.7.refs_3_), channel_id=1, source_target_pairs={{0,4},{4,12},{12,8},{8,0},{1,5},{5,13},{13,9},{9,1},{2,6},{6,14},{... | collective-permute-start | bytes 884744 | tf_op jit(solution)/shard_map/ppermute | solution.py:202
  24.8 0.1 stack.2.refs_3_
  24.9 0.1 collective-permute-start.8
  25.0 3.4 %collective-permute-done.9.refs_0_ = bf16[128,1152]{1,0:T(8,128)(2,1)S(1)} collective-permute-done((bf16[128,1152]{1,0:T(8,128)(2,1)S(1)}, bf16[128,1152]{1,0:T(8,128)(2,1)S(1)}, u32[]{:S(2)}, u32[]{:S(2)}) %collective-permute-start.9) | collective-permute-done | bytes 294944 | tf_op jit(solution)/shard_map/ppermute | solution.py:202
  28.4 1.0 %collective-permute-start.14 = (bf16[128,1152]{1,0:T(8,128)(2,1)S(1)}, bf16[128,1152]{1,0:T(8,128)(2,1)S(1)}, u32[]{:S(2)}, u32[]{:S(2)}) collective-permute-start(bf16[128,1152]{1,0:T(8,128)(2,1)S(1)} %collective-permute-done.9.refs_0_), channel_id=1, source_target_pairs={{0,4},{4,12},{12,8},{8,0},{1,5},{5,13},{13,9},{9,1},{2,6},{6,14},{... | collective-permute-start | bytes 884744 | tf_op jit(solution)/shard_map/ppermute | solution.py:202
  29.4 5.3 %collective-permute-done.10.refs_1_.ref = bf16[128,1152]{1,0:T(8,128)(2,1)S(1)} collective-permute-done((bf16[128,1152]{1,0:T(8,128)(2,1)S(1)}, bf16[128,1152]{1,0:T(8,128)(2,1)S(1)}, u32[]{:S(2)}, u32[]{:S(2)}) %collective-permute-start.10) | collective-permute-done | bytes 294944 | tf_op jit(solution)/shard_map/ppermute | solution.py:202
  34.8 0.1 collective-permute-start.11
  34.9 0.0 collective-permute-done.4.refs_1_.ref
  34.9 1.1 %collective-permute-start.16 = (bf16[128,640]{1,0:T(8,128)(2,1)S(1)}, bf16[128,640]{1,0:T(8,128)(2,1)S(1)}, u32[]{:S(2)}, u32[]{:S(2)}) collective-permute-start(bf16[128,640]{1,0:T(8,128)(2,1)S(1)} %get-tuple-element.52), channel_id=1, source_target_pairs={{0,4},{4,12},{12,8},{8,0},{1,5},{5,13},{13,9},{9,1},{2,6},{6,14},{... | collective-permute-start | bytes 491528 | tf_op jit(solution)/shard_map/ppermute | solution.py:202
  36.0 1.6 %collective-permute-start.13 = (bf16[128,1024]{1,0:T(8,128)(2,1)S(1)}, bf16[128,1024]{1,0:T(8,128)(2,1)S(1)}, u32[]{:S(2)}, u32[]{:S(2)}) collective-permute-start(bf16[128,1024]{1,0:T(8,128)(2,1)S(1)} %halves.3), channel_id=1, source_target_pairs={{0,16},{16,0},{1,17},{17,1},{2,18},{18,2},{3,19},{19,3},{4,20},{20... | collective-permute-start | bytes 786440 | tf_op jit(solution)/shard_map/ppermute | solution.py:202
  37.6 1.6 %collective-permute-start.12 = (bf16[128,1024]{1,0:T(8,128)(2,1)S(1)}, bf16[128,1024]{1,0:T(8,128)(2,1)S(1)}, u32[]{:S(2)}, u32[]{:S(2)}) collective-permute-start(bf16[128,1024]{1,0:T(8,128)(2,1)S(1)} %halves.2), channel_id=1, source_target_pairs={{0,2},{2,0},{1,3},{3,1},{4,6},{6,4},{5,7},{7,5},{8,10},{10,8},{9,1... | collective-permute-start | bytes 786440 | tf_op jit(solution)/shard_map/ppermute | solution.py:202
  39.2 0.4 collective-permute-done.14.refs_2_
  39.6 3.0 %collective-permute-start.21 = (bf16[128,512]{1,0:T(8,128)(2,1)S(1)}, bf16[128,512]{1,0:T(8,128)(2,1)S(1)}, u32[]{:S(2)}, u32[]{:S(2)}) collective-permute-start(bf16[128,512]{1,0:T(8,128)(2,1)S(1)} %get-tuple-element.58), channel_id=1, source_target_pairs={{0,4},{4,12},{12,8},{8,0},{1,5},{5,13},{13,9},{9,1},{2,6},{6,14},{... | collective-permute-start | bytes 393224 | tf_op jit(solution)/shard_map/ppermute | solution.py:202
  42.6 0.5 collective-permute-done.16.refs_4_
  43.1 0.5 collective-permute-start.15
  43.6 1.8 %early.1 = (f32[384,1152]{1,0:T(8,128)S(1)}, bf16[384,2048]{1,0:T(8,128)(2,1)S(1)}, bf16[1536,1152]{1,0:T(8,128)(2,1)S(1)}) custom-call(bf16[128,2048]{1,0:T(8,128)(2,1)S(1)} %attend.1.refs_0_, bf16[128,2048]{1,0:T(8,128)(2,1)S(1)} %collective-permute-done.4.refs_1_.ref, bf16[128,2048]{1,0:T(8,128)(2,1)S(1)} %collective-permute-done.5.refs_2_.ref, ...), custom_call_target="tpu_custom_call" | custom-call | flops 3145728000 | tf_op jit(solution)/shard_map/early/pallas_call | solution.py:348
  45.5 0.4 collective-permute-done.12.refs_0_
  45.8 1.0 %project.2 = (bf16[128,640]{1,0:T(8,128)(2,1)S(1)}, bf16[128,640]{1,0:T(8,128)(2,1)S(1)}, bf16[128,640]{1,0:T(8,128)(2,1)S(1)}, bf16[128,640]{1,0:T(8,128)(2,1)S(1)}) custom-call(f32[384,1152]{1,0:T(8,128)S(1)} %get-tuple-element.45.acc, bf16[384,2048]{1,0:T(8,128)(2,1)S(1)} %get-tuple-element.46.a_all, bf16[1536,1152]{1,0:T(8,128)(2,1)S(1)} %get-tuple-element.47.w_all, ...), custom_call_target="tpu_custom_call" | custom-call | flops 786432000 | tf_op jit(solution)/shard_map/project/pallas_call | solution.py:348
  46.8 2.2 %collective-permute-start.20 = (bf16[128,640]{1,0:T(8,128)(2,1)S(1)}, bf16[128,640]{1,0:T(8,128)(2,1)S(1)}, u32[]{:S(2)}, u32[]{:S(2)}) collective-permute-start(bf16[128,640]{1,0:T(8,128)(2,1)S(1)} %get-tuple-element.56), channel_id=1, source_target_pairs={{0,18},{2,16},{16,2},{18,0},{1,19},{3,17},{17,3},{19,1},{4,22},{6,... | collective-permute-start | bytes 491528 | tf_op jit(solution)/shard_map/ppermute | solution.py:201
  49.0 0.5 collective-permute-start.18
  49.5 0.9 %collective-permute-start.19 = (bf16[128,640]{1,0:T(8,128)(2,1)S(1)}, bf16[128,640]{1,0:T(8,128)(2,1)S(1)}, u32[]{:S(2)}, u32[]{:S(2)}) collective-permute-start(bf16[128,640]{1,0:T(8,128)(2,1)S(1)} %get-tuple-element.55), channel_id=1, source_target_pairs={{0,16},{16,0},{1,17},{17,1},{2,18},{18,2},{3,19},{19,3},{4,20},{20... | collective-permute-start | bytes 491528 | tf_op jit(solution)/shard_map/ppermute | solution.py:202
  50.4 0.7 %project.3 = (bf16[128,512]{1,0:T(8,128)(2,1)S(1)}, bf16[128,512]{1,0:T(8,128)(2,1)S(1)}, bf16[128,512]{1,0:T(8,128)(2,1)S(1)}, bf16[128,512]{1,0:T(8,128)(2,1)S(1)}) custom-call(f32[384,1152]{1,0:T(8,128)S(1)} %get-tuple-element.45.acc, bf16[384,2048]{1,0:T(8,128)(2,1)S(1)} %get-tuple-element.46.a_all, bf16[1536,1152]{1,0:T(8,128)(2,1)S(1)} %get-tuple-element.47.w_all, ...), custom_call_target="tpu_custom_call" | custom-call | flops 1 | tf_op jit(solution)/shard_map/project/pallas_call | solution.py:348
  51.0 1.6 %collective-permute-start.23 = (bf16[128,512]{1,0:T(8,128)(2,1)S(1)}, bf16[128,512]{1,0:T(8,128)(2,1)S(1)}, u32[]{:S(2)}, u32[]{:S(2)}) collective-permute-start(bf16[128,512]{1,0:T(8,128)(2,1)S(1)} %get-tuple-element.60), channel_id=1, source_target_pairs={{0,2},{2,0},{1,3},{3,1},{4,6},{6,4},{5,7},{7,5},{8,10},{10,8},{9,1... | collective-permute-start | bytes 393224 | tf_op jit(solution)/shard_map/ppermute | solution.py:202
  52.6 1.2 %collective-permute-start.24 = (bf16[128,512]{1,0:T(8,128)(2,1)S(1)}, bf16[128,512]{1,0:T(8,128)(2,1)S(1)}, u32[]{:S(2)}, u32[]{:S(2)}) collective-permute-start(bf16[128,512]{1,0:T(8,128)(2,1)S(1)} %get-tuple-element.61), channel_id=1, source_target_pairs={{0,16},{16,0},{1,17},{17,1},{2,18},{18,2},{3,19},{19,3},{4,20},{20... | collective-permute-start | bytes 393224 | tf_op jit(solution)/shard_map/ppermute | solution.py:202
  53.8 0.9 %collective-permute-done.20.refs_3_ = bf16[128,640]{1,0:T(8,128)(2,1)S(1)} collective-permute-done((bf16[128,640]{1,0:T(8,128)(2,1)S(1)}, bf16[128,640]{1,0:T(8,128)(2,1)S(1)}, u32[]{:S(2)}, u32[]{:S(2)}) %collective-permute-start.20) | collective-permute-done | bytes 163872 | tf_op jit(solution)/shard_map/ppermute | solution.py:201
  54.7 2.2 %collective-permute-start.25 = (bf16[128,512]{1,0:T(8,128)(2,1)S(1)}, bf16[128,512]{1,0:T(8,128)(2,1)S(1)}, u32[]{:S(2)}, u32[]{:S(2)}) collective-permute-start(bf16[128,512]{1,0:T(8,128)(2,1)S(1)} %get-tuple-element.64), channel_id=1, source_target_pairs={{0,18},{2,16},{16,2},{18,0},{1,19},{3,17},{17,3},{19,1},{4,22},{6,... | collective-permute-start | bytes 393224 | tf_op jit(solution)/shard_map/ppermute | solution.py:201
  56.9 3.9 %collective-permute-done.23.refs_5_ = bf16[128,512]{1,0:T(8,128)(2,1)S(1)} collective-permute-done((bf16[128,512]{1,0:T(8,128)(2,1)S(1)}, bf16[128,512]{1,0:T(8,128)(2,1)S(1)}, u32[]{:S(2)}, u32[]{:S(2)}) %collective-permute-start.23) | collective-permute-done | bytes 131104 | tf_op jit(solution)/shard_map/ppermute | solution.py:202
  60.8 0.2 collective-permute-done.24.refs_6_
  61.0 1.6 %collective-permute-done.25.refs_7_ = bf16[128,512]{1,0:T(8,128)(2,1)S(1)} collective-permute-done((bf16[128,512]{1,0:T(8,128)(2,1)S(1)}, bf16[128,512]{1,0:T(8,128)(2,1)S(1)}, u32[]{:S(2)}, u32[]{:S(2)}) %collective-permute-start.25) | collective-permute-done | bytes 131104 | tf_op jit(solution)/shard_map/ppermute | solution.py:201
  62.7 1.8 %finish.1 = bf16[128,4608]{1,0:T(8,128)(2,1)} custom-call(bf16[128,4608]{1,0:T(8,128)(2,1)S(1)} %bitcast.5, f32[1,4608]{1,0:T(1,128)S(1)} %reshape.3.gain_ref, bf16[128,640]{1,0:T(8,128)(2,1)S(1)} %get-tuple-element.53.refs_0_, bf16[128,640]{1,0:T(8,128)(2,1)S(1)} %collective-permute-done.18.refs_1_, bf16[128,640]{1,0:T(8,128)(2,1)S(1)} %collective-permute-done.19.refs_2_, ...), custom_call_target="tpu_custom_call" | custom-call | flops 1 | tf_op jit(solution)/shard_map/finish/pallas_call | solution.py:353
  (31 shorter events, 0.2 us)
Async XLA Ops:
  0.0 5.8 %copy-start.2 = (bf16[1,128,1024]{2,1,0:T(8,128)(2,1)S(1)}, bf16[1,128,1024]{2,1,0:T(8,128)(2,1)}, u32[]{:S(2)}) copy-start(bf16[1,128,1024]{2,1,0:T(8,128)(2,1)} %param.9) | copy-start | bytes 786436
  0.0 7.3 %copy-start.3 = (bf16[1,128,1024]{2,1,0:T(8,128)(2,1)S(1)}, bf16[1,128,1024]{2,1,0:T(8,128)(2,1)}, u32[]{:S(2)}) copy-start(bf16[1,128,1024]{2,1,0:T(8,128)(2,1)} %param.10) | copy-start | bytes 786436
  0.0 13.6 %copy-start.4 = (s32[1,128]{1,0:T(1,128)S(1)}, s32[1,128]{1,0:T(1,128)}, u32[]{:S(2)}) copy-start(s32[1,128]{1,0:T(1,128)} %refs_3_.1) | copy-start | bytes 1540
  0.0 15.1 %copy-start.1 = (bf16[1,128,2048]{2,1,0:T(8,128)(2,1)S(1)}, bf16[1,128,2048]{2,1,0:T(8,128)(2,1)}, u32[]{:S(2)}) copy-start(bf16[1,128,2048]{2,1,0:T(8,128)(2,1)} %param.8) | copy-start | bytes 1572868
  0.0 1.2 %copy-start.5 = (bf16[128,2304]{1,0:T(8,128)(2,1)S(1)}, bf16[128,2304]{1,0:T(8,128)(2,1)}, u32[]{:S(2)}) copy-start(bf16[128,2304]{1,0:T(8,128)(2,1)} %w_ref.1) | copy-start | bytes 1769476
  1.2 10.0 %collective-permute-start.6 = (bf16[128,1152]{1,0:T(8,128)(2,1)S(1)}, bf16[128,1152]{1,0:T(8,128)(2,1)S(1)}, u32[]{:S(2)}, u32[]{:S(2)}) collective-permute-start(bf16[128,1152]{1,0:T(8,128)(2,1)S(1)} %get-tuple-element.42), channel_id=1, source_target_pairs={{0,2},{2,0},{1,3},{3,1},{4,6},{6,4},{5,7},{7,5},{8,10},{10,8},{9,1... | collective-permute-start | bytes 884744 | tf_op jit(solution)/shard_map/ppermute | solution.py:202
  4.2 9.4 %collective-permute-start.2 = (bf16[128,1152]{1,0:T(8,128)(2,1)S(1)}, bf16[128,1152]{1,0:T(8,128)(2,1)S(1)}, u32[]{:S(2)}, u32[]{:S(2)}) collective-permute-start(bf16[128,1152]{1,0:T(8,128)(2,1)S(1)} %get-tuple-element.39.refs_0_), channel_id=1, source_target_pairs={{0,4},{4,12},{12,8},{8,0},{1,5},{5,13},{13,9},{9,1},{2,6},{6,14},{... | collective-permute-start | bytes 884744 | tf_op jit(solution)/shard_map/ppermute | solution.py:202
  5.8 11.5 %collective-permute-start = (bf16[128,1024]{1,0:T(8,128)(2,1)S(1)}, bf16[128,1024]{1,0:T(8,128)(2,1)S(1)}, u32[]{:S(2)}, u32[]{:S(2)}) collective-permute-start(bf16[128,1024]{1,0:T(8,128)(2,1)S(1)} %bitcast.7), channel_id=1, source_target_pairs={{0,16},{16,0},{1,17},{17,1},{2,18},{18,2},{3,19},{19,3},{4,20},{20... | collective-permute-start | bytes 786440 | tf_op jit(solution)/shard_map/ppermute | solution.py:202
  7.3 11.6 %collective-permute-start.1 = (bf16[128,1024]{1,0:T(8,128)(2,1)S(1)}, bf16[128,1024]{1,0:T(8,128)(2,1)S(1)}, u32[]{:S(2)}, u32[]{:S(2)}) collective-permute-start(bf16[128,1024]{1,0:T(8,128)(2,1)S(1)} %bitcast.9), channel_id=1, source_target_pairs={{0,16},{16,0},{1,17},{17,1},{2,18},{18,2},{3,19},{19,3},{4,20},{20... | collective-permute-start | bytes 786440 | tf_op jit(solution)/shard_map/ppermute | solution.py:202
  11.2 11.0 %collective-permute-start.7 = (bf16[128,1152]{1,0:T(8,128)(2,1)S(1)}, bf16[128,1152]{1,0:T(8,128)(2,1)S(1)}, u32[]{:S(2)}, u32[]{:S(2)}) collective-permute-start(bf16[128,1152]{1,0:T(8,128)(2,1)S(1)} %collective-permute-done.6.refs_1_), channel_id=1, source_target_pairs={{0,4},{4,12},{12,8},{8,0},{1,5},{5,13},{13,9},{9,1},{2,6},{6,14},{... | collective-permute-start | bytes 884744 | tf_op jit(solution)/shard_map/ppermute | solution.py:202
  13.6 5.4 %collective-permute-start.3 = (s32[1,128]{1,0:T(1,128)S(1)}, s32[1,128]{1,0:T(1,128)S(1)}, u32[]{:S(2)}, u32[]{:S(2)}) collective-permute-start(s32[1,128]{1,0:T(1,128)S(1)} %copy-done.4), channel_id=1, source_target_pairs={{0,16},{16,0},{1,17},{17,1},{2,18},{18,2},{3,19},{19,3},{4,20},{20... | collective-permute-start | bytes 1544 | tf_op jit(solution)/shard_map/ppermute | solution.py:202
  15.2 13.2 %collective-permute-start.9 = (bf16[128,1152]{1,0:T(8,128)(2,1)S(1)}, bf16[128,1152]{1,0:T(8,128)(2,1)S(1)}, u32[]{:S(2)}, u32[]{:S(2)}) collective-permute-start(bf16[128,1152]{1,0:T(8,128)(2,1)S(1)} %collective-permute-done.2.refs_2_), channel_id=1, source_target_pairs={{0,4},{4,12},{12,8},{8,0},{1,5},{5,13},{13,9},{9,1},{2,6},{6,14},{... | collective-permute-start | bytes 884744 | tf_op jit(solution)/shard_map/ppermute | solution.py:202
  20.1 14.8 %collective-permute-start.4 = (bf16[128,2048]{1,0:T(8,128)(2,1)S(1)}, bf16[128,2048]{1,0:T(8,128)(2,1)S(1)}, u32[]{:S(2)}, u32[]{:S(2)}) collective-permute-start(bf16[128,2048]{1,0:T(8,128)(2,1)S(1)} %attend.1.refs_0_), channel_id=1, source_target_pairs={{0,2},{2,0},{1,3},{3,1},{4,6},{6,4},{5,7},{7,5},{8,10},{10,8},{9,1... | collective-permute-start | bytes 1572872 | tf_op jit(solution)/shard_map/ppermute | solution.py:202
  20.7 15.3 %collective-permute-start.5 = (bf16[128,2048]{1,0:T(8,128)(2,1)S(1)}, bf16[128,2048]{1,0:T(8,128)(2,1)S(1)}, u32[]{:S(2)}, u32[]{:S(2)}) collective-permute-start(bf16[128,2048]{1,0:T(8,128)(2,1)S(1)} %attend.1.refs_0_), channel_id=1, source_target_pairs={{0,16},{16,0},{1,17},{17,1},{2,18},{18,2},{3,19},{19,3},{4,20},{20... | collective-permute-start | bytes 1572872 | tf_op jit(solution)/shard_map/ppermute | solution.py:202
  22.2 12.5 %collective-permute-start.10 = (bf16[128,1152]{1,0:T(8,128)(2,1)S(1)}, bf16[128,1152]{1,0:T(8,128)(2,1)S(1)}, u32[]{:S(2)}, u32[]{:S(2)}) collective-permute-start(bf16[128,1152]{1,0:T(8,128)(2,1)S(1)} %collective-permute-done.7.refs_3_), channel_id=1, source_target_pairs={{0,4},{4,12},{12,8},{8,0},{1,5},{5,13},{13,9},{9,1},{2,6},{6,14},{... | collective-permute-start | bytes 884744 | tf_op jit(solution)/shard_map/ppermute | solution.py:202
  24.9 12.7 %collective-permute-start.8 = (bf16[512,1152]{1,0:T(8,128)(2,1)S(1)}, bf16[512,1152]{1,0:T(8,128)(2,1)S(1)}, u32[]{:S(2)}, u32[]{:S(2)}) collective-permute-start(bf16[512,1152]{1,0:T(8,128)(2,1)S(1)} %stack.2.refs_3_), channel_id=1, source_target_pairs={{0,1},{1,0},{2,3},{3,2},{4,5},{5,4},{6,7},{7,6},{8,9},{9,8},{10,11... | collective-permute-start | bytes 3538952 | tf_op jit(solution)/shard_map/ppermute | solution.py:202
  28.4 11.2 %collective-permute-start.14 = (bf16[128,1152]{1,0:T(8,128)(2,1)S(1)}, bf16[128,1152]{1,0:T(8,128)(2,1)S(1)}, u32[]{:S(2)}, u32[]{:S(2)}) collective-permute-start(bf16[128,1152]{1,0:T(8,128)(2,1)S(1)} %collective-permute-done.9.refs_0_), channel_id=1, source_target_pairs={{0,4},{4,12},{12,8},{8,0},{1,5},{5,13},{13,9},{9,1},{2,6},{6,14},{... | collective-permute-start | bytes 884744 | tf_op jit(solution)/shard_map/ppermute | solution.py:202
  34.8 8.3 %collective-permute-start.11 = (bf16[256,1152]{1,0:T(8,128)(2,1)S(1)}, bf16[256,1152]{1,0:T(8,128)(2,1)S(1)}, u32[]{:S(2)}, u32[]{:S(2)}) collective-permute-start(bf16[256,1152]{1,0:T(8,128)(2,1)S(1)} %stack.3.refs_5_), channel_id=1, source_target_pairs={{0,1},{1,0},{2,3},{3,2},{4,5},{5,4},{6,7},{7,6},{8,9},{9,8},{10,11... | collective-permute-start | bytes 1769480 | tf_op jit(solution)/shard_map/ppermute | solution.py:202
  34.9 8.2 %collective-permute-start.16 = (bf16[128,640]{1,0:T(8,128)(2,1)S(1)}, bf16[128,640]{1,0:T(8,128)(2,1)S(1)}, u32[]{:S(2)}, u32[]{:S(2)}) collective-permute-start(bf16[128,640]{1,0:T(8,128)(2,1)S(1)} %get-tuple-element.52), channel_id=1, source_target_pairs={{0,4},{4,12},{12,8},{8,0},{1,5},{5,13},{13,9},{9,1},{2,6},{6,14},{... | collective-permute-start | bytes 491528 | tf_op jit(solution)/shard_map/ppermute | solution.py:202
  36.0 9.4 %collective-permute-start.13 = (bf16[128,1024]{1,0:T(8,128)(2,1)S(1)}, bf16[128,1024]{1,0:T(8,128)(2,1)S(1)}, u32[]{:S(2)}, u32[]{:S(2)}) collective-permute-start(bf16[128,1024]{1,0:T(8,128)(2,1)S(1)} %halves.3), channel_id=1, source_target_pairs={{0,16},{16,0},{1,17},{17,1},{2,18},{18,2},{3,19},{19,3},{4,20},{20... | collective-permute-start | bytes 786440 | tf_op jit(solution)/shard_map/ppermute | solution.py:202
  37.6 8.2 %collective-permute-start.12 = (bf16[128,1024]{1,0:T(8,128)(2,1)S(1)}, bf16[128,1024]{1,0:T(8,128)(2,1)S(1)}, u32[]{:S(2)}, u32[]{:S(2)}) collective-permute-start(bf16[128,1024]{1,0:T(8,128)(2,1)S(1)} %halves.2), channel_id=1, source_target_pairs={{0,2},{2,0},{1,3},{3,1},{4,6},{6,4},{5,7},{7,5},{8,10},{10,8},{9,1... | collective-permute-start | bytes 786440 | tf_op jit(solution)/shard_map/ppermute | solution.py:202
  39.6 9.4 %collective-permute-start.21 = (bf16[128,512]{1,0:T(8,128)(2,1)S(1)}, bf16[128,512]{1,0:T(8,128)(2,1)S(1)}, u32[]{:S(2)}, u32[]{:S(2)}) collective-permute-start(bf16[128,512]{1,0:T(8,128)(2,1)S(1)} %get-tuple-element.58), channel_id=1, source_target_pairs={{0,4},{4,12},{12,8},{8,0},{1,5},{5,13},{13,9},{9,1},{2,6},{6,14},{... | collective-permute-start | bytes 393224 | tf_op jit(solution)/shard_map/ppermute | solution.py:202
  43.1 2.7 %collective-permute-start.17 = (bf16[128,640]{1,0:T(8,128)(2,1)S(1)}, bf16[128,640]{1,0:T(8,128)(2,1)S(1)}, u32[]{:S(2)}, u32[]{:S(2)}) collective-permute-start(bf16[128,640]{1,0:T(8,128)(2,1)S(1)} %collective-permute-done.16.refs_4_), channel_id=1, source_target_pairs={{0,1},{1,0},{2,3},{3,2},{4,5},{5,4},{6,7},{7,6},{8,9},{9,8},{10,11... | collective-permute-start | bytes 491528 | tf_op jit(solution)/shard_map/ppermute | solution.py:202
  43.1 2.7 %collective-permute-start.15 = (bf16[128,1152]{1,0:T(8,128)(2,1)S(1)}, bf16[128,1152]{1,0:T(8,128)(2,1)S(1)}, u32[]{:S(2)}, u32[]{:S(2)}) collective-permute-start(bf16[128,1152]{1,0:T(8,128)(2,1)S(1)} %collective-permute-done.14.refs_2_), channel_id=1, source_target_pairs={{0,1},{1,0},{2,3},{3,2},{4,5},{5,4},{6,7},{7,6},{8,9},{9,8},{10,11... | collective-permute-start | bytes 884744 | tf_op jit(solution)/shard_map/ppermute | solution.py:202
  46.8 7.9 %collective-permute-start.20 = (bf16[128,640]{1,0:T(8,128)(2,1)S(1)}, bf16[128,640]{1,0:T(8,128)(2,1)S(1)}, u32[]{:S(2)}, u32[]{:S(2)}) collective-permute-start(bf16[128,640]{1,0:T(8,128)(2,1)S(1)} %get-tuple-element.56), channel_id=1, source_target_pairs={{0,18},{2,16},{16,2},{18,0},{1,19},{3,17},{17,3},{19,1},{4,22},{6,... | collective-permute-start | bytes 491528 | tf_op jit(solution)/shard_map/ppermute | solution.py:201
  49.0 1.4 %collective-permute-start.22 = (bf16[128,512]{1,0:T(8,128)(2,1)S(1)}, bf16[128,512]{1,0:T(8,128)(2,1)S(1)}, u32[]{:S(2)}, u32[]{:S(2)}) collective-permute-start(bf16[128,512]{1,0:T(8,128)(2,1)S(1)} %collective-permute-done.21.refs_4_), channel_id=1, source_target_pairs={{0,1},{1,0},{2,3},{3,2},{4,5},{5,4},{6,7},{7,6},{8,9},{9,8},{10,11... | collective-permute-start | bytes 393224 | tf_op jit(solution)/shard_map/ppermute | solution.py:202
  49.0 12.0 %collective-permute-start.18 = (bf16[128,640]{1,0:T(8,128)(2,1)S(1)}, bf16[128,640]{1,0:T(8,128)(2,1)S(1)}, u32[]{:S(2)}, u32[]{:S(2)}) collective-permute-start(bf16[128,640]{1,0:T(8,128)(2,1)S(1)} %get-tuple-element.54), channel_id=1, source_target_pairs={{0,2},{2,0},{1,3},{3,1},{4,6},{6,4},{5,7},{7,5},{8,10},{10,8},{9,1... | collective-permute-start | bytes 491528 | tf_op jit(solution)/shard_map/ppermute | solution.py:202
  49.5 7.4 %copy-start.6 = (f32[4608]{0:T(1024)S(1)}, f32[4608]{0:T(1024)}, u32[]{:S(2)}) copy-start(f32[4608]{0:T(1024)} %param.12) | copy-start | bytes 55300
  49.5 13.2 %copy-start = (bf16[1,128,4608]{2,1,0:T(8,128)(2,1)S(1)}, bf16[1,128,4608]{2,1,0:T(8,128)(2,1)}, u32[]{:S(2)}) copy-start(bf16[1,128,4608]{2,1,0:T(8,128)(2,1)} %param.7) | copy-start | bytes 3538948
  49.5 11.5 %collective-permute-start.19 = (bf16[128,640]{1,0:T(8,128)(2,1)S(1)}, bf16[128,640]{1,0:T(8,128)(2,1)S(1)}, u32[]{:S(2)}, u32[]{:S(2)}) collective-permute-start(bf16[128,640]{1,0:T(8,128)(2,1)S(1)} %get-tuple-element.55), channel_id=1, source_target_pairs={{0,16},{16,0},{1,17},{17,1},{2,18},{18,2},{3,19},{19,3},{4,20},{20... | collective-permute-start | bytes 491528 | tf_op jit(solution)/shard_map/ppermute | solution.py:202
  51.0 9.8 %collective-permute-start.23 = (bf16[128,512]{1,0:T(8,128)(2,1)S(1)}, bf16[128,512]{1,0:T(8,128)(2,1)S(1)}, u32[]{:S(2)}, u32[]{:S(2)}) collective-permute-start(bf16[128,512]{1,0:T(8,128)(2,1)S(1)} %get-tuple-element.60), channel_id=1, source_target_pairs={{0,2},{2,0},{1,3},{3,1},{4,6},{6,4},{5,7},{7,5},{8,10},{10,8},{9,1... | collective-permute-start | bytes 393224 | tf_op jit(solution)/shard_map/ppermute | solution.py:202
  52.6 8.4 %collective-permute-start.24 = (bf16[128,512]{1,0:T(8,128)(2,1)S(1)}, bf16[128,512]{1,0:T(8,128)(2,1)S(1)}, u32[]{:S(2)}, u32[]{:S(2)}) collective-permute-start(bf16[128,512]{1,0:T(8,128)(2,1)S(1)} %get-tuple-element.61), channel_id=1, source_target_pairs={{0,16},{16,0},{1,17},{17,1},{2,18},{18,2},{3,19},{19,3},{4,20},{20... | collective-permute-start | bytes 393224 | tf_op jit(solution)/shard_map/ppermute | solution.py:202
  54.7 8.0 %collective-permute-start.25 = (bf16[128,512]{1,0:T(8,128)(2,1)S(1)}, bf16[128,512]{1,0:T(8,128)(2,1)S(1)}, u32[]{:S(2)}, u32[]{:S(2)}) collective-permute-start(bf16[128,512]{1,0:T(8,128)(2,1)S(1)} %get-tuple-element.64), channel_id=1, source_target_pairs={{0,18},{2,16},{16,2},{18,0},{1,19},{3,17},{17,3},{19,1},{4,22},{6,... | collective-permute-start | bytes 393224 | tf_op jit(solution)/shard_map/ppermute | solution.py:201

commit v5 on v4

--- a/solution.py
+++ b/solution.py
@@ -20,8 +20,8 @@
 CHUNKS = (640, 512)
 PACKS = (('a0', 'B0', 'a1', 'B1'), ('a2', 'B2'))
 WHOLE_STEPS = {'a': 3, 'B': 2}
-TIES = {'rd1': ('rd0',), 'ca3': ('ck0',), 'pos': ('a1',), 'hy': ('k1',)}
-COSTS = {'splitB': 9000, 'hy': 1500, 'proj0': 1500, 'pk0': 9000, 'cut': 3000, 'early': 6000, 'att': 3000, 'pk1': 6000, 'hx': 9000}
+TIES = {'rd1': ('rd0',), 'ca3': ('ck1',), 'pos': ('a1',), 'hy': ('k1',), 'B3_0': ('y1l',)}
+COSTS = {'splitB': 9000, 'hy': 1500, 'proj0': 1500, 'pk0': 9000, 'cut': 3000, 'early': 6000, 'att': 3000, 'pk1': 6000, 'hx': 12000}
 PER_CYCLE = 524288
 FIRST = ()
 ACTS = 1
@@ -165,26 +165,34 @@
 
 def finish(chunks, hidden_ref, gain_ref, *refs):
     pieces, out_hbm, out_ref, sems = refs[:-3], refs[-3], refs[-2], refs[-1]
-    width = hidden_ref.shape[1]
+    rows, width = hidden_ref.shape
     x, y = lax.axis_index("x"), lax.axis_index("ctx")
     owners = ((x, y), (1 - x, y), (x, 1 - y), (1 - x, 1 - y))
-    total = 0.0
-    for piece in pieces:
-        value = piece[...].astype(jnp.float32)
-        total = total + jnp.sum(value * value, axis=-1, keepdims=True)
-    scale = lax.rsqrt(total / width + norm_eps)
+    places = []
     start = 0
+    for columns in chunks:
+        for px, py in owners:
+            places.append(
+                pl.ds(pl.multiple_of((py * 2 + px) * (width // 4) + start, 128), columns)
+            )
+        start += columns
     copies = []
-    for c, columns in enumerate(chunks):
-        for i, (px, py) in enumerate(owners):
-            at = pl.ds(pl.multiple_of((py * 2 + px) * (width // 4) + start, 128), columns)
-            normed = pieces[c * 4 + i][...].astype(jnp.float32) * scale * gain_ref[:, at]
-            out_ref[:, at] = (hidden_ref[:, at].astype(jnp.float32) + normed).astype(jnp.bfloat16)
-            copies.append(
-                pltpu.make_async_copy(out_ref.at[:, at], out_hbm.at[:, at], sems.at[c * 4 + i])
+    step = 16
+    for i, top in enumerate(range(0, rows, step)):
+        block = pl.ds(top, step)
+        squares = jnp.zeros((step, 128), jnp.float32)
+        for piece in pieces:
+            for at in range(0, piece.shape[1], 128):
+                value = piece[block, pl.ds(at, 128)].astype(jnp.float32)
+                squares = squares + value * value
+        scale = lax.rsqrt(jnp.sum(squares, axis=-1, keepdims=True) / width + norm_eps)
+        for piece, at in zip(pieces, places):
+            normed = piece[block, :].astype(jnp.float32) * scale * gain_ref[:, at]
+            out_ref[block, at] = (hidden_ref[block, at].astype(jnp.float32) + normed).astype(
+                jnp.bfloat16
             )
-            copies[-1].start()
-        start += columns
+        copies.append(pltpu.make_async_copy(out_ref.at[block], out_hbm.at[block], sems.at[i]))
+        copies[-1].start()
     for copy in copies:
         copy.wait()
 
@@ -357,7 +365,7 @@
         out_specs=HBM,
         scratch_shapes=[
             pltpu.VMEM((tokens, width), jnp.bfloat16),
-            pltpu.SemaphoreType.DMA((len(pieces),)),
+            pltpu.SemaphoreType.DMA((tokens // 16,)),
         ],
         compiler_params=params(),
         cost_estimate=pl.CostEstimate(flops=1, bytes_accessed=0, transcendentals=0),

time: 64.7 us -> 64.2 us (level)
  transfers between devices with their start and end apart: 26 -> 26, of which waited for: 13 -> 14; matrix products, arithmetic and copies ran while one was open for 0% -> 0% of each run, Pallas kernels for 8% -> 8%
where the time goes in v5:
time: 64.2 us; the launch traced here: 64.1 us
  starting transfers between devices  34.1 us (53%)
  waiting for transfers between devices  22.3 us (35%)
  Pallas kernels  6.32 us (10%)
  local copies, waits for them, and re-layouts  1.18 us (2%)
    ppermute x24, starting transfers between devices, over(): return lax.ppermute(value, axis, along if axis == 'z' else swap)  29.6 us
    ppermute x24, waiting for transfers between devices, over(): return lax.ppermute(value, axis, along if axis == 'z' else swap)  19.8 us
    pallas_call x11, Pallas kernels, shards(): out = kernels[name][0](first, *(held[k] for k in sources[1:]))  4.89 us
    ppermute x2, starting transfers between devices, over(): return lax.ppermute(value, ('ctx', 'x'), [(i, 3 - i) for i in range(4)])  4.51 us
    ppermute x2, waiting for transfers between devices, over(): return lax.ppermute(value, ('ctx', 'x'), [(i, 3 - i) for i in range(4)])  2.48 us
    pallas_call x1, Pallas kernels, shards(): pl.pallas_call(functools.partial(finish, chunks), out_shape=bf16(tokens,...  1.43 us
  transfers between devices with their start and end apart: 26, of which 14 were waited for; matrix products, arithmetic and copies ran while one was open for 0% of the time, Pallas kernels for 8%

profile of v5, /device:TPU:0, one launch (start us, length us, event | category | flops | bytes accessed | tf_op | source)
XLA Modules:
  0.0 64.1 jit_solution(10686901444276442621)
XLA Ops:
  0.0 1.1 %copy-done.5 = bf16[128,2304]{1,0:T(8,128)(2,1)S(1)} copy-done((bf16[128,2304]{1,0:T(8,128)(2,1)S(1)}, bf16[128,2304]{1,0:T(8,128)(2,1)}, u32[]{:S(2)}) %copy-start.5) | copy-done | bytes 589848
  1.2 3.0 %collective-permute-start.6 = (bf16[128,1152]{1,0:T(8,128)(2,1)S(1)}, bf16[128,1152]{1,0:T(8,128)(2,1)S(1)}, u32[]{:S(2)}, u32[]{:S(2)}) collective-permute-start(bf16[128,1152]{1,0:T(8,128)(2,1)S(1)} %get-tuple-element.44), channel_id=1, source_target_pairs={{0,2},{2,0},{1,3},{3,1},{4,6},{6,4},{5,7},{7,5},{8,10},{10,8},{9,1... | collective-permute-start | bytes 884744 | tf_op jit(solution)/shard_map/ppermute | solution.py:210
  4.2 1.6 %collective-permute-start.2 = (bf16[128,1152]{1,0:T(8,128)(2,1)S(1)}, bf16[128,1152]{1,0:T(8,128)(2,1)S(1)}, u32[]{:S(2)}, u32[]{:S(2)}) collective-permute-start(bf16[128,1152]{1,0:T(8,128)(2,1)S(1)} %get-tuple-element.41.refs_0_), channel_id=1, source_target_pairs={{0,4},{4,12},{12,8},{8,0},{1,5},{5,13},{13,9},{9,1},{2,6},{6,14},{... | collective-permute-start | bytes 884744 | tf_op jit(solution)/shard_map/ppermute | solution.py:210
  5.8 1.5 %collective-permute-start = (bf16[128,1024]{1,0:T(8,128)(2,1)S(1)}, bf16[128,1024]{1,0:T(8,128)(2,1)S(1)}, u32[]{:S(2)}, u32[]{:S(2)}) collective-permute-start(bf16[128,1024]{1,0:T(8,128)(2,1)S(1)} %bitcast.7), channel_id=1, source_target_pairs={{0,16},{16,0},{1,17},{17,1},{2,18},{18,2},{3,19},{19,3},{4,20},{20... | collective-permute-start | bytes 786440 | tf_op jit(solution)/shard_map/ppermute | solution.py:210
  7.3 0.5 collective-permute-start.1
  7.8 3.4 %collective-permute-done.6.refs_1_ = bf16[128,1152]{1,0:T(8,128)(2,1)S(1)} collective-permute-done((bf16[128,1152]{1,0:T(8,128)(2,1)S(1)}, bf16[128,1152]{1,0:T(8,128)(2,1)S(1)}, u32[]{:S(2)}, u32[]{:S(2)}) %collective-permute-start.6) | collective-permute-done | bytes 294944 | tf_op jit(solution)/shard_map/ppermute | solution.py:210
  11.2 1.8 %collective-permute-start.7 = (bf16[128,1152]{1,0:T(8,128)(2,1)S(1)}, bf16[128,1152]{1,0:T(8,128)(2,1)S(1)}, u32[]{:S(2)}, u32[]{:S(2)}) collective-permute-start(bf16[128,1152]{1,0:T(8,128)(2,1)S(1)} %collective-permute-done.6.refs_1_), channel_id=1, source_target_pairs={{0,4},{4,12},{12,8},{8,0},{1,5},{5,13},{13,9},{9,1},{2,6},{6,14},{... | collective-permute-start | bytes 884744 | tf_op jit(solution)/shard_map/ppermute | solution.py:210
  13.1 0.5 collective-permute-done.2.refs_2_
  13.6 1.5 %collective-permute-start.3 = (s32[1,128]{1,0:T(1,128)S(1)}, s32[1,128]{1,0:T(1,128)S(1)}, u32[]{:S(2)}, u32[]{:S(2)}) collective-permute-start(s32[1,128]{1,0:T(1,128)S(1)} %copy-done.4), channel_id=1, source_target_pairs={{0,16},{16,0},{1,17},{17,1},{2,18},{18,2},{3,19},{19,3},{4,20},{20... | collective-permute-start | bytes 1544 | tf_op jit(solution)/shard_map/ppermute | solution.py:210
  15.1 0.1 stage.1
  15.2 2.1 %collective-permute-start.9 = (bf16[128,1152]{1,0:T(8,128)(2,1)S(1)}, bf16[128,1152]{1,0:T(8,128)(2,1)S(1)}, u32[]{:S(2)}, u32[]{:S(2)}) collective-permute-start(bf16[128,1152]{1,0:T(8,128)(2,1)S(1)} %collective-permute-done.2.refs_2_), channel_id=1, source_target_pairs={{0,4},{4,12},{12,8},{8,0},{1,5},{5,13},{13,9},{9,1},{2,6},{6,14},{... | collective-permute-start | bytes 884744 | tf_op jit(solution)/shard_map/ppermute | solution.py:210
  17.3 0.0 collective-permute-done.k_far
  17.3 1.6 %collective-permute-done.1.v_far = bf16[128,1024]{1,0:T(8,128)(2,1)S(1)} collective-permute-done((bf16[128,1024]{1,0:T(8,128)(2,1)S(1)}, bf16[128,1024]{1,0:T(8,128)(2,1)S(1)}, u32[]{:S(2)}, u32[]{:S(2)}) %collective-permute-start.1) | collective-permute-done | bytes 262176 | tf_op jit(solution)/shard_map/ppermute | solution.py:210
  18.9 0.1 collective-permute-done.3.pos_far
  19.0 1.1 %attend.1.refs_0_ = bf16[128,2048]{1,0:T(8,128)(2,1)S(1)} custom-call(bf16[128,2048]{1,0:T(8,128)(2,1)S(1)} %get-tuple-element.37.q_ref, bf16[128,1024]{1,0:T(8,128)(2,1)S(1)} %get-tuple-element.38.k_own, bf16[128,1024]{1,0:T(8,128)(2,1)S(1)} %collective-permute-done.k_far, bf16[128,1024]{1,0:T(8,128)(2,1)S(1)} %get-tuple-element.39.v_own, ...), custom_call_target="tpu_custom_call" | custom-call | flops 1572864000 | tf_op jit(solution)/shard_map/attend/pallas_call | solution.py:356
  20.1 0.6 collective-permute-start.4
  20.7 1.5 %collective-permute-start.5 = (bf16[128,2048]{1,0:T(8,128)(2,1)S(1)}, bf16[128,2048]{1,0:T(8,128)(2,1)S(1)}, u32[]{:S(2)}, u32[]{:S(2)}) collective-permute-start(bf16[128,2048]{1,0:T(8,128)(2,1)S(1)} %attend.1.refs_0_), channel_id=1, source_target_pairs={{0,16},{16,0},{1,17},{17,1},{2,18},{18,2},{3,19},{19,3},{4,20},{20... | collective-permute-start | bytes 1572872 | tf_op jit(solution)/shard_map/ppermute | solution.py:210
  22.2 0.0 collective-permute-done.7.refs_3_
  22.2 2.6 %collective-permute-start.10 = (bf16[128,1152]{1,0:T(8,128)(2,1)S(1)}, bf16[128,1152]{1,0:T(8,128)(2,1)S(1)}, u32[]{:S(2)}, u32[]{:S(2)}) collective-permute-start(bf16[128,1152]{1,0:T(8,128)(2,1)S(1)} %collective-permute-done.7.refs_3_), channel_id=1, source_target_pairs={{0,4},{4,12},{12,8},{8,0},{1,5},{5,13},{13,9},{9,1},{2,6},{6,14},{... | collective-permute-start | bytes 884744 | tf_op jit(solution)/shard_map/ppermute | solution.py:210
  24.8 0.1 stack.2.refs_3_
  24.9 0.1 collective-permute-start.8
  25.0 3.4 %collective-permute-done.9.refs_0_ = bf16[128,1152]{1,0:T(8,128)(2,1)S(1)} collective-permute-done((bf16[128,1152]{1,0:T(8,128)(2,1)S(1)}, bf16[128,1152]{1,0:T(8,128)(2,1)S(1)}, u32[]{:S(2)}, u32[]{:S(2)}) %collective-permute-start.9) | collective-permute-done | bytes 294944 | tf_op jit(solution)/shard_map/ppermute | solution.py:210
  28.4 1.0 %collective-permute-start.14 = (bf16[128,1152]{1,0:T(8,128)(2,1)S(1)}, bf16[128,1152]{1,0:T(8,128)(2,1)S(1)}, u32[]{:S(2)}, u32[]{:S(2)}) collective-permute-start(bf16[128,1152]{1,0:T(8,128)(2,1)S(1)} %collective-permute-done.9.refs_0_), channel_id=1, source_target_pairs={{0,4},{4,12},{12,8},{8,0},{1,5},{5,13},{13,9},{9,1},{2,6},{6,14},{... | collective-permute-start | bytes 884744 | tf_op jit(solution)/shard_map/ppermute | solution.py:210
  29.4 5.3 %collective-permute-done.10.refs_1_.ref = bf16[128,1152]{1,0:T(8,128)(2,1)S(1)} collective-permute-done((bf16[128,1152]{1,0:T(8,128)(2,1)S(1)}, bf16[128,1152]{1,0:T(8,128)(2,1)S(1)}, u32[]{:S(2)}, u32[]{:S(2)}) %collective-permute-start.10) | collective-permute-done | bytes 294944 | tf_op jit(solution)/shard_map/ppermute | solution.py:210
  34.8 0.1 collective-permute-start.11
  34.9 1.1 %collective-permute-start.16 = (bf16[128,640]{1,0:T(8,128)(2,1)S(1)}, bf16[128,640]{1,0:T(8,128)(2,1)S(1)}, u32[]{:S(2)}, u32[]{:S(2)}) collective-permute-start(bf16[128,640]{1,0:T(8,128)(2,1)S(1)} %get-tuple-element.56), channel_id=1, source_target_pairs={{0,4},{4,12},{12,8},{8,0},{1,5},{5,13},{13,9},{9,1},{2,6},{6,14},{... | collective-permute-start | bytes 491528 | tf_op jit(solution)/shard_map/ppermute | solution.py:210
  36.0 1.6 %collective-permute-start.13 = (bf16[128,1024]{1,0:T(8,128)(2,1)S(1)}, bf16[128,1024]{1,0:T(8,128)(2,1)S(1)}, u32[]{:S(2)}, u32[]{:S(2)}) collective-permute-start(bf16[128,1024]{1,0:T(8,128)(2,1)S(1)} %halves.3), channel_id=1, source_target_pairs={{0,16},{16,0},{1,17},{17,1},{2,18},{18,2},{3,19},{19,3},{4,20},{20... | collective-permute-start | bytes 786440 | tf_op jit(solution)/shard_map/ppermute | solution.py:210
  37.6 1.5 %collective-permute-start.12 = (bf16[128,1024]{1,0:T(8,128)(2,1)S(1)}, bf16[128,1024]{1,0:T(8,128)(2,1)S(1)}, u32[]{:S(2)}, u32[]{:S(2)}) collective-permute-start(bf16[128,1024]{1,0:T(8,128)(2,1)S(1)} %halves.2), channel_id=1, source_target_pairs={{0,2},{2,0},{1,3},{3,1},{4,6},{6,4},{5,7},{7,5},{8,10},{10,8},{9,1... | collective-permute-start | bytes 786440 | tf_op jit(solution)/shard_map/ppermute | solution.py:210
  39.1 0.5 collective-permute-done.14.refs_2_
  39.6 2.9 %collective-permute-start.21 = (bf16[128,512]{1,0:T(8,128)(2,1)S(1)}, bf16[128,512]{1,0:T(8,128)(2,1)S(1)}, u32[]{:S(2)}, u32[]{:S(2)}) collective-permute-start(bf16[128,512]{1,0:T(8,128)(2,1)S(1)} %get-tuple-element.62), channel_id=1, source_target_pairs={{0,4},{4,12},{12,8},{8,0},{1,5},{5,13},{13,9},{9,1},{2,6},{6,14},{... | collective-permute-start | bytes 393224 | tf_op jit(solution)/shard_map/ppermute | solution.py:210
  42.5 0.6 collective-permute-done.16.refs_4_
  43.1 0.5 collective-permute-start.15
  43.6 1.8 %early.1 = (f32[384,1152]{1,0:T(8,128)S(1)}, bf16[384,2048]{1,0:T(8,128)(2,1)S(1)}, bf16[1536,1152]{1,0:T(8,128)(2,1)S(1)}) custom-call(bf16[128,2048]{1,0:T(8,128)(2,1)S(1)} %attend.1.refs_0_, bf16[128,2048]{1,0:T(8,128)(2,1)S(1)} %collective-permute-done.4.refs_1_.ref, bf16[128,2048]{1,0:T(8,128)(2,1)S(1)} %collective-permute-done.5.refs_2_.ref, ...), custom_call_target="tpu_custom_call" | custom-call | flops 3145728000 | tf_op jit(solution)/shard_map/early/pallas_call | solution.py:356
  45.4 0.3 collective-permute-done.12.refs_0_
  45.8 1.0 %project.2 = (bf16[128,640]{1,0:T(8,128)(2,1)S(1)}, bf16[128,640]{1,0:T(8,128)(2,1)S(1)}, bf16[128,640]{1,0:T(8,128)(2,1)S(1)}, bf16[128,640]{1,0:T(8,128)(2,1)S(1)}) custom-call(f32[384,1152]{1,0:T(8,128)S(1)} %get-tuple-element.47.acc, bf16[384,2048]{1,0:T(8,128)(2,1)S(1)} %get-tuple-element.48.a_all, bf16[1536,1152]{1,0:T(8,128)(2,1)S(1)} %get-tuple-element.49.w_all, ...), custom_call_target="tpu_custom_call" | custom-call | flops 786432000 | tf_op jit(solution)/shard_map/project/pallas_call | solution.py:356
  46.7 2.3 %collective-permute-start.20 = (bf16[128,640]{1,0:T(8,128)(2,1)S(1)}, bf16[128,640]{1,0:T(8,128)(2,1)S(1)}, u32[]{:S(2)}, u32[]{:S(2)}) collective-permute-start(bf16[128,640]{1,0:T(8,128)(2,1)S(1)} %get-tuple-element.60), channel_id=1, source_target_pairs={{0,18},{2,16},{16,2},{18,0},{1,19},{3,17},{17,3},{19,1},{4,22},{6,... | collective-permute-start | bytes 491528 | tf_op jit(solution)/shard_map/ppermute | solution.py:209
  49.0 0.5 collective-permute-start.18
  49.5 0.8 %collective-permute-start.19 = (bf16[128,640]{1,0:T(8,128)(2,1)S(1)}, bf16[128,640]{1,0:T(8,128)(2,1)S(1)}, u32[]{:S(2)}, u32[]{:S(2)}) collective-permute-start(bf16[128,640]{1,0:T(8,128)(2,1)S(1)} %get-tuple-element.59), channel_id=1, source_target_pairs={{0,16},{16,0},{1,17},{17,1},{2,18},{18,2},{3,19},{19,3},{4,20},{20... | collective-permute-start | bytes 491528 | tf_op jit(solution)/shard_map/ppermute | solution.py:210
  50.3 0.1 collective-permute-done.22.refs_5_
  50.3 0.7 %project.3 = (bf16[128,512]{1,0:T(8,128)(2,1)S(1)}, bf16[128,512]{1,0:T(8,128)(2,1)S(1)}, bf16[128,512]{1,0:T(8,128)(2,1)S(1)}, bf16[128,512]{1,0:T(8,128)(2,1)S(1)}) custom-call(f32[384,1152]{1,0:T(8,128)S(1)} %get-tuple-element.47.acc, bf16[384,2048]{1,0:T(8,128)(2,1)S(1)} %get-tuple-element.48.a_all, bf16[1536,1152]{1,0:T(8,128)(2,1)S(1)} %get-tuple-element.49.w_all, ...), custom_call_target="tpu_custom_call" | custom-call | flops 1 | tf_op jit(solution)/shard_map/project/pallas_call | solution.py:356
  51.0 1.5 %collective-permute-start.23 = (bf16[128,512]{1,0:T(8,128)(2,1)S(1)}, bf16[128,512]{1,0:T(8,128)(2,1)S(1)}, u32[]{:S(2)}, u32[]{:S(2)}) collective-permute-start(bf16[128,512]{1,0:T(8,128)(2,1)S(1)} %get-tuple-element.64), channel_id=1, source_target_pairs={{0,2},{2,0},{1,3},{3,1},{4,6},{6,4},{5,7},{7,5},{8,10},{10,8},{9,1... | collective-permute-start | bytes 393224 | tf_op jit(solution)/shard_map/ppermute | solution.py:210
  52.5 1.3 %collective-permute-start.24 = (bf16[128,512]{1,0:T(8,128)(2,1)S(1)}, bf16[128,512]{1,0:T(8,128)(2,1)S(1)}, u32[]{:S(2)}, u32[]{:S(2)}) collective-permute-start(bf16[128,512]{1,0:T(8,128)(2,1)S(1)} %get-tuple-element.65), channel_id=1, source_target_pairs={{0,16},{16,0},{1,17},{17,1},{2,18},{18,2},{3,19},{19,3},{4,20},{20... | collective-permute-start | bytes 393224 | tf_op jit(solution)/shard_map/ppermute | solution.py:210
  53.8 0.9 %collective-permute-done.20.refs_3_ = bf16[128,640]{1,0:T(8,128)(2,1)S(1)} collective-permute-done((bf16[128,640]{1,0:T(8,128)(2,1)S(1)}, bf16[128,640]{1,0:T(8,128)(2,1)S(1)}, u32[]{:S(2)}, u32[]{:S(2)}) %collective-permute-start.20) | collective-permute-done | bytes 163872 | tf_op jit(solution)/shard_map/ppermute | solution.py:209
  54.7 2.2 %collective-permute-start.25 = (bf16[128,512]{1,0:T(8,128)(2,1)S(1)}, bf16[128,512]{1,0:T(8,128)(2,1)S(1)}, u32[]{:S(2)}, u32[]{:S(2)}) collective-permute-start(bf16[128,512]{1,0:T(8,128)(2,1)S(1)} %get-tuple-element.68), channel_id=1, source_target_pairs={{0,18},{2,16},{16,2},{18,0},{1,19},{3,17},{17,3},{19,1},{4,22},{6,... | collective-permute-start | bytes 393224 | tf_op jit(solution)/shard_map/ppermute | solution.py:209
  57.0 3.9 %collective-permute-done.23.refs_5_ = bf16[128,512]{1,0:T(8,128)(2,1)S(1)} collective-permute-done((bf16[128,512]{1,0:T(8,128)(2,1)S(1)}, bf16[128,512]{1,0:T(8,128)(2,1)S(1)}, u32[]{:S(2)}, u32[]{:S(2)}) %collective-permute-start.23) | collective-permute-done | bytes 131104 | tf_op jit(solution)/shard_map/ppermute | solution.py:210
  60.9 0.2 collective-permute-done.24.refs_6_
  61.1 1.6 %collective-permute-done.25.refs_7_ = bf16[128,512]{1,0:T(8,128)(2,1)S(1)} collective-permute-done((bf16[128,512]{1,0:T(8,128)(2,1)S(1)}, bf16[128,512]{1,0:T(8,128)(2,1)S(1)}, u32[]{:S(2)}, u32[]{:S(2)}) %collective-permute-start.25) | collective-permute-done | bytes 131104 | tf_op jit(solution)/shard_map/ppermute | solution.py:209
  62.7 1.4 %finish.1 = bf16[128,4608]{1,0:T(8,128)(2,1)} custom-call(bf16[128,4608]{1,0:T(8,128)(2,1)S(1)} %bitcast.5, f32[1,4608]{1,0:T(1,128)S(1)} %reshape.3.gain_ref, bf16[128,640]{1,0:T(8,128)(2,1)S(1)} %get-tuple-element.57.refs_0_, bf16[128,640]{1,0:T(8,128)(2,1)S(1)} %collective-permute-done.18.refs_1_, bf16[128,640]{1,0:T(8,128)(2,1)S(1)} %collective-permute-done.19.refs_2_, ...), custom_call_target="tpu_custom_call" | custom-call | flops 1 | tf_op jit(solution)/shard_map/finish/pallas_call | solution.py:361
  (31 shorter events, 0.2 us)
Async XLA Ops:
  0.0 5.8 %copy-start.2 = (bf16[1,128,1024]{2,1,0:T(8,128)(2,1)S(1)}, bf16[1,128,1024]{2,1,0:T(8,128)(2,1)}, u32[]{:S(2)}) copy-start(bf16[1,128,1024]{2,1,0:T(8,128)(2,1)} %param.9) | copy-start | bytes 786436
  0.0 7.3 %copy-start.3 = (bf16[1,128,1024]{2,1,0:T(8,128)(2,1)S(1)}, bf16[1,128,1024]{2,1,0:T(8,128)(2,1)}, u32[]{:S(2)}) copy-start(bf16[1,128,1024]{2,1,0:T(8,128)(2,1)} %param.10) | copy-start | bytes 786436
  0.0 13.6 %copy-start.4 = (s32[1,128]{1,0:T(1,128)S(1)}, s32[1,128]{1,0:T(1,128)}, u32[]{:S(2)}) copy-start(s32[1,128]{1,0:T(1,128)} %refs_3_.1) | copy-start | bytes 1540
  0.0 15.1 %copy-start.1 = (bf16[1,128,2048]{2,1,0:T(8,128)(2,1)S(1)}, bf16[1,128,2048]{2,1,0:T(8,128)(2,1)}, u32[]{:S(2)}) copy-start(bf16[1,128,2048]{2,1,0:T(8,128)(2,1)} %param.8) | copy-start | bytes 1572868
  0.0 1.2 %copy-start.5 = (bf16[128,2304]{1,0:T(8,128)(2,1)S(1)}, bf16[128,2304]{1,0:T(8,128)(2,1)}, u32[]{:S(2)}) copy-start(bf16[128,2304]{1,0:T(8,128)(2,1)} %w_ref.1) | copy-start | bytes 1769476
  1.2 10.0 %collective-permute-start.6 = (bf16[128,1152]{1,0:T(8,128)(2,1)S(1)}, bf16[128,1152]{1,0:T(8,128)(2,1)S(1)}, u32[]{:S(2)}, u32[]{:S(2)}) collective-permute-start(bf16[128,1152]{1,0:T(8,128)(2,1)S(1)} %get-tuple-element.44), channel_id=1, source_target_pairs={{0,2},{2,0},{1,3},{3,1},{4,6},{6,4},{5,7},{7,5},{8,10},{10,8},{9,1... | collective-permute-start | bytes 884744 | tf_op jit(solution)/shard_map/ppermute | solution.py:210
  4.2 9.4 %collective-permute-start.2 = (bf16[128,1152]{1,0:T(8,128)(2,1)S(1)}, bf16[128,1152]{1,0:T(8,128)(2,1)S(1)}, u32[]{:S(2)}, u32[]{:S(2)}) collective-permute-start(bf16[128,1152]{1,0:T(8,128)(2,1)S(1)} %get-tuple-element.41.refs_0_), channel_id=1, source_target_pairs={{0,4},{4,12},{12,8},{8,0},{1,5},{5,13},{13,9},{9,1},{2,6},{6,14},{... | collective-permute-start | bytes 884744 | tf_op jit(solution)/shard_map/ppermute | solution.py:210
  5.8 11.5 %collective-permute-start = (bf16[128,1024]{1,0:T(8,128)(2,1)S(1)}, bf16[128,1024]{1,0:T(8,128)(2,1)S(1)}, u32[]{:S(2)}, u32[]{:S(2)}) collective-permute-start(bf16[128,1024]{1,0:T(8,128)(2,1)S(1)} %bitcast.7), channel_id=1, source_target_pairs={{0,16},{16,0},{1,17},{17,1},{2,18},{18,2},{3,19},{19,3},{4,20},{20... | collective-permute-start | bytes 786440 | tf_op jit(solution)/shard_map/ppermute | solution.py:210
  7.3 11.6 %collective-permute-start.1 = (bf16[128,1024]{1,0:T(8,128)(2,1)S(1)}, bf16[128,1024]{1,0:T(8,128)(2,1)S(1)}, u32[]{:S(2)}, u32[]{:S(2)}) collective-permute-start(bf16[128,1024]{1,0:T(8,128)(2,1)S(1)} %bitcast.9), channel_id=1, source_target_pairs={{0,16},{16,0},{1,17},{17,1},{2,18},{18,2},{3,19},{19,3},{4,20},{20... | collective-permute-start | bytes 786440 | tf_op jit(solution)/shard_map/ppermute | solution.py:210
  11.2 11.0 %collective-permute-start.7 = (bf16[128,1152]{1,0:T(8,128)(2,1)S(1)}, bf16[128,1152]{1,0:T(8,128)(2,1)S(1)}, u32[]{:S(2)}, u32[]{:S(2)}) collective-permute-start(bf16[128,1152]{1,0:T(8,128)(2,1)S(1)} %collective-permute-done.6.refs_1_), channel_id=1, source_target_pairs={{0,4},{4,12},{12,8},{8,0},{1,5},{5,13},{13,9},{9,1},{2,6},{6,14},{... | collective-permute-start | bytes 884744 | tf_op jit(solution)/shard_map/ppermute | solution.py:210
  13.6 5.4 %collective-permute-start.3 = (s32[1,128]{1,0:T(1,128)S(1)}, s32[1,128]{1,0:T(1,128)S(1)}, u32[]{:S(2)}, u32[]{:S(2)}) collective-permute-start(s32[1,128]{1,0:T(1,128)S(1)} %copy-done.4), channel_id=1, source_target_pairs={{0,16},{16,0},{1,17},{17,1},{2,18},{18,2},{3,19},{19,3},{4,20},{20... | collective-permute-start | bytes 1544 | tf_op jit(solution)/shard_map/ppermute | solution.py:210
  15.2 13.2 %collective-permute-start.9 = (bf16[128,1152]{1,0:T(8,128)(2,1)S(1)}, bf16[128,1152]{1,0:T(8,128)(2,1)S(1)}, u32[]{:S(2)}, u32[]{:S(2)}) collective-permute-start(bf16[128,1152]{1,0:T(8,128)(2,1)S(1)} %collective-permute-done.2.refs_2_), channel_id=1, source_target_pairs={{0,4},{4,12},{12,8},{8,0},{1,5},{5,13},{13,9},{9,1},{2,6},{6,14},{... | collective-permute-start | bytes 884744 | tf_op jit(solution)/shard_map/ppermute | solution.py:210
  20.1 15.9 %collective-permute-start.4 = (bf16[128,2048]{1,0:T(8,128)(2,1)S(1)}, bf16[128,2048]{1,0:T(8,128)(2,1)S(1)}, u32[]{:S(2)}, u32[]{:S(2)}) collective-permute-start(bf16[128,2048]{1,0:T(8,128)(2,1)S(1)} %attend.1.refs_0_), channel_id=1, source_target_pairs={{0,2},{2,0},{1,3},{3,1},{4,6},{6,4},{5,7},{7,5},{8,10},{10,8},{9,1... | collective-permute-start | bytes 1572872 | tf_op jit(solution)/shard_map/ppermute | solution.py:210
  20.7 14.1 %collective-permute-start.5 = (bf16[128,2048]{1,0:T(8,128)(2,1)S(1)}, bf16[128,2048]{1,0:T(8,128)(2,1)S(1)}, u32[]{:S(2)}, u32[]{:S(2)}) collective-permute-start(bf16[128,2048]{1,0:T(8,128)(2,1)S(1)} %attend.1.refs_0_), channel_id=1, source_target_pairs={{0,16},{16,0},{1,17},{17,1},{2,18},{18,2},{3,19},{19,3},{4,20},{20... | collective-permute-start | bytes 1572872 | tf_op jit(solution)/shard_map/ppermute | solution.py:210
  22.2 12.5 %collective-permute-start.10 = (bf16[128,1152]{1,0:T(8,128)(2,1)S(1)}, bf16[128,1152]{1,0:T(8,128)(2,1)S(1)}, u32[]{:S(2)}, u32[]{:S(2)}) collective-permute-start(bf16[128,1152]{1,0:T(8,128)(2,1)S(1)} %collective-permute-done.7.refs_3_), channel_id=1, source_target_pairs={{0,4},{4,12},{12,8},{8,0},{1,5},{5,13},{13,9},{9,1},{2,6},{6,14},{... | collective-permute-start | bytes 884744 | tf_op jit(solution)/shard_map/ppermute | solution.py:210
  24.9 18.2 %collective-permute-start.8 = (bf16[512,1152]{1,0:T(8,128)(2,1)S(1)}, bf16[512,1152]{1,0:T(8,128)(2,1)S(1)}, u32[]{:S(2)}, u32[]{:S(2)}) collective-permute-start(bf16[512,1152]{1,0:T(8,128)(2,1)S(1)} %stack.2.refs_3_), channel_id=1, source_target_pairs={{0,1},{1,0},{2,3},{3,2},{4,5},{5,4},{6,7},{7,6},{8,9},{9,8},{10,11... | collective-permute-start | bytes 3538952 | tf_op jit(solution)/shard_map/ppermute | solution.py:210
  28.4 11.2 %collective-permute-start.14 = (bf16[128,1152]{1,0:T(8,128)(2,1)S(1)}, bf16[128,1152]{1,0:T(8,128)(2,1)S(1)}, u32[]{:S(2)}, u32[]{:S(2)}) collective-permute-start(bf16[128,1152]{1,0:T(8,128)(2,1)S(1)} %collective-permute-done.9.refs_0_), channel_id=1, source_target_pairs={{0,4},{4,12},{12,8},{8,0},{1,5},{5,13},{13,9},{9,1},{2,6},{6,14},{... | collective-permute-start | bytes 884744 | tf_op jit(solution)/shard_map/ppermute | solution.py:210
  34.8 2.8 %collective-permute-start.11 = (bf16[256,1152]{1,0:T(8,128)(2,1)S(1)}, bf16[256,1152]{1,0:T(8,128)(2,1)S(1)}, u32[]{:S(2)}, u32[]{:S(2)}) collective-permute-start(bf16[256,1152]{1,0:T(8,128)(2,1)S(1)} %stack.3.refs_5_), channel_id=1, source_target_pairs={{0,1},{1,0},{2,3},{3,2},{4,5},{5,4},{6,7},{7,6},{8,9},{9,8},{10,11... | collective-permute-start | bytes 1769480 | tf_op jit(solution)/shard_map/ppermute | solution.py:210
  34.9 8.2 %collective-permute-start.16 = (bf16[128,640]{1,0:T(8,128)(2,1)S(1)}, bf16[128,640]{1,0:T(8,128)(2,1)S(1)}, u32[]{:S(2)}, u32[]{:S(2)}) collective-permute-start(bf16[128,640]{1,0:T(8,128)(2,1)S(1)} %get-tuple-element.56), channel_id=1, source_target_pairs={{0,4},{4,12},{12,8},{8,0},{1,5},{5,13},{13,9},{9,1},{2,6},{6,14},{... | collective-permute-start | bytes 491528 | tf_op jit(solution)/shard_map/ppermute | solution.py:210
  36.0 9.4 %collective-permute-start.13 = (bf16[128,1024]{1,0:T(8,128)(2,1)S(1)}, bf16[128,1024]{1,0:T(8,128)(2,1)S(1)}, u32[]{:S(2)}, u32[]{:S(2)}) collective-permute-start(bf16[128,1024]{1,0:T(8,128)(2,1)S(1)} %halves.3), channel_id=1, source_target_pairs={{0,16},{16,0},{1,17},{17,1},{2,18},{18,2},{3,19},{19,3},{4,20},{20... | collective-permute-start | bytes 786440 | tf_op jit(solution)/shard_map/ppermute | solution.py:210
  37.6 8.1 %collective-permute-start.12 = (bf16[128,1024]{1,0:T(8,128)(2,1)S(1)}, bf16[128,1024]{1,0:T(8,128)(2,1)S(1)}, u32[]{:S(2)}, u32[]{:S(2)}) collective-permute-start(bf16[128,1024]{1,0:T(8,128)(2,1)S(1)} %halves.2), channel_id=1, source_target_pairs={{0,2},{2,0},{1,3},{3,1},{4,6},{6,4},{5,7},{7,5},{8,10},{10,8},{9,1... | collective-permute-start | bytes 786440 | tf_op jit(solution)/shard_map/ppermute | solution.py:210
  39.6 9.4 %collective-permute-start.21 = (bf16[128,512]{1,0:T(8,128)(2,1)S(1)}, bf16[128,512]{1,0:T(8,128)(2,1)S(1)}, u32[]{:S(2)}, u32[]{:S(2)}) collective-permute-start(bf16[128,512]{1,0:T(8,128)(2,1)S(1)} %get-tuple-element.62), channel_id=1, source_target_pairs={{0,4},{4,12},{12,8},{8,0},{1,5},{5,13},{13,9},{9,1},{2,6},{6,14},{... | collective-permute-start | bytes 393224 | tf_op jit(solution)/shard_map/ppermute | solution.py:210
  43.1 2.7 %collective-permute-start.17 = (bf16[128,640]{1,0:T(8,128)(2,1)S(1)}, bf16[128,640]{1,0:T(8,128)(2,1)S(1)}, u32[]{:S(2)}, u32[]{:S(2)}) collective-permute-start(bf16[128,640]{1,0:T(8,128)(2,1)S(1)} %collective-permute-done.16.refs_4_), channel_id=1, source_target_pairs={{0,1},{1,0},{2,3},{3,2},{4,5},{5,4},{6,7},{7,6},{8,9},{9,8},{10,11... | collective-permute-start | bytes 491528 | tf_op jit(solution)/shard_map/ppermute | solution.py:210
  43.1 2.7 %collective-permute-start.15 = (bf16[128,1152]{1,0:T(8,128)(2,1)S(1)}, bf16[128,1152]{1,0:T(8,128)(2,1)S(1)}, u32[]{:S(2)}, u32[]{:S(2)}) collective-permute-start(bf16[128,1152]{1,0:T(8,128)(2,1)S(1)} %collective-permute-done.14.refs_2_), channel_id=1, source_target_pairs={{0,1},{1,0},{2,3},{3,2},{4,5},{5,4},{6,7},{7,6},{8,9},{9,8},{10,11... | collective-permute-start | bytes 884744 | tf_op jit(solution)/shard_map/ppermute | solution.py:210
  46.7 8.0 %collective-permute-start.20 = (bf16[128,640]{1,0:T(8,128)(2,1)S(1)}, bf16[128,640]{1,0:T(8,128)(2,1)S(1)}, u32[]{:S(2)}, u32[]{:S(2)}) collective-permute-start(bf16[128,640]{1,0:T(8,128)(2,1)S(1)} %get-tuple-element.60), channel_id=1, source_target_pairs={{0,18},{2,16},{16,2},{18,0},{1,19},{3,17},{17,3},{19,1},{4,22},{6,... | collective-permute-start | bytes 491528 | tf_op jit(solution)/shard_map/ppermute | solution.py:209
  49.0 1.3 %collective-permute-start.22 = (bf16[128,512]{1,0:T(8,128)(2,1)S(1)}, bf16[128,512]{1,0:T(8,128)(2,1)S(1)}, u32[]{:S(2)}, u32[]{:S(2)}) collective-permute-start(bf16[128,512]{1,0:T(8,128)(2,1)S(1)} %collective-permute-done.21.refs_4_), channel_id=1, source_target_pairs={{0,1},{1,0},{2,3},{3,2},{4,5},{5,4},{6,7},{7,6},{8,9},{9,8},{10,11... | collective-permute-start | bytes 393224 | tf_op jit(solution)/shard_map/ppermute | solution.py:210
  49.0 12.1 %collective-permute-start.18 = (bf16[128,640]{1,0:T(8,128)(2,1)S(1)}, bf16[128,640]{1,0:T(8,128)(2,1)S(1)}, u32[]{:S(2)}, u32[]{:S(2)}) collective-permute-start(bf16[128,640]{1,0:T(8,128)(2,1)S(1)} %get-tuple-element.58), channel_id=1, source_target_pairs={{0,2},{2,0},{1,3},{3,1},{4,6},{6,4},{5,7},{7,5},{8,10},{10,8},{9,1... | collective-permute-start | bytes 491528 | tf_op jit(solution)/shard_map/ppermute | solution.py:210
  49.5 7.4 %copy-start.6 = (f32[4608]{0:T(1024)S(1)}, f32[4608]{0:T(1024)}, u32[]{:S(2)}) copy-start(f32[4608]{0:T(1024)} %param.12) | copy-start | bytes 55300
  49.5 13.1 %copy-start = (bf16[1,128,4608]{2,1,0:T(8,128)(2,1)S(1)}, bf16[1,128,4608]{2,1,0:T(8,128)(2,1)}, u32[]{:S(2)}) copy-start(bf16[1,128,4608]{2,1,0:T(8,128)(2,1)} %param.7) | copy-start | bytes 3538948
  49.5 11.6 %collective-permute-start.19 = (bf16[128,640]{1,0:T(8,128)(2,1)S(1)}, bf16[128,640]{1,0:T(8,128)(2,1)S(1)}, u32[]{:S(2)}, u32[]{:S(2)}) collective-permute-start(bf16[128,640]{1,0:T(8,128)(2,1)S(1)} %get-tuple-element.59), channel_id=1, source_target_pairs={{0,16},{16,0},{1,17},{17,1},{2,18},{18,2},{3,19},{19,3},{4,20},{20... | collective-permute-start | bytes 491528 | tf_op jit(solution)/shard_map/ppermute | solution.py:210
  51.0 9.8 %collective-permute-start.23 = (bf16[128,512]{1,0:T(8,128)(2,1)S(1)}, bf16[128,512]{1,0:T(8,128)(2,1)S(1)}, u32[]{:S(2)}, u32[]{:S(2)}) collective-permute-start(bf16[128,512]{1,0:T(8,128)(2,1)S(1)} %get-tuple-element.64), channel_id=1, source_target_pairs={{0,2},{2,0},{1,3},{3,1},{4,6},{6,4},{5,7},{7,5},{8,10},{10,8},{9,1... | collective-permute-start | bytes 393224 | tf_op jit(solution)/shard_map/ppermute | solution.py:210
  52.5 8.5 %collective-permute-start.24 = (bf16[128,512]{1,0:T(8,128)(2,1)S(1)}, bf16[128,512]{1,0:T(8,128)(2,1)S(1)}, u32[]{:S(2)}, u32[]{:S(2)}) collective-permute-start(bf16[128,512]{1,0:T(8,128)(2,1)S(1)} %get-tuple-element.65), channel_id=1, source_target_pairs={{0,16},{16,0},{1,17},{17,1},{2,18},{18,2},{3,19},{19,3},{4,20},{20... | collective-permute-start | bytes 393224 | tf_op jit(solution)/shard_map/ppermute | solution.py:210
  54.7 7.9 %collective-permute-start.25 = (bf16[128,512]{1,0:T(8,128)(2,1)S(1)}, bf16[128,512]{1,0:T(8,128)(2,1)S(1)}, u32[]{:S(2)}, u32[]{:S(2)}) collective-permute-start(bf16[128,512]{1,0:T(8,128)(2,1)S(1)} %get-tuple-element.68), channel_id=1, source_target_pairs={{0,18},{2,16},{16,2},{18,0},{1,19},{3,17},{17,3},{19,1},{4,22},{6,... | collective-permute-start | bytes 393224 | tf_op jit(solution)/shard_map/ppermute | solution.py:209

commit v6 on v5

--- a/solution.py
+++ b/solution.py
@@ -21,9 +21,8 @@
 PACKS = (('a0', 'B0', 'a1', 'B1'), ('a2', 'B2'))
 WHOLE_STEPS = {'a': 3, 'B': 2}
 TIES = {'rd1': ('rd0',), 'ca3': ('ck1',), 'pos': ('a1',), 'hy': ('k1',), 'B3_0': ('y1l',)}
-COSTS = {'splitB': 9000, 'hy': 1500, 'proj0': 1500, 'pk0': 9000, 'cut': 3000, 'early': 6000, 'att': 3000, 'pk1': 6000, 'hx': 12000}
+COSTS = {'splitB': 9000, 'hy': 1500, 'proj0': 1500, 'pk0': 9000, 'cut': 3000, 'early': 6000, 'att': 3000, 'pk1': 6000, 'hx': 9000}
 PER_CYCLE = 524288
-FIRST = ()
 ACTS = 1
 VMEM_LIMIT = 20 * 2**20
 VMEM = pl.BlockSpec(memory_space=pltpu.VMEM)
@@ -341,7 +340,6 @@
         return value
 
     pending = list(kernels) + list(moves)
-    pending.sort(key=lambda name: FIRST.index(name) if name in FIRST else len(FIRST))
     while pending:
         for name in pending:
             sources, results = (moves[name][:1], (name,)) if name in moves else kernels[name][1:]

time: 64.2 us -> 64.2 us (level)
  no operation moved by 1% of the time
where the time goes in v6:
time: 64.2 us; the launch traced here: 64.1 us
  starting transfers between devices  34.2 us (53%)
  waiting for transfers between devices  22.3 us (35%)
  Pallas kernels  6.32 us (10%)
  local copies, waits for them, and re-layouts  1.18 us (2%)
    ppermute x24, starting transfers between devices, over(): return lax.ppermute(value, axis, along if axis == 'z' else swap)  29.6 us
    ppermute x24, waiting for transfers between devices, over(): return lax.ppermute(value, axis, along if axis == 'z' else swap)  19.8 us
    pallas_call x11, Pallas kernels, shards(): out = kernels[name][0](first, *(held[k] for k in sources[1:]))  4.89 us
    ppermute x2, starting transfers between devices, over(): return lax.ppermute(value, ('ctx', 'x'), [(i, 3 - i) for i in range(4)])  4.51 us
    ppermute x2, waiting for transfers between devices, over(): return lax.ppermute(value, ('ctx', 'x'), [(i, 3 - i) for i in range(4)])  2.48 us
    pallas_call x1, Pallas kernels, shards(): pl.pallas_call(functools.partial(finish, chunks), out_shape=bf16(tokens,...  1.43 us
  transfers between devices with their start and end apart: 26, of which 14 were waited for; matrix products, arithmetic and copies ran while one was open for 0% of the time, Pallas kernels for 8%

profile of v6, /device:TPU:0, one launch (start us, length us, event | category | flops | bytes accessed | tf_op | source)
XLA Modules:
  0.0 64.1 jit_solution(6708787789111710925)
XLA Ops:
  0.0 1.1 %copy-done.5 = bf16[128,2304]{1,0:T(8,128)(2,1)S(1)} copy-done((bf16[128,2304]{1,0:T(8,128)(2,1)S(1)}, bf16[128,2304]{1,0:T(8,128)(2,1)}, u32[]{:S(2)}) %copy-start.5) | copy-done | bytes 589848
  1.2 3.0 %collective-permute-start.6 = (bf16[128,1152]{1,0:T(8,128)(2,1)S(1)}, bf16[128,1152]{1,0:T(8,128)(2,1)S(1)}, u32[]{:S(2)}, u32[]{:S(2)}) collective-permute-start(bf16[128,1152]{1,0:T(8,128)(2,1)S(1)} %get-tuple-element.44), channel_id=1, source_target_pairs={{0,2},{2,0},{1,3},{3,1},{4,6},{6,4},{5,7},{7,5},{8,10},{10,8},{9,1... | collective-permute-start | bytes 884744 | tf_op jit(solution)/shard_map/ppermute | solution.py:209
  4.2 1.6 %collective-permute-start.2 = (bf16[128,1152]{1,0:T(8,128)(2,1)S(1)}, bf16[128,1152]{1,0:T(8,128)(2,1)S(1)}, u32[]{:S(2)}, u32[]{:S(2)}) collective-permute-start(bf16[128,1152]{1,0:T(8,128)(2,1)S(1)} %get-tuple-element.41.refs_0_), channel_id=1, source_target_pairs={{0,4},{4,12},{12,8},{8,0},{1,5},{5,13},{13,9},{9,1},{2,6},{6,14},{... | collective-permute-start | bytes 884744 | tf_op jit(solution)/shard_map/ppermute | solution.py:209
  5.8 1.5 %collective-permute-start = (bf16[128,1024]{1,0:T(8,128)(2,1)S(1)}, bf16[128,1024]{1,0:T(8,128)(2,1)S(1)}, u32[]{:S(2)}, u32[]{:S(2)}) collective-permute-start(bf16[128,1024]{1,0:T(8,128)(2,1)S(1)} %bitcast.7), channel_id=1, source_target_pairs={{0,16},{16,0},{1,17},{17,1},{2,18},{18,2},{3,19},{19,3},{4,20},{20... | collective-permute-start | bytes 786440 | tf_op jit(solution)/shard_map/ppermute | solution.py:209
  7.3 0.5 collective-permute-start.1
  7.8 3.4 %collective-permute-done.6.refs_1_ = bf16[128,1152]{1,0:T(8,128)(2,1)S(1)} collective-permute-done((bf16[128,1152]{1,0:T(8,128)(2,1)S(1)}, bf16[128,1152]{1,0:T(8,128)(2,1)S(1)}, u32[]{:S(2)}, u32[]{:S(2)}) %collective-permute-start.6) | collective-permute-done | bytes 294944 | tf_op jit(solution)/shard_map/ppermute | solution.py:209
  11.2 1.8 %collective-permute-start.7 = (bf16[128,1152]{1,0:T(8,128)(2,1)S(1)}, bf16[128,1152]{1,0:T(8,128)(2,1)S(1)}, u32[]{:S(2)}, u32[]{:S(2)}) collective-permute-start(bf16[128,1152]{1,0:T(8,128)(2,1)S(1)} %collective-permute-done.6.refs_1_), channel_id=1, source_target_pairs={{0,4},{4,12},{12,8},{8,0},{1,5},{5,13},{13,9},{9,1},{2,6},{6,14},{... | collective-permute-start | bytes 884744 | tf_op jit(solution)/shard_map/ppermute | solution.py:209
  13.1 0.5 collective-permute-done.2.refs_2_
  13.6 1.5 %collective-permute-start.3 = (s32[1,128]{1,0:T(1,128)S(1)}, s32[1,128]{1,0:T(1,128)S(1)}, u32[]{:S(2)}, u32[]{:S(2)}) collective-permute-start(s32[1,128]{1,0:T(1,128)S(1)} %copy-done.4), channel_id=1, source_target_pairs={{0,16},{16,0},{1,17},{17,1},{2,18},{18,2},{3,19},{19,3},{4,20},{20... | collective-permute-start | bytes 1544 | tf_op jit(solution)/shard_map/ppermute | solution.py:209
  15.1 0.1 stage.1
  15.2 2.1 %collective-permute-start.9 = (bf16[128,1152]{1,0:T(8,128)(2,1)S(1)}, bf16[128,1152]{1,0:T(8,128)(2,1)S(1)}, u32[]{:S(2)}, u32[]{:S(2)}) collective-permute-start(bf16[128,1152]{1,0:T(8,128)(2,1)S(1)} %collective-permute-done.2.refs_2_), channel_id=1, source_target_pairs={{0,4},{4,12},{12,8},{8,0},{1,5},{5,13},{13,9},{9,1},{2,6},{6,14},{... | collective-permute-start | bytes 884744 | tf_op jit(solution)/shard_map/ppermute | solution.py:209
  17.3 0.0 collective-permute-done.k_far
  17.3 1.6 %collective-permute-done.1.v_far = bf16[128,1024]{1,0:T(8,128)(2,1)S(1)} collective-permute-done((bf16[128,1024]{1,0:T(8,128)(2,1)S(1)}, bf16[128,1024]{1,0:T(8,128)(2,1)S(1)}, u32[]{:S(2)}, u32[]{:S(2)}) %collective-permute-start.1) | collective-permute-done | bytes 262176 | tf_op jit(solution)/shard_map/ppermute | solution.py:209
  18.9 0.1 collective-permute-done.3.pos_far
  19.0 1.1 %attend.1.refs_0_ = bf16[128,2048]{1,0:T(8,128)(2,1)S(1)} custom-call(bf16[128,2048]{1,0:T(8,128)(2,1)S(1)} %get-tuple-element.37.q_ref, bf16[128,1024]{1,0:T(8,128)(2,1)S(1)} %get-tuple-element.38.k_own, bf16[128,1024]{1,0:T(8,128)(2,1)S(1)} %collective-permute-done.k_far, bf16[128,1024]{1,0:T(8,128)(2,1)S(1)} %get-tuple-element.39.v_own, ...), custom_call_target="tpu_custom_call" | custom-call | flops 1572864000 | tf_op jit(solution)/shard_map/attend/pallas_call | solution.py:354
  20.1 0.6 collective-permute-start.4
  20.7 1.5 %collective-permute-start.5 = (bf16[128,2048]{1,0:T(8,128)(2,1)S(1)}, bf16[128,2048]{1,0:T(8,128)(2,1)S(1)}, u32[]{:S(2)}, u32[]{:S(2)}) collective-permute-start(bf16[128,2048]{1,0:T(8,128)(2,1)S(1)} %attend.1.refs_0_), channel_id=1, source_target_pairs={{0,16},{16,0},{1,17},{17,1},{2,18},{18,2},{3,19},{19,3},{4,20},{20... | collective-permute-start | bytes 1572872 | tf_op jit(solution)/shard_map/ppermute | solution.py:209
  22.2 0.0 collective-permute-done.7.refs_3_
  22.2 2.6 %collective-permute-start.10 = (bf16[128,1152]{1,0:T(8,128)(2,1)S(1)}, bf16[128,1152]{1,0:T(8,128)(2,1)S(1)}, u32[]{:S(2)}, u32[]{:S(2)}) collective-permute-start(bf16[128,1152]{1,0:T(8,128)(2,1)S(1)} %collective-permute-done.7.refs_3_), channel_id=1, source_target_pairs={{0,4},{4,12},{12,8},{8,0},{1,5},{5,13},{13,9},{9,1},{2,6},{6,14},{... | collective-permute-start | bytes 884744 | tf_op jit(solution)/shard_map/ppermute | solution.py:209
  24.8 0.1 stack.2.refs_3_
  24.9 0.1 collective-permute-start.8
  25.0 3.4 %collective-permute-done.9.refs_0_ = bf16[128,1152]{1,0:T(8,128)(2,1)S(1)} collective-permute-done((bf16[128,1152]{1,0:T(8,128)(2,1)S(1)}, bf16[128,1152]{1,0:T(8,128)(2,1)S(1)}, u32[]{:S(2)}, u32[]{:S(2)}) %collective-permute-start.9) | collective-permute-done | bytes 294944 | tf_op jit(solution)/shard_map/ppermute | solution.py:209
  28.4 1.0 %collective-permute-start.14 = (bf16[128,1152]{1,0:T(8,128)(2,1)S(1)}, bf16[128,1152]{1,0:T(8,128)(2,1)S(1)}, u32[]{:S(2)}, u32[]{:S(2)}) collective-permute-start(bf16[128,1152]{1,0:T(8,128)(2,1)S(1)} %collective-permute-done.9.refs_0_), channel_id=1, source_target_pairs={{0,4},{4,12},{12,8},{8,0},{1,5},{5,13},{13,9},{9,1},{2,6},{6,14},{... | collective-permute-start | bytes 884744 | tf_op jit(solution)/shard_map/ppermute | solution.py:209
  29.4 5.3 %collective-permute-done.10.refs_1_.ref = bf16[128,1152]{1,0:T(8,128)(2,1)S(1)} collective-permute-done((bf16[128,1152]{1,0:T(8,128)(2,1)S(1)}, bf16[128,1152]{1,0:T(8,128)(2,1)S(1)}, u32[]{:S(2)}, u32[]{:S(2)}) %collective-permute-start.10) | collective-permute-done | bytes 294944 | tf_op jit(solution)/shard_map/ppermute | solution.py:209
  34.8 0.1 collective-permute-start.11
  34.9 1.1 %collective-permute-start.16 = (bf16[128,640]{1,0:T(8,128)(2,1)S(1)}, bf16[128,640]{1,0:T(8,128)(2,1)S(1)}, u32[]{:S(2)}, u32[]{:S(2)}) collective-permute-start(bf16[128,640]{1,0:T(8,128)(2,1)S(1)} %get-tuple-element.56), channel_id=1, source_target_pairs={{0,4},{4,12},{12,8},{8,0},{1,5},{5,13},{13,9},{9,1},{2,6},{6,14},{... | collective-permute-start | bytes 491528 | tf_op jit(solution)/shard_map/ppermute | solution.py:209
  36.0 1.6 %collective-permute-start.13 = (bf16[128,1024]{1,0:T(8,128)(2,1)S(1)}, bf16[128,1024]{1,0:T(8,128)(2,1)S(1)}, u32[]{:S(2)}, u32[]{:S(2)}) collective-permute-start(bf16[128,1024]{1,0:T(8,128)(2,1)S(1)} %halves.3), channel_id=1, source_target_pairs={{0,16},{16,0},{1,17},{17,1},{2,18},{18,2},{3,19},{19,3},{4,20},{20... | collective-permute-start | bytes 786440 | tf_op jit(solution)/shard_map/ppermute | solution.py:209
  37.6 1.5 %collective-permute-start.12 = (bf16[128,1024]{1,0:T(8,128)(2,1)S(1)}, bf16[128,1024]{1,0:T(8,128)(2,1)S(1)}, u32[]{:S(2)}, u32[]{:S(2)}) collective-permute-start(bf16[128,1024]{1,0:T(8,128)(2,1)S(1)} %halves.2), channel_id=1, source_target_pairs={{0,2},{2,0},{1,3},{3,1},{4,6},{6,4},{5,7},{7,5},{8,10},{10,8},{9,1... | collective-permute-start | bytes 786440 | tf_op jit(solution)/shard_map/ppermute | solution.py:209
  39.1 0.5 collective-permute-done.14.refs_2_
  39.6 2.9 %collective-permute-start.21 = (bf16[128,512]{1,0:T(8,128)(2,1)S(1)}, bf16[128,512]{1,0:T(8,128)(2,1)S(1)}, u32[]{:S(2)}, u32[]{:S(2)}) collective-permute-start(bf16[128,512]{1,0:T(8,128)(2,1)S(1)} %get-tuple-element.62), channel_id=1, source_target_pairs={{0,4},{4,12},{12,8},{8,0},{1,5},{5,13},{13,9},{9,1},{2,6},{6,14},{... | collective-permute-start | bytes 393224 | tf_op jit(solution)/shard_map/ppermute | solution.py:209
  42.5 0.6 collective-permute-done.16.refs_4_
  43.1 0.5 collective-permute-start.15
  43.6 1.8 %early.1 = (f32[384,1152]{1,0:T(8,128)S(1)}, bf16[384,2048]{1,0:T(8,128)(2,1)S(1)}, bf16[1536,1152]{1,0:T(8,128)(2,1)S(1)}) custom-call(bf16[128,2048]{1,0:T(8,128)(2,1)S(1)} %attend.1.refs_0_, bf16[128,2048]{1,0:T(8,128)(2,1)S(1)} %collective-permute-done.4.refs_1_.ref, bf16[128,2048]{1,0:T(8,128)(2,1)S(1)} %collective-permute-done.5.refs_2_.ref, ...), custom_call_target="tpu_custom_call" | custom-call | flops 3145728000 | tf_op jit(solution)/shard_map/early/pallas_call | solution.py:354
  45.4 0.3 collective-permute-done.12.refs_0_
  45.8 1.0 %project.2 = (bf16[128,640]{1,0:T(8,128)(2,1)S(1)}, bf16[128,640]{1,0:T(8,128)(2,1)S(1)}, bf16[128,640]{1,0:T(8,128)(2,1)S(1)}, bf16[128,640]{1,0:T(8,128)(2,1)S(1)}) custom-call(f32[384,1152]{1,0:T(8,128)S(1)} %get-tuple-element.47.acc, bf16[384,2048]{1,0:T(8,128)(2,1)S(1)} %get-tuple-element.48.a_all, bf16[1536,1152]{1,0:T(8,128)(2,1)S(1)} %get-tuple-element.49.w_all, ...), custom_call_target="tpu_custom_call" | custom-call | flops 786432000 | tf_op jit(solution)/shard_map/project/pallas_call | solution.py:354
  46.7 2.3 %collective-permute-start.20 = (bf16[128,640]{1,0:T(8,128)(2,1)S(1)}, bf16[128,640]{1,0:T(8,128)(2,1)S(1)}, u32[]{:S(2)}, u32[]{:S(2)}) collective-permute-start(bf16[128,640]{1,0:T(8,128)(2,1)S(1)} %get-tuple-element.60), channel_id=1, source_target_pairs={{0,18},{2,16},{16,2},{18,0},{1,19},{3,17},{17,3},{19,1},{4,22},{6,... | collective-permute-start | bytes 491528 | tf_op jit(solution)/shard_map/ppermute | solution.py:208
  49.0 0.5 collective-permute-start.18
  49.5 0.8 %collective-permute-start.19 = (bf16[128,640]{1,0:T(8,128)(2,1)S(1)}, bf16[128,640]{1,0:T(8,128)(2,1)S(1)}, u32[]{:S(2)}, u32[]{:S(2)}) collective-permute-start(bf16[128,640]{1,0:T(8,128)(2,1)S(1)} %get-tuple-element.59), channel_id=1, source_target_pairs={{0,16},{16,0},{1,17},{17,1},{2,18},{18,2},{3,19},{19,3},{4,20},{20... | collective-permute-start | bytes 491528 | tf_op jit(solution)/shard_map/ppermute | solution.py:209
  50.3 0.1 collective-permute-done.22.refs_5_
  50.3 0.7 %project.3 = (bf16[128,512]{1,0:T(8,128)(2,1)S(1)}, bf16[128,512]{1,0:T(8,128)(2,1)S(1)}, bf16[128,512]{1,0:T(8,128)(2,1)S(1)}, bf16[128,512]{1,0:T(8,128)(2,1)S(1)}) custom-call(f32[384,1152]{1,0:T(8,128)S(1)} %get-tuple-element.47.acc, bf16[384,2048]{1,0:T(8,128)(2,1)S(1)} %get-tuple-element.48.a_all, bf16[1536,1152]{1,0:T(8,128)(2,1)S(1)} %get-tuple-element.49.w_all, ...), custom_call_target="tpu_custom_call" | custom-call | flops 1 | tf_op jit(solution)/shard_map/project/pallas_call | solution.py:354
  51.0 1.5 %collective-permute-start.23 = (bf16[128,512]{1,0:T(8,128)(2,1)S(1)}, bf16[128,512]{1,0:T(8,128)(2,1)S(1)}, u32[]{:S(2)}, u32[]{:S(2)}) collective-permute-start(bf16[128,512]{1,0:T(8,128)(2,1)S(1)} %get-tuple-element.64), channel_id=1, source_target_pairs={{0,2},{2,0},{1,3},{3,1},{4,6},{6,4},{5,7},{7,5},{8,10},{10,8},{9,1... | collective-permute-start | bytes 393224 | tf_op jit(solution)/shard_map/ppermute | solution.py:209
  52.5 1.3 %collective-permute-start.24 = (bf16[128,512]{1,0:T(8,128)(2,1)S(1)}, bf16[128,512]{1,0:T(8,128)(2,1)S(1)}, u32[]{:S(2)}, u32[]{:S(2)}) collective-permute-start(bf16[128,512]{1,0:T(8,128)(2,1)S(1)} %get-tuple-element.65), channel_id=1, source_target_pairs={{0,16},{16,0},{1,17},{17,1},{2,18},{18,2},{3,19},{19,3},{4,20},{20... | collective-permute-start | bytes 393224 | tf_op jit(solution)/shard_map/ppermute | solution.py:209
  53.8 0.9 %collective-permute-done.20.refs_3_ = bf16[128,640]{1,0:T(8,128)(2,1)S(1)} collective-permute-done((bf16[128,640]{1,0:T(8,128)(2,1)S(1)}, bf16[128,640]{1,0:T(8,128)(2,1)S(1)}, u32[]{:S(2)}, u32[]{:S(2)}) %collective-permute-start.20) | collective-permute-done | bytes 163872 | tf_op jit(solution)/shard_map/ppermute | solution.py:208
  54.7 2.2 %collective-permute-start.25 = (bf16[128,512]{1,0:T(8,128)(2,1)S(1)}, bf16[128,512]{1,0:T(8,128)(2,1)S(1)}, u32[]{:S(2)}, u32[]{:S(2)}) collective-permute-start(bf16[128,512]{1,0:T(8,128)(2,1)S(1)} %get-tuple-element.68), channel_id=1, source_target_pairs={{0,18},{2,16},{16,2},{18,0},{1,19},{3,17},{17,3},{19,1},{4,22},{6,... | collective-permute-start | bytes 393224 | tf_op jit(solution)/shard_map/ppermute | solution.py:208
  57.0 3.9 %collective-permute-done.23.refs_5_ = bf16[128,512]{1,0:T(8,128)(2,1)S(1)} collective-permute-done((bf16[128,512]{1,0:T(8,128)(2,1)S(1)}, bf16[128,512]{1,0:T(8,128)(2,1)S(1)}, u32[]{:S(2)}, u32[]{:S(2)}) %collective-permute-start.23) | collective-permute-done | bytes 131104 | tf_op jit(solution)/shard_map/ppermute | solution.py:209
  60.9 0.2 collective-permute-done.24.refs_6_
  61.1 1.6 %collective-permute-done.25.refs_7_ = bf16[128,512]{1,0:T(8,128)(2,1)S(1)} collective-permute-done((bf16[128,512]{1,0:T(8,128)(2,1)S(1)}, bf16[128,512]{1,0:T(8,128)(2,1)S(1)}, u32[]{:S(2)}, u32[]{:S(2)}) %collective-permute-start.25) | collective-permute-done | bytes 131104 | tf_op jit(solution)/shard_map/ppermute | solution.py:208
  62.7 1.4 %finish.1 = bf16[128,4608]{1,0:T(8,128)(2,1)} custom-call(bf16[128,4608]{1,0:T(8,128)(2,1)S(1)} %bitcast.5, f32[1,4608]{1,0:T(1,128)S(1)} %reshape.3.gain_ref, bf16[128,640]{1,0:T(8,128)(2,1)S(1)} %get-tuple-element.57.refs_0_, bf16[128,640]{1,0:T(8,128)(2,1)S(1)} %collective-permute-done.18.refs_1_, bf16[128,640]{1,0:T(8,128)(2,1)S(1)} %collective-permute-done.19.refs_2_, ...), custom_call_target="tpu_custom_call" | custom-call | flops 1 | tf_op jit(solution)/shard_map/finish/pallas_call | solution.py:359
  (31 shorter events, 0.2 us)
Async XLA Ops:
  0.0 5.8 %copy-start.2 = (bf16[1,128,1024]{2,1,0:T(8,128)(2,1)S(1)}, bf16[1,128,1024]{2,1,0:T(8,128)(2,1)}, u32[]{:S(2)}) copy-start(bf16[1,128,1024]{2,1,0:T(8,128)(2,1)} %param.9) | copy-start | bytes 786436
  0.0 7.3 %copy-start.3 = (bf16[1,128,1024]{2,1,0:T(8,128)(2,1)S(1)}, bf16[1,128,1024]{2,1,0:T(8,128)(2,1)}, u32[]{:S(2)}) copy-start(bf16[1,128,1024]{2,1,0:T(8,128)(2,1)} %param.10) | copy-start | bytes 786436
  0.0 13.6 %copy-start.4 = (s32[1,128]{1,0:T(1,128)S(1)}, s32[1,128]{1,0:T(1,128)}, u32[]{:S(2)}) copy-start(s32[1,128]{1,0:T(1,128)} %refs_3_.1) | copy-start | bytes 1540
  0.0 15.1 %copy-start.1 = (bf16[1,128,2048]{2,1,0:T(8,128)(2,1)S(1)}, bf16[1,128,2048]{2,1,0:T(8,128)(2,1)}, u32[]{:S(2)}) copy-start(bf16[1,128,2048]{2,1,0:T(8,128)(2,1)} %param.8) | copy-start | bytes 1572868
  0.0 1.2 %copy-start.5 = (bf16[128,2304]{1,0:T(8,128)(2,1)S(1)}, bf16[128,2304]{1,0:T(8,128)(2,1)}, u32[]{:S(2)}) copy-start(bf16[128,2304]{1,0:T(8,128)(2,1)} %w_ref.1) | copy-start | bytes 1769476
  1.2 10.0 %collective-permute-start.6 = (bf16[128,1152]{1,0:T(8,128)(2,1)S(1)}, bf16[128,1152]{1,0:T(8,128)(2,1)S(1)}, u32[]{:S(2)}, u32[]{:S(2)}) collective-permute-start(bf16[128,1152]{1,0:T(8,128)(2,1)S(1)} %get-tuple-element.44), channel_id=1, source_target_pairs={{0,2},{2,0},{1,3},{3,1},{4,6},{6,4},{5,7},{7,5},{8,10},{10,8},{9,1... | collective-permute-start | bytes 884744 | tf_op jit(solution)/shard_map/ppermute | solution.py:209
  4.2 9.4 %collective-permute-start.2 = (bf16[128,1152]{1,0:T(8,128)(2,1)S(1)}, bf16[128,1152]{1,0:T(8,128)(2,1)S(1)}, u32[]{:S(2)}, u32[]{:S(2)}) collective-permute-start(bf16[128,1152]{1,0:T(8,128)(2,1)S(1)} %get-tuple-element.41.refs_0_), channel_id=1, source_target_pairs={{0,4},{4,12},{12,8},{8,0},{1,5},{5,13},{13,9},{9,1},{2,6},{6,14},{... | collective-permute-start | bytes 884744 | tf_op jit(solution)/shard_map/ppermute | solution.py:209
  5.8 11.5 %collective-permute-start = (bf16[128,1024]{1,0:T(8,128)(2,1)S(1)}, bf16[128,1024]{1,0:T(8,128)(2,1)S(1)}, u32[]{:S(2)}, u32[]{:S(2)}) collective-permute-start(bf16[128,1024]{1,0:T(8,128)(2,1)S(1)} %bitcast.7), channel_id=1, source_target_pairs={{0,16},{16,0},{1,17},{17,1},{2,18},{18,2},{3,19},{19,3},{4,20},{20... | collective-permute-start | bytes 786440 | tf_op jit(solution)/shard_map/ppermute | solution.py:209
  7.3 11.6 %collective-permute-start.1 = (bf16[128,1024]{1,0:T(8,128)(2,1)S(1)}, bf16[128,1024]{1,0:T(8,128)(2,1)S(1)}, u32[]{:S(2)}, u32[]{:S(2)}) collective-permute-start(bf16[128,1024]{1,0:T(8,128)(2,1)S(1)} %bitcast.9), channel_id=1, source_target_pairs={{0,16},{16,0},{1,17},{17,1},{2,18},{18,2},{3,19},{19,3},{4,20},{20... | collective-permute-start | bytes 786440 | tf_op jit(solution)/shard_map/ppermute | solution.py:209
  11.2 11.0 %collective-permute-start.7 = (bf16[128,1152]{1,0:T(8,128)(2,1)S(1)}, bf16[128,1152]{1,0:T(8,128)(2,1)S(1)}, u32[]{:S(2)}, u32[]{:S(2)}) collective-permute-start(bf16[128,1152]{1,0:T(8,128)(2,1)S(1)} %collective-permute-done.6.refs_1_), channel_id=1, source_target_pairs={{0,4},{4,12},{12,8},{8,0},{1,5},{5,13},{13,9},{9,1},{2,6},{6,14},{... | collective-permute-start | bytes 884744 | tf_op jit(solution)/shard_map/ppermute | solution.py:209
  13.6 5.4 %collective-permute-start.3 = (s32[1,128]{1,0:T(1,128)S(1)}, s32[1,128]{1,0:T(1,128)S(1)}, u32[]{:S(2)}, u32[]{:S(2)}) collective-permute-start(s32[1,128]{1,0:T(1,128)S(1)} %copy-done.4), channel_id=1, source_target_pairs={{0,16},{16,0},{1,17},{17,1},{2,18},{18,2},{3,19},{19,3},{4,20},{20... | collective-permute-start | bytes 1544 | tf_op jit(solution)/shard_map/ppermute | solution.py:209
  15.2 13.2 %collective-permute-start.9 = (bf16[128,1152]{1,0:T(8,128)(2,1)S(1)}, bf16[128,1152]{1,0:T(8,128)(2,1)S(1)}, u32[]{:S(2)}, u32[]{:S(2)}) collective-permute-start(bf16[128,1152]{1,0:T(8,128)(2,1)S(1)} %collective-permute-done.2.refs_2_), channel_id=1, source_target_pairs={{0,4},{4,12},{12,8},{8,0},{1,5},{5,13},{13,9},{9,1},{2,6},{6,14},{... | collective-permute-start | bytes 884744 | tf_op jit(solution)/shard_map/ppermute | solution.py:209
  20.1 15.9 %collective-permute-start.4 = (bf16[128,2048]{1,0:T(8,128)(2,1)S(1)}, bf16[128,2048]{1,0:T(8,128)(2,1)S(1)}, u32[]{:S(2)}, u32[]{:S(2)}) collective-permute-start(bf16[128,2048]{1,0:T(8,128)(2,1)S(1)} %attend.1.refs_0_), channel_id=1, source_target_pairs={{0,2},{2,0},{1,3},{3,1},{4,6},{6,4},{5,7},{7,5},{8,10},{10,8},{9,1... | collective-permute-start | bytes 1572872 | tf_op jit(solution)/shard_map/ppermute | solution.py:209
  20.7 14.2 %collective-permute-start.5 = (bf16[128,2048]{1,0:T(8,128)(2,1)S(1)}, bf16[128,2048]{1,0:T(8,128)(2,1)S(1)}, u32[]{:S(2)}, u32[]{:S(2)}) collective-permute-start(bf16[128,2048]{1,0:T(8,128)(2,1)S(1)} %attend.1.refs_0_), channel_id=1, source_target_pairs={{0,16},{16,0},{1,17},{17,1},{2,18},{18,2},{3,19},{19,3},{4,20},{20... | collective-permute-start | bytes 1572872 | tf_op jit(solution)/shard_map/ppermute | solution.py:209
  22.2 12.5 %collective-permute-start.10 = (bf16[128,1152]{1,0:T(8,128)(2,1)S(1)}, bf16[128,1152]{1,0:T(8,128)(2,1)S(1)}, u32[]{:S(2)}, u32[]{:S(2)}) collective-permute-start(bf16[128,1152]{1,0:T(8,128)(2,1)S(1)} %collective-permute-done.7.refs_3_), channel_id=1, source_target_pairs={{0,4},{4,12},{12,8},{8,0},{1,5},{5,13},{13,9},{9,1},{2,6},{6,14},{... | collective-permute-start | bytes 884744 | tf_op jit(solution)/shard_map/ppermute | solution.py:209
  24.9 18.2 %collective-permute-start.8 = (bf16[512,1152]{1,0:T(8,128)(2,1)S(1)}, bf16[512,1152]{1,0:T(8,128)(2,1)S(1)}, u32[]{:S(2)}, u32[]{:S(2)}) collective-permute-start(bf16[512,1152]{1,0:T(8,128)(2,1)S(1)} %stack.2.refs_3_), channel_id=1, source_target_pairs={{0,1},{1,0},{2,3},{3,2},{4,5},{5,4},{6,7},{7,6},{8,9},{9,8},{10,11... | collective-permute-start | bytes 3538952 | tf_op jit(solution)/shard_map/ppermute | solution.py:209
  28.4 11.2 %collective-permute-start.14 = (bf16[128,1152]{1,0:T(8,128)(2,1)S(1)}, bf16[128,1152]{1,0:T(8,128)(2,1)S(1)}, u32[]{:S(2)}, u32[]{:S(2)}) collective-permute-start(bf16[128,1152]{1,0:T(8,128)(2,1)S(1)} %collective-permute-done.9.refs_0_), channel_id=1, source_target_pairs={{0,4},{4,12},{12,8},{8,0},{1,5},{5,13},{13,9},{9,1},{2,6},{6,14},{... | collective-permute-start | bytes 884744 | tf_op jit(solution)/shard_map/ppermute | solution.py:209
  34.8 2.8 %collective-permute-start.11 = (bf16[256,1152]{1,0:T(8,128)(2,1)S(1)}, bf16[256,1152]{1,0:T(8,128)(2,1)S(1)}, u32[]{:S(2)}, u32[]{:S(2)}) collective-permute-start(bf16[256,1152]{1,0:T(8,128)(2,1)S(1)} %stack.3.refs_5_), channel_id=1, source_target_pairs={{0,1},{1,0},{2,3},{3,2},{4,5},{5,4},{6,7},{7,6},{8,9},{9,8},{10,11... | collective-permute-start | bytes 1769480 | tf_op jit(solution)/shard_map/ppermute | solution.py:209
  34.9 8.2 %collective-permute-start.16 = (bf16[128,640]{1,0:T(8,128)(2,1)S(1)}, bf16[128,640]{1,0:T(8,128)(2,1)S(1)}, u32[]{:S(2)}, u32[]{:S(2)}) collective-permute-start(bf16[128,640]{1,0:T(8,128)(2,1)S(1)} %get-tuple-element.56), channel_id=1, source_target_pairs={{0,4},{4,12},{12,8},{8,0},{1,5},{5,13},{13,9},{9,1},{2,6},{6,14},{... | collective-permute-start | bytes 491528 | tf_op jit(solution)/shard_map/ppermute | solution.py:209
  36.0 9.4 %collective-permute-start.13 = (bf16[128,1024]{1,0:T(8,128)(2,1)S(1)}, bf16[128,1024]{1,0:T(8,128)(2,1)S(1)}, u32[]{:S(2)}, u32[]{:S(2)}) collective-permute-start(bf16[128,1024]{1,0:T(8,128)(2,1)S(1)} %halves.3), channel_id=1, source_target_pairs={{0,16},{16,0},{1,17},{17,1},{2,18},{18,2},{3,19},{19,3},{4,20},{20... | collective-permute-start | bytes 786440 | tf_op jit(solution)/shard_map/ppermute | solution.py:209
  37.6 8.1 %collective-permute-start.12 = (bf16[128,1024]{1,0:T(8,128)(2,1)S(1)}, bf16[128,1024]{1,0:T(8,128)(2,1)S(1)}, u32[]{:S(2)}, u32[]{:S(2)}) collective-permute-start(bf16[128,1024]{1,0:T(8,128)(2,1)S(1)} %halves.2), channel_id=1, source_target_pairs={{0,2},{2,0},{1,3},{3,1},{4,6},{6,4},{5,7},{7,5},{8,10},{10,8},{9,1... | collective-permute-start | bytes 786440 | tf_op jit(solution)/shard_map/ppermute | solution.py:209
  39.6 9.4 %collective-permute-start.21 = (bf16[128,512]{1,0:T(8,128)(2,1)S(1)}, bf16[128,512]{1,0:T(8,128)(2,1)S(1)}, u32[]{:S(2)}, u32[]{:S(2)}) collective-permute-start(bf16[128,512]{1,0:T(8,128)(2,1)S(1)} %get-tuple-element.62), channel_id=1, source_target_pairs={{0,4},{4,12},{12,8},{8,0},{1,5},{5,13},{13,9},{9,1},{2,6},{6,14},{... | collective-permute-start | bytes 393224 | tf_op jit(solution)/shard_map/ppermute | solution.py:209
  43.1 2.7 %collective-permute-start.17 = (bf16[128,640]{1,0:T(8,128)(2,1)S(1)}, bf16[128,640]{1,0:T(8,128)(2,1)S(1)}, u32[]{:S(2)}, u32[]{:S(2)}) collective-permute-start(bf16[128,640]{1,0:T(8,128)(2,1)S(1)} %collective-permute-done.16.refs_4_), channel_id=1, source_target_pairs={{0,1},{1,0},{2,3},{3,2},{4,5},{5,4},{6,7},{7,6},{8,9},{9,8},{10,11... | collective-permute-start | bytes 491528 | tf_op jit(solution)/shard_map/ppermute | solution.py:209
  43.1 2.7 %collective-permute-start.15 = (bf16[128,1152]{1,0:T(8,128)(2,1)S(1)}, bf16[128,1152]{1,0:T(8,128)(2,1)S(1)}, u32[]{:S(2)}, u32[]{:S(2)}) collective-permute-start(bf16[128,1152]{1,0:T(8,128)(2,1)S(1)} %collective-permute-done.14.refs_2_), channel_id=1, source_target_pairs={{0,1},{1,0},{2,3},{3,2},{4,5},{5,4},{6,7},{7,6},{8,9},{9,8},{10,11... | collective-permute-start | bytes 884744 | tf_op jit(solution)/shard_map/ppermute | solution.py:209
  46.7 8.0 %collective-permute-start.20 = (bf16[128,640]{1,0:T(8,128)(2,1)S(1)}, bf16[128,640]{1,0:T(8,128)(2,1)S(1)}, u32[]{:S(2)}, u32[]{:S(2)}) collective-permute-start(bf16[128,640]{1,0:T(8,128)(2,1)S(1)} %get-tuple-element.60), channel_id=1, source_target_pairs={{0,18},{2,16},{16,2},{18,0},{1,19},{3,17},{17,3},{19,1},{4,22},{6,... | collective-permute-start | bytes 491528 | tf_op jit(solution)/shard_map/ppermute | solution.py:208
  49.0 1.3 %collective-permute-start.22 = (bf16[128,512]{1,0:T(8,128)(2,1)S(1)}, bf16[128,512]{1,0:T(8,128)(2,1)S(1)}, u32[]{:S(2)}, u32[]{:S(2)}) collective-permute-start(bf16[128,512]{1,0:T(8,128)(2,1)S(1)} %collective-permute-done.21.refs_4_), channel_id=1, source_target_pairs={{0,1},{1,0},{2,3},{3,2},{4,5},{5,4},{6,7},{7,6},{8,9},{9,8},{10,11... | collective-permute-start | bytes 393224 | tf_op jit(solution)/shard_map/ppermute | solution.py:209
  49.0 12.1 %collective-permute-start.18 = (bf16[128,640]{1,0:T(8,128)(2,1)S(1)}, bf16[128,640]{1,0:T(8,128)(2,1)S(1)}, u32[]{:S(2)}, u32[]{:S(2)}) collective-permute-start(bf16[128,640]{1,0:T(8,128)(2,1)S(1)} %get-tuple-element.58), channel_id=1, source_target_pairs={{0,2},{2,0},{1,3},{3,1},{4,6},{6,4},{5,7},{7,5},{8,10},{10,8},{9,1... | collective-permute-start | bytes 491528 | tf_op jit(solution)/shard_map/ppermute | solution.py:209
  49.5 7.4 %copy-start.6 = (f32[4608]{0:T(1024)S(1)}, f32[4608]{0:T(1024)}, u32[]{:S(2)}) copy-start(f32[4608]{0:T(1024)} %param.12) | copy-start | bytes 55300
  49.5 13.1 %copy-start = (bf16[1,128,4608]{2,1,0:T(8,128)(2,1)S(1)}, bf16[1,128,4608]{2,1,0:T(8,128)(2,1)}, u32[]{:S(2)}) copy-start(bf16[1,128,4608]{2,1,0:T(8,128)(2,1)} %param.7) | copy-start | bytes 3538948
  49.5 11.5 %collective-permute-start.19 = (bf16[128,640]{1,0:T(8,128)(2,1)S(1)}, bf16[128,640]{1,0:T(8,128)(2,1)S(1)}, u32[]{:S(2)}, u32[]{:S(2)}) collective-permute-start(bf16[128,640]{1,0:T(8,128)(2,1)S(1)} %get-tuple-element.59), channel_id=1, source_target_pairs={{0,16},{16,0},{1,17},{17,1},{2,18},{18,2},{3,19},{19,3},{4,20},{20... | collective-permute-start | bytes 491528 | tf_op jit(solution)/shard_map/ppermute | solution.py:209
  51.0 9.8 %collective-permute-start.23 = (bf16[128,512]{1,0:T(8,128)(2,1)S(1)}, bf16[128,512]{1,0:T(8,128)(2,1)S(1)}, u32[]{:S(2)}, u32[]{:S(2)}) collective-permute-start(bf16[128,512]{1,0:T(8,128)(2,1)S(1)} %get-tuple-element.64), channel_id=1, source_target_pairs={{0,2},{2,0},{1,3},{3,1},{4,6},{6,4},{5,7},{7,5},{8,10},{10,8},{9,1... | collective-permute-start | bytes 393224 | tf_op jit(solution)/shard_map/ppermute | solution.py:209
  52.5 8.5 %collective-permute-start.24 = (bf16[128,512]{1,0:T(8,128)(2,1)S(1)}, bf16[128,512]{1,0:T(8,128)(2,1)S(1)}, u32[]{:S(2)}, u32[]{:S(2)}) collective-permute-start(bf16[128,512]{1,0:T(8,128)(2,1)S(1)} %get-tuple-element.65), channel_id=1, source_target_pairs={{0,16},{16,0},{1,17},{17,1},{2,18},{18,2},{3,19},{19,3},{4,20},{20... | collective-permute-start | bytes 393224 | tf_op jit(solution)/shard_map/ppermute | solution.py:209
  54.7 7.9 %collective-permute-start.25 = (bf16[128,512]{1,0:T(8,128)(2,1)S(1)}, bf16[128,512]{1,0:T(8,128)(2,1)S(1)}, u32[]{:S(2)}, u32[]{:S(2)}) collective-permute-start(bf16[128,512]{1,0:T(8,128)(2,1)S(1)} %get-tuple-element.68), channel_id=1, source_target_pairs={{0,18},{2,16},{16,2},{18,0},{1,19},{3,17},{17,3},{19,1},{4,22},{6,... | collective-permute-start | bytes 393224 | tf_op jit(solution)/shard_map/ppermute | solution.py:208
